TPU v7x, 32 devices: a whole 2x2x4 slice. The times are simulated.
32 devices in a mesh: tile: 8 (over z, core), member: 4 (over y, x).
Axes of the slice: x: 2, y: 2, z: 4, core: 2. Of those that a mesh axis runs over, the one named last changes fastest.
Arguments:
- coeffs: float32 [40, 32, 8192], P('member', None, 'tile'), may hold values from -6 to 6
- perturb: bfloat16 [2, 40, 32, 8192], P(None, 'member', None, 'tile'), may hold values from -2 to 2
- blocks: bfloat16 [8, 5, 1024, 1024], P('tile'), may hold values from -0.125 to 0.125
- neighbours: int32 [8, 5], P('tile'), may hold values from 0 to 7, as said below
- live: int32 [8], P('tile'), may hold values from 2 to 5, as said below
- obs_count: int32 [8], P('tile'), may hold values from 256 to 1024, as said below
- innovation: float32 [2, 32, 8192], P(None, None, 'tile'), may hold values from -6 to 6
- obs_weight: float32 [32, 8192], P(None, 'tile'), may hold values from 0.25 to 4
Outputs:
- increment: float32 [2, 32, 8192], P(None, None, ('tile', 'member'))
- gradient: float32 [40, 32, 8192], P('member', None, 'tile')
Inputs may be any that keep to these rules, and one draw needn't show every extreme that they name: `neighbours`: each row lists 5 different tiles, each at a distance of at most 2 from the row's tile along the tile cycle (indices taken modulo 8); only the first live[i] slots of row i are used. Some tile has all 5 slots live. Observations of tile i lie in its first obs_count[i] columns.
All inputs are finite; a program needn't handle non-finite values.
Results may differ from a plain program's by a relative error of at most 0.0038.
Values may be sent and summed in bfloat16 or wider, within the bound.
No kernel may reach another device: no remote copies, remote signals or barrier semaphores. Data moves between devices by JAX's collectives and lax.ppermute only.
A program may use at most 64 MiB of HBM per device.

v0:
```python
import jax
import jax.numpy as jnp
from jax import lax
from jax.sharding import PartitionSpec as P


def shifted(value, axis, steps):
    count = lax.axis_size(axis)
    pairs = [(source, (source + steps) % count) for source in range(count)]
    return lax.ppermute(value, axis, pairs)


def shards(coeffs, perturb, blocks, neighbours, live, obs_count, innovation, obs_weight):
    members, levels, cell_count = coeffs.shape
    row_count = members * levels
    slot_count = blocks.shape[1]
    radius = (slot_count - 1) // 2
    tile_count = lax.axis_size("tile")
    tile_index = lax.axis_index("tile")
    sources = neighbours[0]
    slot_live = jnp.arange(slot_count) < live[0]
    offset = (sources - tile_index) % tile_count
    offset = jnp.where(offset > radius, offset - tile_count, offset)
    coeff_half = coeffs.astype(jnp.bfloat16).reshape(row_count, cell_count)
    nearby = []
    for shift_by in range(-radius, radius + 1):
        if shift_by == 0:
            nearby.append(coeff_half)
        else:
            nearby.append(shifted(coeff_half, "tile", -shift_by))
    pieces = jnp.take(jnp.stack(nearby), offset + radius, axis=0)
    pieces = jnp.where(slot_live[:, None, None], pieces, jnp.zeros_like(pieces))
    localized = jnp.einsum("krc,kcd->rd", pieces, blocks[0], preferred_element_type=jnp.float32)
    localized = localized.reshape(members, levels, cell_count)
    partial_value = jnp.sum(perturb.astype(jnp.float32) * localized[None], axis=1)
    groups = lax.axis_size("member")
    group_index = lax.axis_index("member")
    own_width = cell_count // groups
    summed = lax.psum(partial_value, "member")
    column = jnp.arange(cell_count)
    residual = obs_weight[None] * jnp.where(
        column[None, None, :] < obs_count[0], summed - innovation, 0.0
    )
    increment = lax.dynamic_slice_in_dim(summed, group_index * own_width, own_width, 2)
    adjoint_in = jnp.sum(perturb.astype(jnp.float32) * residual[:, None], axis=0)
    adjoint_in = adjoint_in.astype(jnp.bfloat16).reshape(row_count, cell_count)
    products = jnp.einsum("rd,kcd->krc", adjoint_in, blocks[0], preferred_element_type=jnp.float32)
    products = jnp.where(slot_live[:, None, None], products, jnp.zeros_like(products))
    distances = jnp.arange(2 * radius + 1) - radius
    choose = ((offset[None, :] == distances[:, None]) & slot_live[None, :]).astype(jnp.float32)
    by_offset = jnp.einsum("dk,krc->drc", choose, products, precision=lax.Precision.HIGHEST)
    received = by_offset[radius]
    for shift_by in range(-radius, radius + 1):
        if shift_by != 0:
            received = received + shifted(by_offset[shift_by + radius], "tile", shift_by)
    gradient = coeffs + received.reshape(members, levels, cell_count)
    return (increment, gradient)


def solution(mesh):
    placed = (
        P("member", None, "tile"),
        P(None, "member", None, "tile"),
        P("tile", None, None, None),
        P("tile", None),
        P("tile"),
        P("tile"),
        P(None, None, "tile"),
        P(None, "tile"),
    )
    return jax.shard_map(
        shards,
        mesh=mesh,
        in_specs=placed,
        out_specs=(P(None, None, ("tile", "member")), P("member", None, "tile")),
        check_vma=False,
    )
```

profile of v0, /device:TPU:0, one launch (start us, length us, event | category | flops | bytes accessed | tf_op | source)
XLA Modules:
  0.0 252.2 jit_solution(16864393036810016443)
XLA Ops:
  7.2 1.4 convert_element_type.22
  8.6 5.1 %collective-permute-start.3 = (bf16[320,1024]{1,0:T(8,128)(2,1)S(1)}, bf16[320,1024]{1,0:T(8,128)(2,1)S(1)}, u32[]{:S(2)}, u32[]{:S(2)}) collective-permute-start(bf16[320,1024]{1,0:T(8,128)(2,1)S(1)} %bitcast.79), channel_id=1, source_target_pairs={{0,24},{4,28},{8,0},{12,4},{16,8},{20,12},{24,16},{28,20},{1,25},{... | collective-permute-start | bytes 1966088 | tf_op jit(solution)/shard_map/ppermute | solution.py:10
  17.6 39.1 %collective-permute-done = bf16[320,1024]{1,0:T(8,128)(2,1)S(1)} collective-permute-done((bf16[320,1024]{1,0:T(8,128)(2,1)S(1)}, bf16[320,1024]{1,0:T(8,128)(2,1)S(1)}, u32[]{:S(2)}, u32[]{:S(2)}) %collective-permute-start) | collective-permute-done | bytes 655392 | tf_op jit(solution)/shard_map/ppermute | solution.py:10
  61.2 2.7 %gather_fusion = bf16[5,320,1024]{2,1,0:T(8,128)(2,1)S(1)} fusion(bf16[5,320,1024]{2,1,0:T(8,128)(2,1)} %bitcast_dynamic-update-slice_fusion, s32[1024]{0:T(1024)S(1)} %pad_clamp_fusion), kind=kCustom, calls=%fused_computation | custom fusion | bytes 6553620 | tf_op jit(solution)/shard_map/jit(_take)/gather | solution.py:31
  64.3 6.4 %fusion.10 = f32[10,32,1024]{2,1,0:T(8,128)S(1)} fusion(bf16[10,32,1024,5]{2,1,0,3:T(8,128)(2,1)S(1)} %bitcast.78, bf16[1,5,1024,1024]{3,2,1,0:T(8,128)(2,1)} %param.10), kind=kOutput, calls=%fused_computation.15 | convolution fusion | flops 3355443200 | bytes 15073280 | tf_op jit(solution)/shard_map/krc,kcd->rd/dot_general | solution.py:33
  70.8 1.0 fusion.8
  71.8 42.8 %all-reduce.2.cloned.1.call-done = f32[2,32,1024]{2,1,0:T(8,128)} async-done(((f32[2,32,1024]{2,1,0:T(8,128)}), f32[2,32,1024]{2,1,0:T(8,128)}) %all-reduce.2.cloned.1.call-update) | async-done | bytes 262160 | tf_op jit(solution)/shard_map/psum | solution.py:39
  115.9 12.9 %fusion.4 = f32[320,5,1024]{2,0,1:T(8,128)} fusion(bf16[320,1024,1]{1,0,2:T(8,128)(2,1)S(1)} %bitcast.85, bf16[1,5,1024,1024]{3,2,1,0:T(8,128)(2,1)} %param.10), kind=kOutput, calls=%fused_computation.5 | convolution fusion | flops 3355443200 | bytes 17694720 | tf_op jit(solution)/shard_map/rd,kcd->krc/dot_general | solution.py:47
  128.8 13.3 %fusion.2 = f32[5,320,1024]{2,0,1:T(8,128)S(1)} fusion(f32[320,5,1024]{2,0,1:T(8,128)} %fusion.4, pred[5]{0:T(512)(128)(4,1)S(1)} %get-tuple-element.8, s32[5]{0:T(128)S(1)} %fusion.27, s32[5]{0:T(128)S(1)} %iota_add_fusion), kind=kOutput, calls=%fused_computation.3 | convolution fusion | flops 99942448 | bytes 13107245 | tf_op jit(solution)/shard_map/dk,krc->drc/dot_general | solution.py:51
  142.2 6.1 %fusion.29 = (f32[1,320,1024]{2,0,1:T(1,128)}, f32[1,320,1024]{2,0,1:T(1,128)}, f32[1,320,1024]{2,0,1:T(1,128)}, f32[1,320,1024]{2,0,1:T(1,128)}, f32[1,320,1024]{2,0,1:T(1,128)S(1)}) fusion(f32[5,320,1024]{2,0,1:T(8,128)S(1)} %fusion.2), kind=kLoop, calls=%fused_computation.64 | loop fusion | bytes 13107200 | tf_op jit(solution)/shard_map/slice | solution.py:52
  148.2 1.7 copy.45
  150.0 1.3 copy.46
  151.3 1.3 copy.47
  152.7 1.4 copy.44
  154.1 1.5 collective-permute-start.7
  155.6 2.3 collective-permute-start.4
  157.9 1.2 collective-permute-start.5
  159.1 1.5 constant_dynamic-slice_fusion
  160.5 26.3 %collective-permute-done.6 = f32[320,1024]{1,0:T(8,128)} collective-permute-done((f32[320,1024]{1,0:T(8,128)}, f32[320,1024]{1,0:T(8,128)}, u32[]{:S(2)}, u32[]{:S(2)}) %collective-permute-start.6) | collective-permute-done | bytes 1310752 | tf_op jit(solution)/shard_map/ppermute | solution.py:10
  186.9 1.1 collective-permute-done.7
  188.0 41.4 %collective-permute-done.4 = f32[320,1024]{1,0:T(8,128)} collective-permute-done((f32[320,1024]{1,0:T(8,128)}, f32[320,1024]{1,0:T(8,128)}, u32[]{:S(2)}, u32[]{:S(2)}) %collective-permute-start.4) | collective-permute-done | bytes 1310752 | tf_op jit(solution)/shard_map/ppermute | solution.py:10
  229.4 11.2 %collective-permute-done.5 = f32[320,1024]{1,0:T(8,128)} collective-permute-done((f32[320,1024]{1,0:T(8,128)S(1)}, f32[320,1024]{1,0:T(8,128)}, u32[]{:S(2)}, u32[]{:S(2)}) %collective-permute-start.5) | collective-permute-done | bytes 1310752 | tf_op jit(solution)/shard_map/ppermute | solution.py:10
  240.5 3.5 %fusion.16 = f32[320,1024]{1,0:T(8,128)S(1)} fusion(f32[320,1024]{1,0:T(8,128)} %collective-permute-done.7, f32[320,1024]{1,0:T(8,128)} %collective-permute-done.6, f32[320,1024]{1,0:T(8,128)} %collective-permute-done.5, f32[320,1024]{1,0:T(8,128)} %collective-permute-done.4, f32[1,320,1024]{2,0,1:T(1,128)S(1)} %copy-done.4), kind=kLoop, calls=%fused_computation.23 | loop fusion | flops 1310720 | bytes 7864320 | tf_op jit(solution)/shard_map/add | solution.py:55
  244.0 1.3 add.99
  (39 shorter events, 8.8 us)
Async XLA Ops:
  7.2 107.4 %all-reduce.2.cloned.1.call-start = ((), (), s32[]{:S(2)}) async-start(), calls=%async_computation | async-start | bytes 524288 | tf_op jit(solution)/shard_map/psum | solution.py:39
  8.6 51.7 %collective-permute-start.3 = (bf16[320,1024]{1,0:T(8,128)(2,1)S(1)}, bf16[320,1024]{1,0:T(8,128)(2,1)S(1)}, u32[]{:S(2)}, u32[]{:S(2)}) collective-permute-start(bf16[320,1024]{1,0:T(8,128)(2,1)S(1)} %bitcast.79), channel_id=1, source_target_pairs={{0,24},{4,28},{8,0},{12,4},{16,8},{20,12},{24,16},{28,20},{1,25},{... | collective-permute-start | bytes 1966088 | tf_op jit(solution)/shard_map/ppermute | solution.py:10
  13.7 45.7 %collective-permute-start.2 = (bf16[320,1024]{1,0:T(8,128)(2,1)S(1)}, bf16[320,1024]{1,0:T(8,128)(2,1)S(1)}, u32[]{:S(2)}, u32[]{:S(2)}) collective-permute-start(bf16[320,1024]{1,0:T(8,128)(2,1)S(1)} %bitcast.80), channel_id=1, source_target_pairs={{0,28},{4,0},{8,4},{12,8},{16,12},{20,16},{24,20},{28,24},{1,29},{... | collective-permute-start | bytes 1966088 | tf_op jit(solution)/shard_map/ppermute | solution.py:10
  13.7 43.9 %collective-permute-start.1 = (bf16[320,1024]{1,0:T(8,128)(2,1)S(1)}, bf16[320,1024]{1,0:T(8,128)(2,1)S(1)}, u32[]{:S(2)}, u32[]{:S(2)}) collective-permute-start(bf16[320,1024]{1,0:T(8,128)(2,1)S(1)} %bitcast.81), channel_id=1, source_target_pairs={{0,4},{4,8},{8,12},{12,16},{16,20},{20,24},{24,28},{28,0},{1,5},{5... | collective-permute-start | bytes 1966088 | tf_op jit(solution)/shard_map/ppermute | solution.py:10
  14.2 42.5 %collective-permute-start = (bf16[320,1024]{1,0:T(8,128)(2,1)S(1)}, bf16[320,1024]{1,0:T(8,128)(2,1)S(1)}, u32[]{:S(2)}, u32[]{:S(2)}) collective-permute-start(bf16[320,1024]{1,0:T(8,128)(2,1)S(1)} %bitcast.82), channel_id=1, source_target_pairs={{0,8},{4,12},{8,16},{12,20},{16,24},{20,28},{24,0},{28,4},{1,9},{5... | collective-permute-start | bytes 1966088 | tf_op jit(solution)/shard_map/ppermute | solution.py:10
  64.3 6.5 %copy-start.2 = (bf16[2,10,32,1024]{3,2,1,0:T(8,128)(2,1)S(1)}, bf16[2,10,32,1024]{3,2,1,0:T(8,128)(2,1)}, u32[]{:S(2)}) copy-start(bf16[2,10,32,1024]{3,2,1,0:T(8,128)(2,1)} %param.9) | copy-start | bytes 3932164
  64.3 7.5 %copy-start.7 = (s32[1,5]{1,0:T(1,128)S(1)}, s32[1,5]{1,0:T(1,128)}, u32[]{:S(2)}) copy-start(s32[1,5]{1,0:T(1,128)} %param.11) | copy-start | bytes 64
  64.3 50.3 %copy-start.6 = (f32[32,1024]{1,0:T(8,128)S(1)}, f32[32,1024]{1,0:T(8,128)}, u32[]{:S(2)}) copy-start(f32[32,1024]{1,0:T(8,128)} %param.15) | copy-start | bytes 393220
  70.8 43.8 %copy-start.5 = (f32[2,32,1024]{2,1,0:T(8,128)S(1)}, f32[2,32,1024]{2,1,0:T(8,128)}, u32[]{:S(2)}) copy-start(f32[2,32,1024]{2,1,0:T(8,128)} %param.14) | copy-start | bytes 786436
  148.2 1.7 copy-start.1
  148.2 3.1 %copy-start = (f32[1,320,1024]{2,0,1:T(1,128)S(1)}, f32[1,320,1024]{2,0,1:T(1,128)}, u32[]{:S(2)}) copy-start(f32[1,320,1024]{2,0,1:T(1,128)} %get-tuple-element.5) | copy-start | bytes 3932164
  151.3 89.2 %copy-start.4 = (f32[1,320,1024]{2,0,1:T(1,128)S(1)}, f32[1,320,1024]{2,0,1:T(1,128)}, u32[]{:S(2)}) copy-start(f32[1,320,1024]{2,0,1:T(1,128)} %get-tuple-element.2) | copy-start | bytes 3932164
  154.1 32.8 %collective-permute-start.6 = (f32[320,1024]{1,0:T(8,128)}, f32[320,1024]{1,0:T(8,128)}, u32[]{:S(2)}, u32[]{:S(2)}) collective-permute-start(f32[320,1024]{1,0:T(8,128)} %bitcast.70), channel_id=1, source_target_pairs={{0,4},{4,8},{8,12},{12,16},{16,20},{20,24},{24,28},{28,0},{1,5},{5... | collective-permute-start | bytes 3932168 | tf_op jit(solution)/shard_map/ppermute | solution.py:10
  154.1 33.9 %collective-permute-start.7 = (f32[320,1024]{1,0:T(8,128)}, f32[320,1024]{1,0:T(8,128)}, u32[]{:S(2)}, u32[]{:S(2)}) collective-permute-start(f32[320,1024]{1,0:T(8,128)} %bitcast.73), channel_id=1, source_target_pairs={{0,8},{4,12},{8,16},{12,20},{16,24},{20,28},{24,0},{28,4},{1,9},{5... | collective-permute-start | bytes 3932168 | tf_op jit(solution)/shard_map/ppermute | solution.py:10
  155.6 73.8 %collective-permute-start.4 = (f32[320,1024]{1,0:T(8,128)}, f32[320,1024]{1,0:T(8,128)}, u32[]{:S(2)}, u32[]{:S(2)}) collective-permute-start(f32[320,1024]{1,0:T(8,128)} %bitcast.72), channel_id=1, source_target_pairs={{0,24},{4,28},{8,0},{12,4},{16,8},{20,12},{24,16},{28,20},{1,25},{... | collective-permute-start | bytes 3932168 | tf_op jit(solution)/shard_map/ppermute | solution.py:10
  157.9 82.6 %collective-permute-start.5 = (f32[320,1024]{1,0:T(8,128)S(1)}, f32[320,1024]{1,0:T(8,128)}, u32[]{:S(2)}, u32[]{:S(2)}) collective-permute-start(f32[320,1024]{1,0:T(8,128)S(1)} %bitcast.84), channel_id=1, source_target_pairs={{0,28},{4,0},{8,4},{12,8},{16,12},{20,16},{24,20},{28,24},{1,29},{... | collective-permute-start | bytes 3932168 | tf_op jit(solution)/shard_map/ppermute | solution.py:10
  240.5 3.5 %copy-start.3 = (f32[10,32,1024]{2,1,0:T(8,128)S(1)}, f32[10,32,1024]{2,1,0:T(8,128)}, u32[]{:S(2)}) copy-start(f32[10,32,1024]{2,1,0:T(8,128)} %param.8) | copy-start | bytes 3932164
Sparse Core Ops, SparseCore 0:
  71.9 42.6 all-reduce.1
where the time goes:
time: 255 us; the launch traced here: 252 us
  waiting for transfers between devices  162 us (64%)
  matrix products  32.7 us (13%)
  local copies, waits for them, and re-layouts  20.5 us (8%)
  between operations  15.5 us (6%)
  starting transfers between devices  11.4 us (4%)
  other arithmetic  10.2 us (4%)
    ppermute x8, waiting for transfers between devices, shifted(): return lax.ppermute(value, axis, pairs)  119 us
    psum x1, waiting for transfers between devices, shards(): summed = lax.psum(partial_value, 'member')  42.8 us
    dot_general x1, matrix products, shards(): jnp.einsum('dk,krc->drc', choose, products, precision=lax.Precision.HIGHEST)  13.3 us
    dot_general x1, matrix products, shards(): jnp.einsum('rd,kcd->krc', adjoint_in, blocks[0], preferred_element_type=j...  12.9 us
    ppermute x8, starting transfers between devices, shifted(): return lax.ppermute(value, axis, pairs)  11.3 us
    unnamed x24, local copies, waits for them, and re-layouts  9.39 us
    dot_general x1, matrix products, shards(): jnp.einsum('krc,kcd->rd', pieces, blocks[0], preferred_element_type=jnp.f...  6.43 us
    slice x1, local copies, waits for them, and re-layouts, shards(): received = by_offset[radius]  6.05 us
  transfers between devices with their start and end apart: 9, of which 6 were waited for; matrix products, arithmetic and copies ran while one was open for 3% of the time, Pallas kernels for 0%

commit v1 on v0

v1 whole, which is shorter than its diff:
```python
import functools
import jax
import jax.numpy as jnp
from jax import lax
from jax.experimental import pallas as pl
from jax.experimental.pallas import tpu as pltpu
from jax.sharding import PartitionSpec as P

CHUNKS = 2
VMEM_LIMIT = 20 * 1024 * 1024
OWN, PARTNER, EARLY, SWAPPED, LATE = range(5)
PLACES = {"partner": PARTNER, "early": EARLY, "late": LATE}
ORDER = (0, 1, 2, -1, -2)
TURNED = (SWAPPED, LATE, EARLY)


def shift_pairs(count, step):
    return [(source, (source + step(source % 2)) % count) for source in range(count)]


def member_terms(value, sent, groups):
    terms, done = [value], 1
    while done < groups:
        if done > 1:
            value = functools.reduce(jnp.add, terms)
            sent = value.astype(sent.dtype)
        masks = (1, 2, 3) if groups // done >= 4 else (1,)
        terms = [value]
        for mask in masks:
            pairs = [(g, g ^ (mask * done)) for g in range(groups)]
            terms.append(lax.ppermute(sent, "member", pairs))
        done *= len(masks) + 1
    return terms


def after(value, *others):
    return lax.optimization_barrier((value, *others))[0]


def resident(value):
    return pltpu.with_memory_space_constraint(value, pltpu.VMEM)


def call(body, meta, operands, outs, name, scratch=(), spaces=None):
    spaces = spaces or [pltpu.VMEM] * len(operands)
    return pl.pallas_call(
        body,
        in_specs=[pl.BlockSpec(memory_space=pltpu.SMEM)]
        + [pl.BlockSpec(memory_space=space) for space in spaces],
        out_specs=[pl.BlockSpec(memory_space=pltpu.VMEM) for _ in outs],
        out_shape=outs,
        scratch_shapes=scratch,
        compiler_params=pltpu.CompilerParams(vmem_limit_bytes=VMEM_LIMIT),
        cost_estimate=pl.CostEstimate(flops=0, bytes_accessed=0, transcendentals=0),
        name=name,
    )(meta, *operands)


def times(rows, block):
    return jnp.dot(rows, block, preferred_element_type=jnp.float32)


def times_transposed(rows, block):
    return lax.dot_general(
        rows, block, (((1,), (1,)), ((), ())), preferred_element_type=jnp.float32
    )


def add_times(meta, held, place, rows, out):
    @pl.when(meta[place] > 0)
    def _():
        out[...] += times(rows[...], held[place])


def load(chunks, meta, blocks, perturb, innovation, weight, *refs):
    own, outs = refs[:chunks], refs[chunks:2 * chunks]
    held, held_perturb, held_innovation, held_weight, turned, arrived = refs[2 * chunks:]
    slots = held.shape[0]
    copies = [
        pltpu.make_async_copy(blocks.at[0, meta[slots + k]], held.at[k], arrived.at[k])
        for k in range(slots)
    ]
    copies += [
        pltpu.make_async_copy(source, target, arrived.at[slots + k])
        for k, (source, target) in enumerate((
            (perturb, held_perturb), (innovation, held_innovation), (weight, held_weight),
        ))
    ]
    for copy in copies:
        copy.start()
    for out in outs:
        out[...] = jnp.zeros_like(out)
    copies[OWN].wait()
    for rows, out in zip(own, outs):
        add_times(meta, held, OWN, rows, out)
    for k, place in enumerate(TURNED):
        copies[place].wait()

        @pl.when(meta[place] > 0)
        def _(k=k, place=place):
            turned[k] = held[place].T

    for k, copy in enumerate(copies):
        if k not in (OWN, *TURNED):
            copy.wait()


def forward_add(chunk, places, meta, held, before, *refs):
    out = refs[-1]
    out[...] = before[...]
    count = out.shape[0]
    for place, rows in zip(places, refs):
        if rows.shape[0] > count:
            rows = rows.at[chunk * count:(chunk + 1) * count]
        add_times(meta, held, place, rows, out)


def forward_far(chunk, meta, held, perturb, before, swapped, out, sent, total):
    levels = out.shape[1]
    at = slice(chunk * levels, (chunk + 1) * levels)
    total[...] = before[...]
    add_times(meta, held, SWAPPED, swapped, total)
    for t in range(out.shape[0]):
        value = sum(
            perturb[t, m, at].astype(jnp.float32) * total[m * levels:(m + 1) * levels]
            for m in range(perturb.shape[1])
        )
        out[t] = value
        sent[t] = value.astype(sent.dtype)


def back_times(held, turned, place, rows):
    if place in TURNED:
        return times(rows[...], turned[TURNED.index(place)])
    return times_transposed(rows[...], held[place])


def transposed_or_zero(meta, held, turned, place, rows, *outs):
    size = outs[0].shape[0]
    alive = meta[place] > 0

    @pl.when(alive)
    def _():
        value = back_times(held, turned, place, rows)
        for k, out in enumerate(outs):
            out[...] = value[k * size:(k + 1) * size].astype(out.dtype)

    @pl.when(jnp.logical_not(alive))
    def _():
        for out in outs:
            out[...] = jnp.zeros_like(out)


def backward_first(chunk, pieces, meta, turned, perturb, innovation, weight, *refs):
    terms, refs = refs[:-4 - pieces], refs[-4 - pieces:]
    adjoint_in, *swap, direct, part, summed = refs
    slots = len(ORDER)
    count, levels, cells = summed.shape
    width = part.shape[-1]
    at = slice(chunk * levels, (chunk + 1) * levels)
    seen = lax.broadcasted_iota(jnp.int32, (levels, cells), 1) < meta[2 * slots]
    residual = []
    for t in range(count):
        value = sum(term[t].astype(jnp.float32) for term in terms)
        summed[t] = value
        residual.append(weight[at] * jnp.where(seen, value - innovation[t, at], 0.0))
    part[...] = summed[:, :, pl.ds(pl.multiple_of(meta[2 * slots + 1] * width, 128), width)]
    for m in range(perturb.shape[1]):
        value = sum(perturb[t, m, at].astype(jnp.float32) * residual[t] for t in range(count))
        adjoint_in[m * levels:(m + 1) * levels] = value.astype(adjoint_in.dtype)
    transposed_or_zero(meta, None, turned, SWAPPED, adjoint_in, *swap)
    transposed_or_zero(meta, None, turned, LATE, adjoint_in, direct)


def backward_through(meta, turned, adjoint_in, *refs):
    *swap, out = refs
    size = swap[0].shape[0]
    alive = meta[EARLY] > 0

    @pl.when(alive)
    def _():
        value = back_times(None, turned, EARLY, adjoint_in)
        for k, piece in enumerate(swap):
            at = slice(k * size, (k + 1) * size)
            out[at] = (value[at] + piece[...].astype(jnp.float32)).astype(out.dtype)

    @pl.when(jnp.logical_not(alive))
    def _():
        for k, piece in enumerate(swap):
            out[k * size:(k + 1) * size] = piece[...]


def backward_rest(meta, held, adjoint_in, *outs):
    transposed_or_zero(meta, held, None, PARTNER, adjoint_in, *outs[:-1])
    transposed_or_zero(meta, held, None, OWN, adjoint_in, outs[-1])


def finish(pieces, coeffs, kept, direct, through, *refs):
    second, out = refs[:pieces], refs[-1]
    value = kept[...] + jnp.concatenate([v[...].astype(jnp.float32) for v in second])
    for term in (direct, through):
        value = value + term[...].astype(jnp.float32)
    out[...] = coeffs[...] + value.reshape(out.shape)


def shards(coeffs, perturb, blocks, neighbours, live, obs_count, innovation, obs_weight):
    members, levels, cells = coeffs.shape
    window = perturb.shape[0]
    slots = blocks.shape[1]
    tile_count = lax.axis_size("tile")
    groups = lax.axis_size("member")
    tile_index = lax.axis_index("tile")
    group_index = lax.axis_index("member")
    half, full = jnp.bfloat16, jnp.float32
    part = levels // CHUNKS
    rows = members * part
    width = cells // groups
    shape = jax.ShapeDtypeStruct
    rows_half, rows_full = shape((rows, cells), half), shape((rows, cells), full)

    side = 1 - 2 * (tile_index % 2)
    radius = (slots - 1) // 2
    offset = (neighbours[0] - tile_index) % tile_count
    offset = jnp.where(offset > radius, offset - tile_count, offset) * side
    match = offset[None, :] == jnp.array(ORDER, jnp.int32)[:, None]
    slot = jnp.sum(jnp.where(match, jnp.arange(slots)[None, :], 0), axis=1)
    meta = jnp.concatenate(
        [(slot < live[0]).astype(slot.dtype), slot, obs_count, group_index[None]]
    ).astype(jnp.int32)

    inward = shift_pairs(tile_count, lambda core: -2 if core == 0 else 2)
    outward = shift_pairs(tile_count, lambda core: 2 if core == 0 else -2)
    across = shift_pairs(tile_count, lambda core: 1 if core == 0 else -1)

    own = []
    for c in range(CHUNKS):
        source = coeffs if c == 0 else after(coeffs, own[c - 1])
        own.append(source[:, c * part:(c + 1) * part].astype(half).reshape(rows, cells))
    distant = [
        pltpu.with_memory_space_constraint(v, pltpu.HBM)
        for v in (blocks, perturb, innovation, obs_weight)
    ]
    *near, held, held_perturb, held_innovation, held_weight, turned = call(
        functools.partial(load, CHUNKS), meta, (*distant, *own),
        [rows_full] * CHUNKS
        + [pltpu.VMEM(v.shape, v.dtype) for v in (blocks[0], perturb, innovation, obs_weight)]
        + [pltpu.VMEM((len(TURNED), cells, cells), half)],
        "load", [pltpu.SemaphoreType.DMA((slots + 3,))],
        [pltpu.HBM] * 4 + [pltpu.VMEM] * CHUNKS,
    )
    held, held_perturb, held_innovation, held_weight, turned = map(
        resident, (held, held_perturb, held_innovation, held_weight, turned)
    )

    def add(c, before, name, **rows):
        places = tuple(PLACES[key] for key in rows)
        [total] = call(
            functools.partial(forward_add, c, places), meta, (held, before, *rows.values()), [rows_full], name
        )
        return total

    def observe(c, total, swapped):
        return call(
            functools.partial(forward_far, c), meta, (held, held_perturb, total, swapped),
            [shape((window, part, cells), full), shape((window, part, cells), half)],
            "forward_far", [pltpu.VMEM((rows, cells), full)],
        )

    def cut(pieces):
        return [shape((rows // pieces, cells), half)] * pieces

    def respond(c, pieces, terms, *others):
        adjoint_in, *swap, direct, increment = call(
            functools.partial(backward_first, c, pieces), meta,
            (turned, held_perturb, held_innovation, held_weight, after(terms[0], *others), *terms[1:]),
            [rows_half, *cut(pieces), rows_half, shape((window, part, width), full)],
            "backward_first", [pltpu.VMEM((window, part, cells), full)],
        )
        return adjoint_in, swap, direct, increment

    def add_through(adjoint_in, swap):
        [through] = call(backward_through, meta, (turned, adjoint_in, *swap), [rows_half], "backward_through")
        return through

    def rest(pieces, adjoint_in, *others):
        *second, kept = call(
            backward_rest, meta, (held, after(adjoint_in, *others)), [*cut(pieces), rows_full],
            "backward_rest",
        )
        return second, kept

    def finished(c, gradient, second, *terms):
        terms += tuple(second)
        chunk_spec = pl.BlockSpec((members, part, cells), lambda i: (0, c, 0))
        return pl.pallas_call(
            functools.partial(finish, len(second)),
            grid=(1,),
            in_specs=[chunk_spec] + [pl.BlockSpec(v.shape, lambda i: (0, 0)) for v in terms]
            + [pl.BlockSpec(memory_space=pl.ANY)] * len(gradient),
            out_specs=chunk_spec,
            out_shape=shape(coeffs.shape, full),
            input_output_aliases={1 + len(terms): 0} if gradient else {},
            compiler_params=pltpu.CompilerParams(vmem_limit_bytes=VMEM_LIMIT),
            cost_estimate=pl.CostEstimate(flops=0, bytes_accessed=0, transcendentals=0),
            name="finish",
        )(coeffs, *terms, *gradient)

    early0 = lax.ppermute(own[0], "tile", inward)
    late0 = lax.ppermute(own[0], "tile", outward)
    partner = lax.ppermute(jnp.concatenate(after(own, near[0])), "tile", across)
    swapped0 = lax.ppermute(after(early0, late0, near[0]), "tile", across)
    early1 = lax.ppermute(after(own[1], early0, late0), "tile", inward)
    late1 = lax.ppermute(after(own[1], early0, late0), "tile", outward)
    total0 = add(0, near[0], "forward_mid", partner=partner, early=early0, late=late0)
    increment0, sent0 = observe(0, total0, swapped0)
    terms0 = member_terms(increment0, sent0, groups)
    near1 = add(1, near[1], "forward_near", partner=partner)
    adjoint0, swap0, direct0, part0 = respond(0, 1, terms0, near1)
    swap0 = [lax.ppermute(v, "tile", across) for v in swap0]
    direct0 = lax.ppermute(direct0, "tile", inward)
    swapped1 = lax.ppermute(after(early1, late1, adjoint0), "tile", across)
    total1 = add(1, near1, "forward_mid", early=early1, late=late1)
    increment1, sent1 = observe(1, total1, swapped1)
    through0 = add_through(adjoint0, swap0)
    second0, kept0 = rest(1, adjoint0, through0)
    through0 = lax.ppermute(through0, "tile", outward)
    second0 = [lax.ppermute(v, "tile", across) for v in second0]
    terms1 = member_terms(increment1, sent1, groups)
    adjoint1, swap1, direct1, part1 = respond(1, 2, terms1, kept0)
    swap1 = [lax.ppermute(v, "tile", across) for v in swap1]
    direct1 = lax.ppermute(direct1, "tile", inward)
    through1 = lax.ppermute(add_through(after(adjoint1, through0, direct0), swap1), "tile", outward)
    second1, kept1 = rest(2, adjoint1, *swap1)
    second1 = [lax.ppermute(v, "tile", across) for v in second1]
    gradient = finished(0, (), second0, kept0, direct0, through0)
    gradient = finished(1, (gradient,), second1, kept1, direct1, through1)
    return (jnp.concatenate((part0, part1), axis=1), gradient)


def solution(mesh):
    placed = (
        P("member", None, "tile"),
        P(None, "member", None, "tile"),
        P("tile", None, None, None),
        P("tile", None),
        P("tile"),
        P("tile"),
        P(None, None, "tile"),
        P(None, "tile"),
    )
    return jax.shard_map(
        shards,
        mesh=mesh,
        in_specs=placed,
        out_specs=(P(None, None, ("tile", "member")), P("member", None, "tile")),
        check_vma=False,
    )
```

time: 255 us -> 74.3 us (0.29); the launches traced: 252 us -> 74.4 us
  waiting for transfers between devices: 162 us -> 20.2 us
  matrix products: 32.7 us -> 0 us
  Pallas kernels: 0 us -> 19 us
  starting transfers between devices: 11.4 us -> 29.8 us
  local copies, waits for them, and re-layouts: 20.5 us -> 2.29 us
  between operations: 15.5 us -> 2.17 us
  other arithmetic: 10.2 us -> 0.96 us
    ppermute x8 -> x23, waiting for transfers between devices: 119 us -> 20.2 us  [the longest x1 7.03 us: shards(): lax.ppermute(add_through(after(adjoint1, through0, direct0), swap1), 'til...]
    psum x1 -> x0, waiting for transfers between devices: 42.8 us -> none  [shards(): summed = lax.psum(partial_value, 'member')]
    dot_general x3 -> x0, matrix products: 32.7 us -> none  [the longest x1 13.3 us: shards(): jnp.einsum('dk,krc->drc', choose, products, precision=lax.Precision.HIGHEST)]
    pallas_call x0 -> x14, Pallas kernels: none -> 19 us  [the longest x12 16.9 us: call(): pl.pallas_call(body, in_specs=[pl.BlockSpec(memory_space=pltpu.SMEM)] + [...]
    ppermute x8 -> x23, starting transfers between devices: 11.3 us -> 29.8 us  [the longest x6 7.11 us: member_terms(): terms.append(lax.ppermute(sent, 'member', pairs))]
    unnamed x24 -> x6, local copies, waits for them, and re-layouts: 9.39 us -> 0.02 us
    add x2 -> x0, other arithmetic: 4.77 us -> none  [the longest x1 3.49 us: shards(): received + shifted(by_offset[shift_by + radius], 'tile', shift_by)]
    slice x1 -> x2, local copies, waits for them, and re-layouts: 6.05 us -> 2.27 us  [shards(): source[:, c * part:(c + 1) * part].astype(half).reshape(rows, cells)]
  transfers between devices with their start and end apart: 9 -> 23, of which waited for: 6 -> 11; matrix products, arithmetic and copies ran while one was open for 3% -> 3% of each run, Pallas kernels for 0% -> 24%
where the time goes in v1:
time: 74.3 us; the launch traced here: 74.4 us
  starting transfers between devices  29.8 us (40%)
  waiting for transfers between devices  20.2 us (27%)
  Pallas kernels  19 us (26%)
  local copies, waits for them, and re-layouts  2.29 us (3%)
  between operations  2.17 us (3%)
  other arithmetic  0.96 us (1%)
    pallas_call x12, Pallas kernels, call(): pl.pallas_call(body, in_specs=[pl.BlockSpec(memory_space=pltpu.SMEM)] + [...  16.9 us
    ppermute x6, starting transfers between devices, member_terms(): terms.append(lax.ppermute(sent, 'member', pairs))  7.11 us
    ppermute x1, waiting for transfers between devices, shards(): lax.ppermute(add_through(after(adjoint1, through0, direct0), swap1), 'til...  7.03 us
    ppermute x6, waiting for transfers between devices, member_terms(): terms.append(lax.ppermute(sent, 'member', pairs))  5.13 us
    ppermute x1, starting transfers between devices, shards(): direct1 = lax.ppermute(direct1, 'tile', inward)  4.61 us
    ppermute x1, waiting for transfers between devices, shards(): early0 = lax.ppermute(own[0], 'tile', inward)  3.59 us
    ppermute x1, starting transfers between devices, shards(): direct0 = lax.ppermute(direct0, 'tile', inward)  3.27 us
    ppermute x1, starting transfers between devices, shards(): late0 = lax.ppermute(own[0], 'tile', outward)  3.08 us
  transfers between devices with their start and end apart: 23, of which 11 were waited for; matrix products, arithmetic and copies ran while one was open for 3% of the time, Pallas kernels for 24%

profile of v1, /device:TPU:0, one launch (start us, length us, event | category | flops | bytes accessed | tf_op | source)
XLA Modules:
  0.0 74.4 jit_solution(14432432251024036072)
XLA Ops:
  0.7 1.1 %slice.15 = bf16[10,16,1024]{2,1,0:T(8,128)(2,1)S(1)} slice(f32[10,32,1024]{2,1,0:T(8,128)} %coeffs.3), slice={[0:10], [0:16], [0:1024]} | slice | bytes 655360 | tf_op jit(solution)/shard_map/slice | solution.py:238
  1.8 3.1 %collective-permute-start.2 = (bf16[160,1024]{1,0:T(8,128)(2,1)S(1)}, bf16[160,1024]{1,0:T(8,128)(2,1)S(1)}, u32[]{:S(2)}, u32[]{:S(2)}) collective-permute-start(bf16[160,1024]{1,0:T(8,128)(2,1)S(1)} %bitcast.11), channel_id=1, source_target_pairs={{0,8},{4,28},{8,16},{12,4},{16,24},{20,12},{24,0},{28,20},{1,9},{5... | collective-permute-start | bytes 983048 | tf_op jit(solution)/shard_map/ppermute | solution.py:309
  4.9 2.1 %collective-permute-start.1 = (bf16[160,1024]{1,0:T(8,128)(2,1)S(1)}, bf16[160,1024]{1,0:T(8,128)(2,1)S(1)}, u32[]{:S(2)}, u32[]{:S(2)}) collective-permute-start(bf16[160,1024]{1,0:T(8,128)(2,1)S(1)} %bitcast.12), channel_id=1, source_target_pairs={{0,24},{4,12},{8,0},{12,20},{16,8},{20,28},{24,16},{28,4},{1,25},{... | collective-permute-start | bytes 983048 | tf_op jit(solution)/shard_map/ppermute | solution.py:308
  9.7 5.0 %load.1 = (f32[160,1024]{1,0:T(8,128)S(1)}, f32[160,1024]{1,0:T(8,128)S(1)}, bf16[5,1024,1024]{2,1,0:T(8,128)(2,1)S(1)}, bf16[2,10,32,1024]{3,2,1,0:T(8,128)(2,1...) custom-call(s32[12]{0:T(128)S(1)} %pad_add_fusion.meta, ...), custom_call_target="tpu_custom_call" | custom-call | tf_op jit(solution)/shard_map/load/pallas_call | solution.py:46
  15.5 3.6 %collective-permute-done.1.refs_1_ = bf16[160,1024]{1,0:T(8,128)(2,1)S(1)} collective-permute-done((bf16[160,1024]{1,0:T(8,128)(2,1)S(1)}, bf16[160,1024]{1,0:T(8,128)(2,1)S(1)}, u32[]{:S(2)}, u32[]{:S(2)}) %collective-permute-start.1) | collective-permute-done | bytes 327712 | tf_op jit(solution)/shard_map/ppermute | solution.py:308
  19.1 1.8 %collective-permute-start.3 = (bf16[160,1024]{1,0:T(8,128)(2,1)S(1)}, bf16[160,1024]{1,0:T(8,128)(2,1)S(1)}, u32[]{:S(2)}, u32[]{:S(2)}) collective-permute-start(bf16[160,1024]{1,0:T(8,128)(2,1)S(1)} %collective-permute-done.1.refs_1_), channel_id=1, source_target_pairs={{0,4},{4,0},{8,12},{12,8},{16,20},{20,16},{24,28},{28,24},{1,5},{5... | collective-permute-start | bytes 983048 | tf_op jit(solution)/shard_map/ppermute | solution.py:311
  21.0 1.3 %collective-permute-start.8 = (bf16[160,1024]{1,0:T(8,128)(2,1)S(1)}, bf16[160,1024]{1,0:T(8,128)(2,1)S(1)}, u32[]{:S(2)}, u32[]{:S(2)}) collective-permute-start(bf16[160,1024]{1,0:T(8,128)(2,1)S(1)} %bitcast.9), channel_id=1, source_target_pairs={{0,8},{4,28},{8,16},{12,4},{16,24},{20,12},{24,0},{28,20},{1,9},{5... | collective-permute-start | bytes 983048 | tf_op jit(solution)/shard_map/ppermute | solution.py:313
  22.3 2.5 %collective-permute-start.7 = (bf16[160,1024]{1,0:T(8,128)(2,1)S(1)}, bf16[160,1024]{1,0:T(8,128)(2,1)S(1)}, u32[]{:S(2)}, u32[]{:S(2)}) collective-permute-start(bf16[160,1024]{1,0:T(8,128)(2,1)S(1)} %bitcast.10), channel_id=1, source_target_pairs={{0,24},{4,12},{8,0},{12,20},{16,8},{20,28},{24,16},{28,4},{1,25},{... | collective-permute-start | bytes 983048 | tf_op jit(solution)/shard_map/ppermute | solution.py:312
  25.9 1.3 %forward_far.2 = (f32[2,16,1024]{2,1,0:T(8,128)S(1)}, bf16[2,16,1024]{2,1,0:T(8,128)(2,1)S(1)}) custom-call(s32[12]{0:T(128)S(1)} %pad_add_fusion.meta, bf16[5,1024,1024]{2,1,0:T(8,128)(2,1)S(1)} %get-tuple-element.43.held, bf16[2,10,32,1024]{3,2,1,0:T(8,128)(2,1)S(1)} %get-tuple-element.40.perturb, f32[160,1024]{1,0:T(8,128)S(1)} %forward_mid.2.before, ...), custom_call_target="tpu_custom_call" | custom-call | tf_op jit(solution)/shard_map/forward_far/pallas_call | solution.py:46
  27.2 2.3 %collective-permute-start.6 = (bf16[2,16,1024]{2,1,0:T(8,128)(2,1)S(1)}, bf16[2,16,1024]{2,1,0:T(8,128)(2,1)S(1)}, u32[]{:S(2)}, u32[]{:S(2)}) collective-permute-start(bf16[2,16,1024]{2,1,0:T(8,128)(2,1)S(1)} %get-tuple-element.51), channel_id=1, source_target_pairs={{0,3},{1,2},{2,1},{3,0},{4,7},{5,6},{6,5},{7,4},{8,11},{9,10},{10,... | collective-permute-start | bytes 196616 | tf_op jit(solution)/shard_map/ppermute | solution.py:31
  32.5 1.2 %collective-permute-done.5.refs_2_ = bf16[2,16,1024]{2,1,0:T(8,128)(2,1)S(1)} collective-permute-done((bf16[2,16,1024]{2,1,0:T(8,128)(2,1)S(1)}, bf16[2,16,1024]{2,1,0:T(8,128)(2,1)S(1)}, u32[]{:S(2)}, u32[]{:S(2)}) %collective-permute-start.5) | collective-permute-done | bytes 65568 | tf_op jit(solution)/shard_map/ppermute | solution.py:31
  34.2 1.3 %backward_first.2 = (bf16[160,1024]{1,0:T(8,128)(2,1)S(1)}, bf16[160,1024]{1,0:T(8,128)(2,1)S(1)}, bf16[160,1024]{1,0:T(8,128)(2,1)S(1)}, f32[2,16,256]{2,1,0:T(8,128)S(1)}) custom-call(s32[12]{0:T(128)S(1)} %pad_add_fusion.meta, bf16[3,1024,1024]{2,1,0:T(8,128)(2,1)S(1)} %get-tuple-element.39.turned, ...), custom_call_target="tpu_custom_call" | custom-call | tf_op jit(solution)/shard_map/backward_first/pallas_call | solution.py:46
  35.6 1.7 %collective-permute-done.7.refs_0_ = bf16[160,1024]{1,0:T(8,128)(2,1)S(1)} collective-permute-done((bf16[160,1024]{1,0:T(8,128)(2,1)S(1)}, bf16[160,1024]{1,0:T(8,128)(2,1)S(1)}, u32[]{:S(2)}, u32[]{:S(2)}) %collective-permute-start.7) | collective-permute-done | bytes 327712 | tf_op jit(solution)/shard_map/ppermute | solution.py:312
  37.7 3.3 %collective-permute-start.18 = (bf16[160,1024]{1,0:T(8,128)(2,1)S(1)}, bf16[160,1024]{1,0:T(8,128)(2,1)S(1)}, u32[]{:S(2)}, u32[]{:S(2)}) collective-permute-start(bf16[160,1024]{1,0:T(8,128)(2,1)S(1)} %get-tuple-element.69), channel_id=1, source_target_pairs={{0,24},{4,12},{8,0},{12,20},{16,8},{20,28},{24,16},{28,4},{1,25},{... | collective-permute-start | bytes 983048 | tf_op jit(solution)/shard_map/ppermute | solution.py:320
  42.2 1.3 %forward_far.3 = (f32[2,16,1024]{2,1,0:T(8,128)S(1)}, bf16[2,16,1024]{2,1,0:T(8,128)(2,1)S(1)}) custom-call(s32[12]{0:T(128)S(1)} %pad_add_fusion.meta, bf16[5,1024,1024]{2,1,0:T(8,128)(2,1)S(1)} %get-tuple-element.43.held, bf16[2,10,32,1024]{3,2,1,0:T(8,128)(2,1)S(1)} %get-tuple-element.40.perturb, f32[160,1024]{1,0:T(8,128)S(1)} %forward_mid.3.before, ...), custom_call_target="tpu_custom_call" | custom-call | tf_op jit(solution)/shard_map/forward_far/pallas_call | solution.py:46
  43.5 2.5 %collective-permute-start.13 = (bf16[2,16,1024]{2,1,0:T(8,128)(2,1)S(1)}, bf16[2,16,1024]{2,1,0:T(8,128)(2,1)S(1)}, u32[]{:S(2)}, u32[]{:S(2)}) collective-permute-start(bf16[2,16,1024]{2,1,0:T(8,128)(2,1)S(1)} %get-tuple-element.61), channel_id=1, source_target_pairs={{0,3},{1,2},{2,1},{3,0},{4,7},{5,6},{6,5},{7,4},{8,11},{9,10},{10,... | collective-permute-start | bytes 196616 | tf_op jit(solution)/shard_map/ppermute | solution.py:31
  47.1 1.4 %backward_rest.2 = (bf16[160,1024]{1,0:T(8,128)(2,1)S(1)}, f32[160,1024]{1,0:T(8,128)S(1)}) custom-call(s32[12]{0:T(128)S(1)} %pad_add_fusion.meta, bf16[5,1024,1024]{2,1,0:T(8,128)(2,1)S(1)} %get-tuple-element.43.held, bf16[160,1024]{1,0:T(8,128)(2,1)S(1)} %get-tuple-element.58.adjoint_in), custom_call_target="tpu_custom_call" | custom-call | tf_op jit(solution)/shard_map/backward_rest/pallas_call | solution.py:46
  49.2 1.8 %collective-permute-done.12.refs_2_ = bf16[2,16,1024]{2,1,0:T(8,128)(2,1)S(1)} collective-permute-done((bf16[2,16,1024]{2,1,0:T(8,128)(2,1)S(1)}, bf16[2,16,1024]{2,1,0:T(8,128)(2,1)S(1)}, u32[]{:S(2)}, u32[]{:S(2)}) %collective-permute-start.12) | collective-permute-done | bytes 65568 | tf_op jit(solution)/shard_map/ppermute | solution.py:31
  51.2 1.3 %backward_first.3 = (bf16[160,1024]{1,0:T(8,128)(2,1)S(1)}, bf16[80,1024]{1,0:T(8,128)(2,1)S(1)}, bf16[80,1024]{1,0:T(8,128)(2,1)S(1)}, bf16[160,1024]{1,0:T(8,128)(2,1)S(1)}, f32[2,16,256]{2,1,0:T(8,128)S(1)}) custom-call(s32[12]{0:T(128)S(1)} %pad_add_fusion.meta, bf16[3,1024,1024]{2,1,0:T(8,128)(2,1)S(1)} %get-tuple-element.39.turned, ...), custom_call_target="tpu_custom_call" | custom-call | tf_op jit(solution)/shard_map/backward_first/pallas_call | solution.py:46
  53.4 4.6 %collective-permute-start.16 = (bf16[160,1024]{1,0:T(8,128)(2,1)S(1)}, bf16[160,1024]{1,0:T(8,128)(2,1)S(1)}, u32[]{:S(2)}, u32[]{:S(2)}) collective-permute-start(bf16[160,1024]{1,0:T(8,128)(2,1)S(1)} %get-tuple-element.68), channel_id=1, source_target_pairs={{0,24},{4,12},{8,0},{12,20},{16,8},{20,28},{24,16},{28,4},{1,25},{... | collective-permute-start | bytes 983048 | tf_op jit(solution)/shard_map/ppermute | solution.py:331
  58.7 1.4 %backward_rest.3 = (bf16[80,1024]{1,0:T(8,128)(2,1)S(1)}, bf16[80,1024]{1,0:T(8,128)(2,1)S(1)}, f32[160,1024]{1,0:T(8,128)S(1)}) custom-call(s32[12]{0:T(128)S(1)} %pad_add_fusion.meta, bf16[5,1024,1024]{2,1,0:T(8,128)(2,1)S(1)} %get-tuple-element.43.held, bf16[160,1024]{1,0:T(8,128)(2,1)S(1)} %get-tuple-element.70.adjoint_in), custom_call_target="tpu_custom_call" | custom-call | tf_op jit(solution)/shard_map/backward_rest/pallas_call | solution.py:46
  60.2 2.4 %collective-permute-start.20 = (bf16[80,1024]{1,0:T(8,128)(2,1)S(1)}, bf16[80,1024]{1,0:T(8,128)(2,1)S(1)}, u32[]{:S(2)}, u32[]{:S(2)}) collective-permute-start(bf16[80,1024]{1,0:T(8,128)(2,1)S(1)} %get-tuple-element.71), channel_id=1, source_target_pairs={{0,4},{4,0},{8,12},{12,8},{16,20},{20,16},{24,28},{28,24},{1,5},{5... | collective-permute-start | bytes 491528 | tf_op jit(solution)/shard_map/ppermute | solution.py:334
  64.3 2.0 %collective-permute-done.16.direct = bf16[160,1024]{1,0:T(8,128)(2,1)S(1)} collective-permute-done((bf16[160,1024]{1,0:T(8,128)(2,1)S(1)}, bf16[160,1024]{1,0:T(8,128)(2,1)S(1)}, u32[]{:S(2)}, u32[]{:S(2)}) %collective-permute-start.16) | collective-permute-done | bytes 327712 | tf_op jit(solution)/shard_map/ppermute | solution.py:331
  66.3 7.0 %collective-permute-done.19.through = bf16[160,1024]{1,0:T(8,128)(2,1)S(1)} collective-permute-done((bf16[160,1024]{1,0:T(8,128)(2,1)S(1)}, bf16[160,1024]{1,0:T(8,128)(2,1)S(1)}, u32[]{:S(2)}, u32[]{:S(2)}) %collective-permute-start.19) | collective-permute-done | bytes 327712 | tf_op jit(solution)/shard_map/ppermute | solution.py:332
  (50 shorter events, 14.9 us)
Async XLA Ops:
  0.6 8.8 %copy-start.2 = (s32[5]{0:T(128)S(1)}, s32[5]{0:T(128)}, u32[]{:S(2)}) copy-start(s32[5]{0:T(128)} %constant.44.clone) | copy-start | bytes 64
  1.8 13.7 %collective-permute-start.2 = (bf16[160,1024]{1,0:T(8,128)(2,1)S(1)}, bf16[160,1024]{1,0:T(8,128)(2,1)S(1)}, u32[]{:S(2)}, u32[]{:S(2)}) collective-permute-start(bf16[160,1024]{1,0:T(8,128)(2,1)S(1)} %bitcast.11), channel_id=1, source_target_pairs={{0,8},{4,28},{8,16},{12,4},{16,24},{20,12},{24,0},{28,20},{1,9},{5... | collective-permute-start | bytes 983048 | tf_op jit(solution)/shard_map/ppermute | solution.py:309
  4.9 14.2 %collective-permute-start.1 = (bf16[160,1024]{1,0:T(8,128)(2,1)S(1)}, bf16[160,1024]{1,0:T(8,128)(2,1)S(1)}, u32[]{:S(2)}, u32[]{:S(2)}) collective-permute-start(bf16[160,1024]{1,0:T(8,128)(2,1)S(1)} %bitcast.12), channel_id=1, source_target_pairs={{0,24},{4,12},{8,0},{12,20},{16,8},{20,28},{24,16},{28,4},{1,25},{... | collective-permute-start | bytes 983048 | tf_op jit(solution)/shard_map/ppermute | solution.py:308
  14.8 10.0 %collective-permute-start = (bf16[320,1024]{1,0:T(8,128)(2,1)S(1)}, bf16[320,1024]{1,0:T(8,128)(2,1)S(1)}, u32[]{:S(2)}, u32[]{:S(2)}) collective-permute-start(bf16[320,1024]{1,0:T(8,128)(2,1)S(1)} %pad_maximum_fusion), channel_id=1, source_target_pairs={{0,4},{4,0},{8,12},{12,8},{16,20},{20,16},{24,28},{28,24},{1,5},{5... | collective-permute-start | bytes 1966088 | tf_op jit(solution)/shard_map/ppermute | solution.py:310
  19.1 6.8 %collective-permute-start.3 = (bf16[160,1024]{1,0:T(8,128)(2,1)S(1)}, bf16[160,1024]{1,0:T(8,128)(2,1)S(1)}, u32[]{:S(2)}, u32[]{:S(2)}) collective-permute-start(bf16[160,1024]{1,0:T(8,128)(2,1)S(1)} %collective-permute-done.1.refs_1_), channel_id=1, source_target_pairs={{0,4},{4,0},{8,12},{12,8},{16,20},{20,16},{24,28},{28,24},{1,5},{5... | collective-permute-start | bytes 983048 | tf_op jit(solution)/shard_map/ppermute | solution.py:311
  21.0 14.6 %collective-permute-start.8 = (bf16[160,1024]{1,0:T(8,128)(2,1)S(1)}, bf16[160,1024]{1,0:T(8,128)(2,1)S(1)}, u32[]{:S(2)}, u32[]{:S(2)}) collective-permute-start(bf16[160,1024]{1,0:T(8,128)(2,1)S(1)} %bitcast.9), channel_id=1, source_target_pairs={{0,8},{4,28},{8,16},{12,4},{16,24},{20,12},{24,0},{28,20},{1,9},{5... | collective-permute-start | bytes 983048 | tf_op jit(solution)/shard_map/ppermute | solution.py:313
  22.3 15.0 %collective-permute-start.7 = (bf16[160,1024]{1,0:T(8,128)(2,1)S(1)}, bf16[160,1024]{1,0:T(8,128)(2,1)S(1)}, u32[]{:S(2)}, u32[]{:S(2)}) collective-permute-start(bf16[160,1024]{1,0:T(8,128)(2,1)S(1)} %bitcast.10), channel_id=1, source_target_pairs={{0,24},{4,12},{8,0},{12,20},{16,8},{20,28},{24,16},{28,4},{1,25},{... | collective-permute-start | bytes 983048 | tf_op jit(solution)/shard_map/ppermute | solution.py:312
  27.2 5.3 %collective-permute-start.6 = (bf16[2,16,1024]{2,1,0:T(8,128)(2,1)S(1)}, bf16[2,16,1024]{2,1,0:T(8,128)(2,1)S(1)}, u32[]{:S(2)}, u32[]{:S(2)}) collective-permute-start(bf16[2,16,1024]{2,1,0:T(8,128)(2,1)S(1)} %get-tuple-element.51), channel_id=1, source_target_pairs={{0,3},{1,2},{2,1},{3,0},{4,7},{5,6},{6,5},{7,4},{8,11},{9,10},{10,... | collective-permute-start | bytes 196616 | tf_op jit(solution)/shard_map/ppermute | solution.py:31
  29.5 4.3 %collective-permute-start.5 = (bf16[2,16,1024]{2,1,0:T(8,128)(2,1)S(1)}, bf16[2,16,1024]{2,1,0:T(8,128)(2,1)S(1)}, u32[]{:S(2)}, u32[]{:S(2)}) collective-permute-start(bf16[2,16,1024]{2,1,0:T(8,128)(2,1)S(1)} %get-tuple-element.51), channel_id=1, source_target_pairs={{0,2},{1,3},{2,0},{3,1},{4,6},{5,7},{6,4},{7,5},{8,10},{9,11},{10,... | collective-permute-start | bytes 196616 | tf_op jit(solution)/shard_map/ppermute | solution.py:31
  30.0 4.3 %collective-permute-start.4 = (bf16[2,16,1024]{2,1,0:T(8,128)(2,1)S(1)}, bf16[2,16,1024]{2,1,0:T(8,128)(2,1)S(1)}, u32[]{:S(2)}, u32[]{:S(2)}) collective-permute-start(bf16[2,16,1024]{2,1,0:T(8,128)(2,1)S(1)} %get-tuple-element.51), channel_id=1, source_target_pairs={{0,1},{1,0},{2,3},{3,2},{4,5},{5,4},{6,7},{7,6},{8,9},{9,8},{10,11... | collective-permute-start | bytes 196616 | tf_op jit(solution)/shard_map/ppermute | solution.py:31
  35.5 5.5 %collective-permute-start.10 = (bf16[160,1024]{1,0:T(8,128)(2,1)S(1)}, bf16[160,1024]{1,0:T(8,128)(2,1)S(1)}, u32[]{:S(2)}, u32[]{:S(2)}) collective-permute-start(bf16[160,1024]{1,0:T(8,128)(2,1)S(1)} %get-tuple-element.57), channel_id=1, source_target_pairs={{0,4},{4,0},{8,12},{12,8},{16,20},{20,16},{24,28},{28,24},{1,5},{5... | collective-permute-start | bytes 983048 | tf_op jit(solution)/shard_map/ppermute | solution.py:319
  37.3 4.9 %collective-permute-start.9 = (bf16[160,1024]{1,0:T(8,128)(2,1)S(1)}, bf16[160,1024]{1,0:T(8,128)(2,1)S(1)}, u32[]{:S(2)}, u32[]{:S(2)}) collective-permute-start(bf16[160,1024]{1,0:T(8,128)(2,1)S(1)} %collective-permute-done.7.refs_0_), channel_id=1, source_target_pairs={{0,4},{4,0},{8,12},{12,8},{16,20},{20,16},{24,28},{28,24},{1,5},{5... | collective-permute-start | bytes 983048 | tf_op jit(solution)/shard_map/ppermute | solution.py:321
  37.7 15.7 %collective-permute-start.18 = (bf16[160,1024]{1,0:T(8,128)(2,1)S(1)}, bf16[160,1024]{1,0:T(8,128)(2,1)S(1)}, u32[]{:S(2)}, u32[]{:S(2)}) collective-permute-start(bf16[160,1024]{1,0:T(8,128)(2,1)S(1)} %get-tuple-element.69), channel_id=1, source_target_pairs={{0,24},{4,12},{8,0},{12,20},{16,8},{20,28},{24,16},{28,4},{1,25},{... | collective-permute-start | bytes 983048 | tf_op jit(solution)/shard_map/ppermute | solution.py:320
  41.5 16.5 %collective-permute-start.17 = (bf16[160,1024]{1,0:T(8,128)(2,1)S(1)}, bf16[160,1024]{1,0:T(8,128)(2,1)S(1)}, u32[]{:S(2)}, u32[]{:S(2)}) collective-permute-start(bf16[160,1024]{1,0:T(8,128)(2,1)S(1)} %backward_through.2), channel_id=1, source_target_pairs={{0,8},{4,28},{8,16},{12,4},{16,24},{20,12},{24,0},{28,20},{1,9},{5... | collective-permute-start | bytes 983048 | tf_op jit(solution)/shard_map/ppermute | solution.py:326
  43.5 5.7 %collective-permute-start.13 = (bf16[2,16,1024]{2,1,0:T(8,128)(2,1)S(1)}, bf16[2,16,1024]{2,1,0:T(8,128)(2,1)S(1)}, u32[]{:S(2)}, u32[]{:S(2)}) collective-permute-start(bf16[2,16,1024]{2,1,0:T(8,128)(2,1)S(1)} %get-tuple-element.61), channel_id=1, source_target_pairs={{0,3},{1,2},{2,1},{3,0},{4,7},{5,6},{6,5},{7,4},{8,11},{9,10},{10,... | collective-permute-start | bytes 196616 | tf_op jit(solution)/shard_map/ppermute | solution.py:31
  46.0 5.0 %collective-permute-start.12 = (bf16[2,16,1024]{2,1,0:T(8,128)(2,1)S(1)}, bf16[2,16,1024]{2,1,0:T(8,128)(2,1)S(1)}, u32[]{:S(2)}, u32[]{:S(2)}) collective-permute-start(bf16[2,16,1024]{2,1,0:T(8,128)(2,1)S(1)} %get-tuple-element.61), channel_id=1, source_target_pairs={{0,2},{1,3},{2,0},{3,1},{4,6},{5,7},{6,4},{7,5},{8,10},{9,11},{10,... | collective-permute-start | bytes 196616 | tf_op jit(solution)/shard_map/ppermute | solution.py:31
  46.5 4.7 %collective-permute-start.11 = (bf16[2,16,1024]{2,1,0:T(8,128)(2,1)S(1)}, bf16[2,16,1024]{2,1,0:T(8,128)(2,1)S(1)}, u32[]{:S(2)}, u32[]{:S(2)}) collective-permute-start(bf16[2,16,1024]{2,1,0:T(8,128)(2,1)S(1)} %get-tuple-element.61), channel_id=1, source_target_pairs={{0,1},{1,0},{2,3},{3,2},{4,5},{5,4},{6,7},{7,6},{8,9},{9,8},{10,11... | collective-permute-start | bytes 196616 | tf_op jit(solution)/shard_map/ppermute | solution.py:31
  52.5 5.6 %collective-permute-start.14 = (bf16[80,1024]{1,0:T(8,128)(2,1)S(1)}, bf16[80,1024]{1,0:T(8,128)(2,1)S(1)}, u32[]{:S(2)}, u32[]{:S(2)}) collective-permute-start(bf16[80,1024]{1,0:T(8,128)(2,1)S(1)} %get-tuple-element.64), channel_id=1, source_target_pairs={{0,4},{4,0},{8,12},{12,8},{16,20},{20,16},{24,28},{28,24},{1,5},{5... | collective-permute-start | bytes 491528 | tf_op jit(solution)/shard_map/ppermute | solution.py:330
  52.9 5.1 %collective-permute-start.15 = (bf16[80,1024]{1,0:T(8,128)(2,1)S(1)}, bf16[80,1024]{1,0:T(8,128)(2,1)S(1)}, u32[]{:S(2)}, u32[]{:S(2)}) collective-permute-start(bf16[80,1024]{1,0:T(8,128)(2,1)S(1)} %get-tuple-element.65), channel_id=1, source_target_pairs={{0,4},{4,0},{8,12},{12,8},{16,20},{20,16},{24,28},{28,24},{1,5},{5... | collective-permute-start | bytes 491528 | tf_op jit(solution)/shard_map/ppermute | solution.py:330
  53.1 10.2 %collective-permute-start.22 = (bf16[160,1024]{1,0:T(8,128)(2,1)S(1)}, bf16[160,1024]{1,0:T(8,128)(2,1)S(1)}, u32[]{:S(2)}, u32[]{:S(2)}) collective-permute-start(bf16[160,1024]{1,0:T(8,128)(2,1)S(1)} %get-tuple-element.73), channel_id=1, source_target_pairs={{0,4},{4,0},{8,12},{12,8},{16,20},{20,16},{24,28},{28,24},{1,5},{5... | collective-permute-start | bytes 983048 | tf_op jit(solution)/shard_map/ppermute | solution.py:327
  53.4 12.9 %collective-permute-start.16 = (bf16[160,1024]{1,0:T(8,128)(2,1)S(1)}, bf16[160,1024]{1,0:T(8,128)(2,1)S(1)}, u32[]{:S(2)}, u32[]{:S(2)}) collective-permute-start(bf16[160,1024]{1,0:T(8,128)(2,1)S(1)} %get-tuple-element.68), channel_id=1, source_target_pairs={{0,24},{4,12},{8,0},{12,20},{16,8},{20,28},{24,16},{28,4},{1,25},{... | collective-permute-start | bytes 983048 | tf_op jit(solution)/shard_map/ppermute | solution.py:331
  58.7 14.7 %collective-permute-start.19 = (bf16[160,1024]{1,0:T(8,128)(2,1)S(1)}, bf16[160,1024]{1,0:T(8,128)(2,1)S(1)}, u32[]{:S(2)}, u32[]{:S(2)}) collective-permute-start(bf16[160,1024]{1,0:T(8,128)(2,1)S(1)} %backward_through.3), channel_id=1, source_target_pairs={{0,8},{4,28},{8,16},{12,4},{16,24},{20,12},{24,0},{28,20},{1,9},{5... | collective-permute-start | bytes 983048 | tf_op jit(solution)/shard_map/ppermute | solution.py:332
  60.2 4.1 %collective-permute-start.20 = (bf16[80,1024]{1,0:T(8,128)(2,1)S(1)}, bf16[80,1024]{1,0:T(8,128)(2,1)S(1)}, u32[]{:S(2)}, u32[]{:S(2)}) collective-permute-start(bf16[80,1024]{1,0:T(8,128)(2,1)S(1)} %get-tuple-element.71), channel_id=1, source_target_pairs={{0,4},{4,0},{8,12},{12,8},{16,20},{20,16},{24,28},{28,24},{1,5},{5... | collective-permute-start | bytes 491528 | tf_op jit(solution)/shard_map/ppermute | solution.py:334
  62.5 1.8 %collective-permute-start.21 = (bf16[80,1024]{1,0:T(8,128)(2,1)S(1)}, bf16[80,1024]{1,0:T(8,128)(2,1)S(1)}, u32[]{:S(2)}, u32[]{:S(2)}) collective-permute-start(bf16[80,1024]{1,0:T(8,128)(2,1)S(1)} %get-tuple-element.72), channel_id=1, source_target_pairs={{0,4},{4,0},{8,12},{12,8},{16,20},{20,16},{24,28},{28,24},{1,5},{5... | collective-permute-start | bytes 491528 | tf_op jit(solution)/shard_map/ppermute | solution.py:334
  (2 other events, 13.4 us)

commit v2 on v1

--- a/solution.py
+++ b/solution.py
@@ -7,6 +7,7 @@
 from jax.sharding import PartitionSpec as P
 
 CHUNKS = 2
+HEAVY = 100 * 10**9
 VMEM_LIMIT = 20 * 1024 * 1024
 OWN, PARTNER, EARLY, SWAPPED, LATE = range(5)
 PLACES = {"partner": PARTNER, "early": EARLY, "late": LATE}
@@ -41,7 +42,7 @@
     return pltpu.with_memory_space_constraint(value, pltpu.VMEM)
 
 
-def call(body, meta, operands, outs, name, scratch=(), spaces=None):
+def call(body, meta, operands, outs, name, scratch=(), spaces=None, flops=0):
     spaces = spaces or [pltpu.VMEM] * len(operands)
     return pl.pallas_call(
         body,
@@ -51,7 +52,7 @@
         out_shape=outs,
         scratch_shapes=scratch,
         compiler_params=pltpu.CompilerParams(vmem_limit_bytes=VMEM_LIMIT),
-        cost_estimate=pl.CostEstimate(flops=0, bytes_accessed=0, transcendentals=0),
+        cost_estimate=pl.CostEstimate(flops=flops, bytes_accessed=0, transcendentals=0),
         name=name,
     )(meta, *operands)
 
@@ -282,10 +283,10 @@
         [through] = call(backward_through, meta, (turned, adjoint_in, *swap), [rows_half], "backward_through")
         return through
 
-    def rest(pieces, adjoint_in, *others):
+    def rest(pieces, adjoint_in, *others, flops=0):
         *second, kept = call(
             backward_rest, meta, (held, after(adjoint_in, *others)), [*cut(pieces), rows_full],
-            "backward_rest",
+            "backward_rest", flops=flops,
         )
         return second, kept
 
@@ -322,7 +323,7 @@
     total1 = add(1, near1, "forward_mid", early=early1, late=late1)
     increment1, sent1 = observe(1, total1, swapped1)
     through0 = add_through(adjoint0, swap0)
-    second0, kept0 = rest(1, adjoint0, through0)
+    second0, kept0 = rest(1, adjoint0, through0, direct0, flops=HEAVY)
     through0 = lax.ppermute(through0, "tile", outward)
     second0 = [lax.ppermute(v, "tile", across) for v in second0]
     terms1 = member_terms(increment1, sent1, groups)

time: 74.3 us -> 72.4 us (0.974); the launches traced: 74.4 us -> 71.6 us
  starting transfers between devices: 29.8 us -> 26.1 us
  waiting for transfers between devices: 20.2 us -> 21.3 us
    ppermute x1, waiting for transfers between devices: 2.05 us -> 7.14 us  [shards(): direct1 = lax.ppermute(direct1, 'tile', inward)]
    ppermute x1, waiting for transfers between devices: 7.03 us -> 2.5 us  [shards(): lax.ppermute(add_through(after(adjoint1, through0, direct0), swap1), 'til...]
    ppermute x1, starting transfers between devices: 4.61 us -> 2.32 us  [shards(): direct1 = lax.ppermute(direct1, 'tile', inward)]
    ppermute x2, starting transfers between devices: 2.44 us -> 0.57 us  [shards(): second1 = [lax.ppermute(v, 'tile', across) for v in second1]]
    ppermute x1, waiting for transfers between devices: 0.01 us -> 1.15 us  [shards(): through0 = lax.ppermute(through0, 'tile', outward)]
  transfers between devices with their start and end apart: 23 -> 23, of which waited for: 11 -> 13; matrix products, arithmetic and copies ran while one was open for 3% -> 3% of each run, Pallas kernels for 24% -> 25%
where the time goes in v2:
time: 72.4 us; the launch traced here: 71.6 us
  starting transfers between devices  26.1 us (36%)
  waiting for transfers between devices  21.3 us (29%)
  Pallas kernels  18.7 us (26%)
  local copies, waits for them, and re-layouts  2.29 us (3%)
  between operations  2.16 us (3%)
  other arithmetic  0.96 us (1%)
    pallas_call x12, Pallas kernels, call(): pl.pallas_call(body, in_specs=[pl.BlockSpec(memory_space=pltpu.SMEM)] + [...  16.6 us
    ppermute x1, waiting for transfers between devices, shards(): direct1 = lax.ppermute(direct1, 'tile', inward)  7.14 us
    ppermute x6, starting transfers between devices, member_terms(): terms.append(lax.ppermute(sent, 'member', pairs))  7.11 us
    ppermute x6, waiting for transfers between devices, member_terms(): terms.append(lax.ppermute(sent, 'member', pairs))  5.16 us
    ppermute x1, starting transfers between devices, shards(): direct0 = lax.ppermute(direct0, 'tile', inward)  3.63 us
    ppermute x1, waiting for transfers between devices, shards(): early0 = lax.ppermute(own[0], 'tile', inward)  3.59 us
    ppermute x1, starting transfers between devices, shards(): late0 = lax.ppermute(own[0], 'tile', outward)  3.08 us
    ppermute x1, waiting for transfers between devices, shards(): lax.ppermute(add_through(after(adjoint1, through0, direct0), swap1), 'til...  2.5 us
  transfers between devices with their start and end apart: 23, of which 13 were waited for; matrix products, arithmetic and copies ran while one was open for 3% of the time, Pallas kernels for 25%

profile of v2, /device:TPU:0, one launch (start us, length us, event | category | flops | bytes accessed | tf_op | source)
XLA Modules:
  0.0 71.6 jit_solution(8975778946955105462)
XLA Ops:
  0.7 1.1 %slice.15 = bf16[10,16,1024]{2,1,0:T(8,128)(2,1)S(1)} slice(f32[10,32,1024]{2,1,0:T(8,128)} %coeffs.3), slice={[0:10], [0:16], [0:1024]} | slice | bytes 655360 | tf_op jit(solution)/shard_map/slice | solution.py:239
  1.8 3.1 %collective-permute-start.2 = (bf16[160,1024]{1,0:T(8,128)(2,1)S(1)}, bf16[160,1024]{1,0:T(8,128)(2,1)S(1)}, u32[]{:S(2)}, u32[]{:S(2)}) collective-permute-start(bf16[160,1024]{1,0:T(8,128)(2,1)S(1)} %bitcast.11), channel_id=1, source_target_pairs={{0,8},{4,28},{8,16},{12,4},{16,24},{20,12},{24,0},{28,20},{1,9},{5... | collective-permute-start | bytes 983048 | tf_op jit(solution)/shard_map/ppermute | solution.py:310
  4.9 2.1 %collective-permute-start.1 = (bf16[160,1024]{1,0:T(8,128)(2,1)S(1)}, bf16[160,1024]{1,0:T(8,128)(2,1)S(1)}, u32[]{:S(2)}, u32[]{:S(2)}) collective-permute-start(bf16[160,1024]{1,0:T(8,128)(2,1)S(1)} %bitcast.12), channel_id=1, source_target_pairs={{0,24},{4,12},{8,0},{12,20},{16,8},{20,28},{24,16},{28,4},{1,25},{... | collective-permute-start | bytes 983048 | tf_op jit(solution)/shard_map/ppermute | solution.py:309
  8.3 1.1 %slice.14 = bf16[10,16,1024]{2,1,0:T(8,128)(2,1)S(1)} slice(f32[10,32,1024]{2,1,0:T(8,128)} %coeffs.3), slice={[0:10], [16:32], [0:1024]} | slice | bytes 655360 | tf_op jit(solution)/shard_map/slice | solution.py:239
  9.7 5.4 %load.1 = (f32[160,1024]{1,0:T(8,128)S(1)}, f32[160,1024]{1,0:T(8,128)S(1)}, bf16[5,1024,1024]{2,1,0:T(8,128)(2,1)S(1)}, bf16[2,10,32,1024]{3,2,1,0:T(8,128)(2,1...) custom-call(s32[12]{0:T(128)S(1)} %pad_add_fusion.meta, ...), custom_call_target="tpu_custom_call" | custom-call | tf_op jit(solution)/shard_map/load/pallas_call | solution.py:47
  15.5 3.6 %collective-permute-done.1.refs_1_ = bf16[160,1024]{1,0:T(8,128)(2,1)S(1)} collective-permute-done((bf16[160,1024]{1,0:T(8,128)(2,1)S(1)}, bf16[160,1024]{1,0:T(8,128)(2,1)S(1)}, u32[]{:S(2)}, u32[]{:S(2)}) %collective-permute-start.1) | collective-permute-done | bytes 327712 | tf_op jit(solution)/shard_map/ppermute | solution.py:309
  19.1 1.8 %collective-permute-start.3 = (bf16[160,1024]{1,0:T(8,128)(2,1)S(1)}, bf16[160,1024]{1,0:T(8,128)(2,1)S(1)}, u32[]{:S(2)}, u32[]{:S(2)}) collective-permute-start(bf16[160,1024]{1,0:T(8,128)(2,1)S(1)} %collective-permute-done.1.refs_1_), channel_id=1, source_target_pairs={{0,4},{4,0},{8,12},{12,8},{16,20},{20,16},{24,28},{28,24},{1,5},{5... | collective-permute-start | bytes 983048 | tf_op jit(solution)/shard_map/ppermute | solution.py:312
  21.0 1.3 %collective-permute-start.8 = (bf16[160,1024]{1,0:T(8,128)(2,1)S(1)}, bf16[160,1024]{1,0:T(8,128)(2,1)S(1)}, u32[]{:S(2)}, u32[]{:S(2)}) collective-permute-start(bf16[160,1024]{1,0:T(8,128)(2,1)S(1)} %bitcast.9), channel_id=1, source_target_pairs={{0,8},{4,28},{8,16},{12,4},{16,24},{20,12},{24,0},{28,20},{1,9},{5... | collective-permute-start | bytes 983048 | tf_op jit(solution)/shard_map/ppermute | solution.py:314
  22.3 2.5 %collective-permute-start.7 = (bf16[160,1024]{1,0:T(8,128)(2,1)S(1)}, bf16[160,1024]{1,0:T(8,128)(2,1)S(1)}, u32[]{:S(2)}, u32[]{:S(2)}) collective-permute-start(bf16[160,1024]{1,0:T(8,128)(2,1)S(1)} %bitcast.10), channel_id=1, source_target_pairs={{0,24},{4,12},{8,0},{12,20},{16,8},{20,28},{24,16},{28,4},{1,25},{... | collective-permute-start | bytes 983048 | tf_op jit(solution)/shard_map/ppermute | solution.py:313
  24.8 1.1 %forward_mid.2.before = f32[160,1024]{1,0:T(8,128)S(1)} custom-call(s32[12]{0:T(128)S(1)} %pad_add_fusion.meta, bf16[5,1024,1024]{2,1,0:T(8,128)(2,1)S(1)} %get-tuple-element.43.held, f32[160,1024]{1,0:T(8,128)S(1)} %get-tuple-element.44.before, bf16[320,1024]{1,0:T(8,128)(2,1)S(1)} %collective-permute-done.refs_0_, ...), custom_call_target="tpu_custom_call" | custom-call | tf_op jit(solution)/shard_map/forward_mid/pallas_call | solution.py:47
  25.9 1.3 %forward_far.2 = (f32[2,16,1024]{2,1,0:T(8,128)S(1)}, bf16[2,16,1024]{2,1,0:T(8,128)(2,1)S(1)}) custom-call(s32[12]{0:T(128)S(1)} %pad_add_fusion.meta, bf16[5,1024,1024]{2,1,0:T(8,128)(2,1)S(1)} %get-tuple-element.43.held, bf16[2,10,32,1024]{3,2,1,0:T(8,128)(2,1)S(1)} %get-tuple-element.40.perturb, f32[160,1024]{1,0:T(8,128)S(1)} %forward_mid.2.before, ...), custom_call_target="tpu_custom_call" | custom-call | tf_op jit(solution)/shard_map/forward_far/pallas_call | solution.py:47
  27.2 2.3 %collective-permute-start.6 = (bf16[2,16,1024]{2,1,0:T(8,128)(2,1)S(1)}, bf16[2,16,1024]{2,1,0:T(8,128)(2,1)S(1)}, u32[]{:S(2)}, u32[]{:S(2)}) collective-permute-start(bf16[2,16,1024]{2,1,0:T(8,128)(2,1)S(1)} %get-tuple-element.51), channel_id=1, source_target_pairs={{0,3},{1,2},{2,1},{3,0},{4,7},{5,6},{6,5},{7,4},{8,11},{9,10},{10,... | collective-permute-start | bytes 196616 | tf_op jit(solution)/shard_map/ppermute | solution.py:32
  31.3 1.4 %collective-permute-done.6.refs_3_ = bf16[2,16,1024]{2,1,0:T(8,128)(2,1)S(1)} collective-permute-done((bf16[2,16,1024]{2,1,0:T(8,128)(2,1)S(1)}, bf16[2,16,1024]{2,1,0:T(8,128)(2,1)S(1)}, u32[]{:S(2)}, u32[]{:S(2)}) %collective-permute-start.6) | collective-permute-done | bytes 65568 | tf_op jit(solution)/shard_map/ppermute | solution.py:32
  34.2 1.8 %backward_first.2 = (bf16[160,1024]{1,0:T(8,128)(2,1)S(1)}, bf16[160,1024]{1,0:T(8,128)(2,1)S(1)}, bf16[160,1024]{1,0:T(8,128)(2,1)S(1)}, f32[2,16,256]{2,1,0:T(8,128)S(1)}) custom-call(s32[12]{0:T(128)S(1)} %pad_add_fusion.meta, bf16[3,1024,1024]{2,1,0:T(8,128)(2,1)S(1)} %get-tuple-element.39.turned, ...), custom_call_target="tpu_custom_call" | custom-call | tf_op jit(solution)/shard_map/backward_first/pallas_call | solution.py:47
  36.0 1.3 %collective-permute-done.7.refs_0_ = bf16[160,1024]{1,0:T(8,128)(2,1)S(1)} collective-permute-done((bf16[160,1024]{1,0:T(8,128)(2,1)S(1)}, bf16[160,1024]{1,0:T(8,128)(2,1)S(1)}, u32[]{:S(2)}, u32[]{:S(2)}) %collective-permute-start.7) | collective-permute-done | bytes 327712 | tf_op jit(solution)/shard_map/ppermute | solution.py:313
  37.8 3.6 %collective-permute-start.11 = (bf16[160,1024]{1,0:T(8,128)(2,1)S(1)}, bf16[160,1024]{1,0:T(8,128)(2,1)S(1)}, u32[]{:S(2)}, u32[]{:S(2)}) collective-permute-start(bf16[160,1024]{1,0:T(8,128)(2,1)S(1)} %get-tuple-element.58), channel_id=1, source_target_pairs={{0,24},{4,12},{8,0},{12,20},{16,8},{20,28},{24,16},{28,4},{1,25},{... | collective-permute-start | bytes 983048 | tf_op jit(solution)/shard_map/ppermute | solution.py:321
  41.5 1.1 %forward_mid.3.before = f32[160,1024]{1,0:T(8,128)S(1)} custom-call(s32[12]{0:T(128)S(1)} %pad_add_fusion.meta, bf16[5,1024,1024]{2,1,0:T(8,128)(2,1)S(1)} %get-tuple-element.43.held, f32[160,1024]{1,0:T(8,128)S(1)} %forward_near.1.before, bf16[160,1024]{1,0:T(8,128)(2,1)S(1)} %collective-permute-done.7.refs_0_, ...), custom_call_target="tpu_custom_call" | custom-call | tf_op jit(solution)/shard_map/forward_mid/pallas_call | solution.py:47
  42.6 1.3 %forward_far.3 = (f32[2,16,1024]{2,1,0:T(8,128)S(1)}, bf16[2,16,1024]{2,1,0:T(8,128)(2,1)S(1)}) custom-call(s32[12]{0:T(128)S(1)} %pad_add_fusion.meta, bf16[5,1024,1024]{2,1,0:T(8,128)(2,1)S(1)} %get-tuple-element.43.held, bf16[2,10,32,1024]{3,2,1,0:T(8,128)(2,1)S(1)} %get-tuple-element.40.perturb, f32[160,1024]{1,0:T(8,128)S(1)} %forward_mid.3.before, ...), custom_call_target="tpu_custom_call" | custom-call | tf_op jit(solution)/shard_map/forward_far/pallas_call | solution.py:47
  43.9 2.5 %collective-permute-start.14 = (bf16[2,16,1024]{2,1,0:T(8,128)(2,1)S(1)}, bf16[2,16,1024]{2,1,0:T(8,128)(2,1)S(1)}, u32[]{:S(2)}, u32[]{:S(2)}) collective-permute-start(bf16[2,16,1024]{2,1,0:T(8,128)(2,1)S(1)} %get-tuple-element.62), channel_id=1, source_target_pairs={{0,3},{1,2},{2,1},{3,0},{4,7},{5,6},{6,5},{7,4},{8,11},{9,10},{10,... | collective-permute-start | bytes 196616 | tf_op jit(solution)/shard_map/ppermute | solution.py:32
  51.2 1.8 %backward_first.3 = (bf16[160,1024]{1,0:T(8,128)(2,1)S(1)}, bf16[80,1024]{1,0:T(8,128)(2,1)S(1)}, bf16[80,1024]{1,0:T(8,128)(2,1)S(1)}, bf16[160,1024]{1,0:T(8,128)(2,1)S(1)}, f32[2,16,256]{2,1,0:T(8,128)S(1)}) custom-call(s32[12]{0:T(128)S(1)} %pad_add_fusion.meta, bf16[3,1024,1024]{2,1,0:T(8,128)(2,1)S(1)} %get-tuple-element.39.turned, ...), custom_call_target="tpu_custom_call" | custom-call | tf_op jit(solution)/shard_map/backward_first/pallas_call | solution.py:47
  53.6 2.3 %collective-permute-start.17 = (bf16[160,1024]{1,0:T(8,128)(2,1)S(1)}, bf16[160,1024]{1,0:T(8,128)(2,1)S(1)}, u32[]{:S(2)}, u32[]{:S(2)}) collective-permute-start(bf16[160,1024]{1,0:T(8,128)(2,1)S(1)} %get-tuple-element.69), channel_id=1, source_target_pairs={{0,24},{4,12},{8,0},{12,20},{16,8},{20,28},{24,16},{28,4},{1,25},{... | collective-permute-start | bytes 983048 | tf_op jit(solution)/shard_map/ppermute | solution.py:332
  55.9 1.1 %collective-permute-done.18.through = bf16[160,1024]{1,0:T(8,128)(2,1)S(1)} collective-permute-done((bf16[160,1024]{1,0:T(8,128)(2,1)S(1)}, bf16[160,1024]{1,0:T(8,128)(2,1)S(1)}, u32[]{:S(2)}, u32[]{:S(2)}) %collective-permute-start.18) | collective-permute-done | bytes 327712 | tf_op jit(solution)/shard_map/ppermute | solution.py:327
  60.9 7.1 %collective-permute-done.17.direct = bf16[160,1024]{1,0:T(8,128)(2,1)S(1)} collective-permute-done((bf16[160,1024]{1,0:T(8,128)(2,1)S(1)}, bf16[160,1024]{1,0:T(8,128)(2,1)S(1)}, u32[]{:S(2)}, u32[]{:S(2)}) %collective-permute-start.17) | collective-permute-done | bytes 327712 | tf_op jit(solution)/shard_map/ppermute | solution.py:332
  68.1 2.5 %collective-permute-done.19.through = bf16[160,1024]{1,0:T(8,128)(2,1)S(1)} collective-permute-done((bf16[160,1024]{1,0:T(8,128)(2,1)S(1)}, bf16[160,1024]{1,0:T(8,128)(2,1)S(1)}, u32[]{:S(2)}, u32[]{:S(2)}) %collective-permute-start.19) | collective-permute-done | bytes 327712 | tf_op jit(solution)/shard_map/ppermute | solution.py:333
  (50 shorter events, 14.9 us)
Async XLA Ops:
  0.6 8.8 %copy-start.2 = (s32[5]{0:T(128)S(1)}, s32[5]{0:T(128)}, u32[]{:S(2)}) copy-start(s32[5]{0:T(128)} %constant.44.clone) | copy-start | bytes 64
  1.8 13.7 %collective-permute-start.2 = (bf16[160,1024]{1,0:T(8,128)(2,1)S(1)}, bf16[160,1024]{1,0:T(8,128)(2,1)S(1)}, u32[]{:S(2)}, u32[]{:S(2)}) collective-permute-start(bf16[160,1024]{1,0:T(8,128)(2,1)S(1)} %bitcast.11), channel_id=1, source_target_pairs={{0,8},{4,28},{8,16},{12,4},{16,24},{20,12},{24,0},{28,20},{1,9},{5... | collective-permute-start | bytes 983048 | tf_op jit(solution)/shard_map/ppermute | solution.py:310
  4.9 14.2 %collective-permute-start.1 = (bf16[160,1024]{1,0:T(8,128)(2,1)S(1)}, bf16[160,1024]{1,0:T(8,128)(2,1)S(1)}, u32[]{:S(2)}, u32[]{:S(2)}) collective-permute-start(bf16[160,1024]{1,0:T(8,128)(2,1)S(1)} %bitcast.12), channel_id=1, source_target_pairs={{0,24},{4,12},{8,0},{12,20},{16,8},{20,28},{24,16},{28,4},{1,25},{... | collective-permute-start | bytes 983048 | tf_op jit(solution)/shard_map/ppermute | solution.py:309
  15.2 9.6 %collective-permute-start = (bf16[320,1024]{1,0:T(8,128)(2,1)S(1)}, bf16[320,1024]{1,0:T(8,128)(2,1)S(1)}, u32[]{:S(2)}, u32[]{:S(2)}) collective-permute-start(bf16[320,1024]{1,0:T(8,128)(2,1)S(1)} %pad_maximum_fusion), channel_id=1, source_target_pairs={{0,4},{4,0},{8,12},{12,8},{16,20},{20,16},{24,28},{28,24},{1,5},{5... | collective-permute-start | bytes 1966088 | tf_op jit(solution)/shard_map/ppermute | solution.py:311
  19.1 6.8 %collective-permute-start.3 = (bf16[160,1024]{1,0:T(8,128)(2,1)S(1)}, bf16[160,1024]{1,0:T(8,128)(2,1)S(1)}, u32[]{:S(2)}, u32[]{:S(2)}) collective-permute-start(bf16[160,1024]{1,0:T(8,128)(2,1)S(1)} %collective-permute-done.1.refs_1_), channel_id=1, source_target_pairs={{0,4},{4,0},{8,12},{12,8},{16,20},{20,16},{24,28},{28,24},{1,5},{5... | collective-permute-start | bytes 983048 | tf_op jit(solution)/shard_map/ppermute | solution.py:312
  21.0 15.0 %collective-permute-start.8 = (bf16[160,1024]{1,0:T(8,128)(2,1)S(1)}, bf16[160,1024]{1,0:T(8,128)(2,1)S(1)}, u32[]{:S(2)}, u32[]{:S(2)}) collective-permute-start(bf16[160,1024]{1,0:T(8,128)(2,1)S(1)} %bitcast.9), channel_id=1, source_target_pairs={{0,8},{4,28},{8,16},{12,4},{16,24},{20,12},{24,0},{28,20},{1,9},{5... | collective-permute-start | bytes 983048 | tf_op jit(solution)/shard_map/ppermute | solution.py:314
  22.3 15.0 %collective-permute-start.7 = (bf16[160,1024]{1,0:T(8,128)(2,1)S(1)}, bf16[160,1024]{1,0:T(8,128)(2,1)S(1)}, u32[]{:S(2)}, u32[]{:S(2)}) collective-permute-start(bf16[160,1024]{1,0:T(8,128)(2,1)S(1)} %bitcast.10), channel_id=1, source_target_pairs={{0,24},{4,12},{8,0},{12,20},{16,8},{20,28},{24,16},{28,4},{1,25},{... | collective-permute-start | bytes 983048 | tf_op jit(solution)/shard_map/ppermute | solution.py:313
  27.2 5.5 %collective-permute-start.6 = (bf16[2,16,1024]{2,1,0:T(8,128)(2,1)S(1)}, bf16[2,16,1024]{2,1,0:T(8,128)(2,1)S(1)}, u32[]{:S(2)}, u32[]{:S(2)}) collective-permute-start(bf16[2,16,1024]{2,1,0:T(8,128)(2,1)S(1)} %get-tuple-element.51), channel_id=1, source_target_pairs={{0,3},{1,2},{2,1},{3,0},{4,7},{5,6},{6,5},{7,4},{8,11},{9,10},{10,... | collective-permute-start | bytes 196616 | tf_op jit(solution)/shard_map/ppermute | solution.py:32
  29.5 4.3 %collective-permute-start.5 = (bf16[2,16,1024]{2,1,0:T(8,128)(2,1)S(1)}, bf16[2,16,1024]{2,1,0:T(8,128)(2,1)S(1)}, u32[]{:S(2)}, u32[]{:S(2)}) collective-permute-start(bf16[2,16,1024]{2,1,0:T(8,128)(2,1)S(1)} %get-tuple-element.51), channel_id=1, source_target_pairs={{0,2},{1,3},{2,0},{3,1},{4,6},{5,7},{6,4},{7,5},{8,10},{9,11},{10,... | collective-permute-start | bytes 196616 | tf_op jit(solution)/shard_map/ppermute | solution.py:32
  30.0 4.3 %collective-permute-start.4 = (bf16[2,16,1024]{2,1,0:T(8,128)(2,1)S(1)}, bf16[2,16,1024]{2,1,0:T(8,128)(2,1)S(1)}, u32[]{:S(2)}, u32[]{:S(2)}) collective-permute-start(bf16[2,16,1024]{2,1,0:T(8,128)(2,1)S(1)} %get-tuple-element.51), channel_id=1, source_target_pairs={{0,1},{1,0},{2,3},{3,2},{4,5},{5,4},{6,7},{7,6},{8,9},{9,8},{10,11... | collective-permute-start | bytes 196616 | tf_op jit(solution)/shard_map/ppermute | solution.py:32
  37.3 5.3 %collective-permute-start.9 = (bf16[160,1024]{1,0:T(8,128)(2,1)S(1)}, bf16[160,1024]{1,0:T(8,128)(2,1)S(1)}, u32[]{:S(2)}, u32[]{:S(2)}) collective-permute-start(bf16[160,1024]{1,0:T(8,128)(2,1)S(1)} %collective-permute-done.7.refs_0_), channel_id=1, source_target_pairs={{0,4},{4,0},{8,12},{12,8},{16,20},{20,16},{24,28},{28,24},{1,5},{5... | collective-permute-start | bytes 983048 | tf_op jit(solution)/shard_map/ppermute | solution.py:322
  37.7 9.7 %collective-permute-start.10 = (bf16[160,1024]{1,0:T(8,128)(2,1)S(1)}, bf16[160,1024]{1,0:T(8,128)(2,1)S(1)}, u32[]{:S(2)}, u32[]{:S(2)}) collective-permute-start(bf16[160,1024]{1,0:T(8,128)(2,1)S(1)} %get-tuple-element.57), channel_id=1, source_target_pairs={{0,4},{4,0},{8,12},{12,8},{16,20},{20,16},{24,28},{28,24},{1,5},{5... | collective-permute-start | bytes 983048 | tf_op jit(solution)/shard_map/ppermute | solution.py:320
  37.8 10.4 %collective-permute-start.11 = (bf16[160,1024]{1,0:T(8,128)(2,1)S(1)}, bf16[160,1024]{1,0:T(8,128)(2,1)S(1)}, u32[]{:S(2)}, u32[]{:S(2)}) collective-permute-start(bf16[160,1024]{1,0:T(8,128)(2,1)S(1)} %get-tuple-element.58), channel_id=1, source_target_pairs={{0,24},{4,12},{8,0},{12,20},{16,8},{20,28},{24,16},{28,4},{1,25},{... | collective-permute-start | bytes 983048 | tf_op jit(solution)/shard_map/ppermute | solution.py:321
  43.9 5.9 %collective-permute-start.14 = (bf16[2,16,1024]{2,1,0:T(8,128)(2,1)S(1)}, bf16[2,16,1024]{2,1,0:T(8,128)(2,1)S(1)}, u32[]{:S(2)}, u32[]{:S(2)}) collective-permute-start(bf16[2,16,1024]{2,1,0:T(8,128)(2,1)S(1)} %get-tuple-element.62), channel_id=1, source_target_pairs={{0,3},{1,2},{2,1},{3,0},{4,7},{5,6},{6,5},{7,4},{8,11},{9,10},{10,... | collective-permute-start | bytes 196616 | tf_op jit(solution)/shard_map/ppermute | solution.py:32
  46.4 4.3 %collective-permute-start.13 = (bf16[2,16,1024]{2,1,0:T(8,128)(2,1)S(1)}, bf16[2,16,1024]{2,1,0:T(8,128)(2,1)S(1)}, u32[]{:S(2)}, u32[]{:S(2)}) collective-permute-start(bf16[2,16,1024]{2,1,0:T(8,128)(2,1)S(1)} %get-tuple-element.62), channel_id=1, source_target_pairs={{0,2},{1,3},{2,0},{3,1},{4,6},{5,7},{6,4},{7,5},{8,10},{9,11},{10,... | collective-permute-start | bytes 196616 | tf_op jit(solution)/shard_map/ppermute | solution.py:32
  46.9 4.3 %collective-permute-start.12 = (bf16[2,16,1024]{2,1,0:T(8,128)(2,1)S(1)}, bf16[2,16,1024]{2,1,0:T(8,128)(2,1)S(1)}, u32[]{:S(2)}, u32[]{:S(2)}) collective-permute-start(bf16[2,16,1024]{2,1,0:T(8,128)(2,1)S(1)} %get-tuple-element.62), channel_id=1, source_target_pairs={{0,1},{1,0},{2,3},{3,2},{4,5},{5,4},{6,7},{7,6},{8,9},{9,8},{10,11... | collective-permute-start | bytes 196616 | tf_op jit(solution)/shard_map/ppermute | solution.py:32
  48.0 9.0 %collective-permute-start.18 = (bf16[160,1024]{1,0:T(8,128)(2,1)S(1)}, bf16[160,1024]{1,0:T(8,128)(2,1)S(1)}, u32[]{:S(2)}, u32[]{:S(2)}) collective-permute-start(bf16[160,1024]{1,0:T(8,128)(2,1)S(1)} %backward_through.2), channel_id=1, source_target_pairs={{0,8},{4,28},{8,16},{12,4},{16,24},{20,12},{24,0},{28,20},{1,9},{5... | collective-permute-start | bytes 983048 | tf_op jit(solution)/shard_map/ppermute | solution.py:327
  52.9 4.1 %collective-permute-start.15 = (bf16[80,1024]{1,0:T(8,128)(2,1)S(1)}, bf16[80,1024]{1,0:T(8,128)(2,1)S(1)}, u32[]{:S(2)}, u32[]{:S(2)}) collective-permute-start(bf16[80,1024]{1,0:T(8,128)(2,1)S(1)} %get-tuple-element.65), channel_id=1, source_target_pairs={{0,4},{4,0},{8,12},{12,8},{16,20},{20,16},{24,28},{28,24},{1,5},{5... | collective-permute-start | bytes 491528 | tf_op jit(solution)/shard_map/ppermute | solution.py:331
  53.0 4.1 %collective-permute-start.16 = (bf16[80,1024]{1,0:T(8,128)(2,1)S(1)}, bf16[80,1024]{1,0:T(8,128)(2,1)S(1)}, u32[]{:S(2)}, u32[]{:S(2)}) collective-permute-start(bf16[80,1024]{1,0:T(8,128)(2,1)S(1)} %get-tuple-element.66), channel_id=1, source_target_pairs={{0,4},{4,0},{8,12},{12,8},{16,20},{20,16},{24,28},{28,24},{1,5},{5... | collective-permute-start | bytes 491528 | tf_op jit(solution)/shard_map/ppermute | solution.py:331
  53.5 6.4 %collective-permute-start.22 = (bf16[160,1024]{1,0:T(8,128)(2,1)S(1)}, bf16[160,1024]{1,0:T(8,128)(2,1)S(1)}, u32[]{:S(2)}, u32[]{:S(2)}) collective-permute-start(bf16[160,1024]{1,0:T(8,128)(2,1)S(1)} %get-tuple-element.73), channel_id=1, source_target_pairs={{0,4},{4,0},{8,12},{12,8},{16,20},{20,16},{24,28},{28,24},{1,5},{5... | collective-permute-start | bytes 983048 | tf_op jit(solution)/shard_map/ppermute | solution.py:328
  53.6 14.5 %collective-permute-start.17 = (bf16[160,1024]{1,0:T(8,128)(2,1)S(1)}, bf16[160,1024]{1,0:T(8,128)(2,1)S(1)}, u32[]{:S(2)}, u32[]{:S(2)}) collective-permute-start(bf16[160,1024]{1,0:T(8,128)(2,1)S(1)} %get-tuple-element.69), channel_id=1, source_target_pairs={{0,24},{4,12},{8,0},{12,20},{16,8},{20,28},{24,16},{28,4},{1,25},{... | collective-permute-start | bytes 983048 | tf_op jit(solution)/shard_map/ppermute | solution.py:332
  57.6 12.9 %collective-permute-start.19 = (bf16[160,1024]{1,0:T(8,128)(2,1)S(1)}, bf16[160,1024]{1,0:T(8,128)(2,1)S(1)}, u32[]{:S(2)}, u32[]{:S(2)}) collective-permute-start(bf16[160,1024]{1,0:T(8,128)(2,1)S(1)} %backward_through.3), channel_id=1, source_target_pairs={{0,8},{4,28},{8,16},{12,4},{16,24},{20,12},{24,0},{28,20},{1,9},{5... | collective-permute-start | bytes 983048 | tf_op jit(solution)/shard_map/ppermute | solution.py:333
  58.7 2.3 %collective-permute-start.20 = (bf16[80,1024]{1,0:T(8,128)(2,1)S(1)}, bf16[80,1024]{1,0:T(8,128)(2,1)S(1)}, u32[]{:S(2)}, u32[]{:S(2)}) collective-permute-start(bf16[80,1024]{1,0:T(8,128)(2,1)S(1)} %get-tuple-element.71), channel_id=1, source_target_pairs={{0,4},{4,0},{8,12},{12,8},{16,20},{20,16},{24,28},{28,24},{1,5},{5... | collective-permute-start | bytes 491528 | tf_op jit(solution)/shard_map/ppermute | solution.py:335
  58.7 2.2 %collective-permute-start.21 = (bf16[80,1024]{1,0:T(8,128)(2,1)S(1)}, bf16[80,1024]{1,0:T(8,128)(2,1)S(1)}, u32[]{:S(2)}, u32[]{:S(2)}) collective-permute-start(bf16[80,1024]{1,0:T(8,128)(2,1)S(1)} %get-tuple-element.72), channel_id=1, source_target_pairs={{0,4},{4,0},{8,12},{12,8},{16,20},{20,16},{24,28},{28,24},{1,5},{5... | collective-permute-start | bytes 491528 | tf_op jit(solution)/shard_map/ppermute | solution.py:335
  (2 other events, 11.0 us)

commit v3 on v2

--- a/solution.py
+++ b/solution.py
@@ -116,11 +116,16 @@
         add_times(meta, held, place, rows, out)
 
 
-def forward_far(chunk, meta, held, perturb, before, swapped, out, sent, total):
+def forward_far(chunk, meta, held, perturb, before, *refs):
+    *swapped, out, sent, total = refs
     levels = out.shape[1]
     at = slice(chunk * levels, (chunk + 1) * levels)
     total[...] = before[...]
-    add_times(meta, held, SWAPPED, swapped, total)
+    @pl.when(meta[SWAPPED] > 0)
+    def _():
+        rows = jnp.concatenate([v[...] for v in swapped])
+        total[...] += times(rows, held[SWAPPED])
+
     for t in range(out.shape[0]):
         value = sum(
             perturb[t, m, at].astype(jnp.float32) * total[m * levels:(m + 1) * levels]
@@ -196,12 +201,36 @@
     transposed_or_zero(meta, held, None, OWN, adjoint_in, outs[-1])
 
 
-def finish(pieces, coeffs, kept, direct, through, *refs):
-    second, out = refs[:pieces], refs[-1]
-    value = kept[...] + jnp.concatenate([v[...].astype(jnp.float32) for v in second])
-    for term in (direct, through):
-        value = value + term[...].astype(jnp.float32)
-    out[...] = coeffs[...] + value.reshape(out.shape)
+def backward_one(place, meta, held, adjoint_in, out):
+    transposed_or_zero(meta, held, None, place, adjoint_in, out)
+
+
+def settle(coeffs, *refs):
+    *terms, out = refs
+    value = coeffs[...].reshape(out.shape)
+    if terms[0].shape == out.shape:
+        value = value + terms[0][...].astype(jnp.float32)
+        terms = terms[1:]
+    if terms:
+        value = value + jnp.concatenate([v[...].astype(jnp.float32) for v in terms])
+    out[...] = value
+
+
+def finish(chunk, terms, *refs):
+    refs, (out, value, sent) = refs[:terms], refs[-3:]
+    members, levels, _ = value.shape
+    size = members // 2
+    copies = []
+    for k in range(2):
+        rows = slice(k * size * levels, (k + 1) * size * levels)
+        some = slice(k * size, (k + 1) * size)
+        value[some] = sum(v[rows].astype(jnp.float32) for v in refs).reshape(size, levels, -1)
+        copies.append(pltpu.make_async_copy(
+            value.at[some], out.at[some, chunk * levels:(chunk + 1) * levels], sent.at[k]
+        ))
+        copies[k].start()
+    for copy in copies:
+        copy.wait()
 
 
 def shards(coeffs, perturb, blocks, neighbours, live, obs_count, innovation, obs_weight):
@@ -260,9 +289,13 @@
         )
         return total
 
+    def forwarded(pieces, early, *others):
+        early, size = after(early, *others), rows // pieces
+        return [lax.ppermute(early[k * size:(k + 1) * size], "tile", across) for k in range(pieces)]
+
     def observe(c, total, swapped):
         return call(
-            functools.partial(forward_far, c), meta, (held, held_perturb, total, swapped),
+            functools.partial(forward_far, c), meta, (held, held_perturb, total, *swapped),
             [shape((window, part, cells), full), shape((window, part, cells), half)],
             "forward_far", [pltpu.VMEM((rows, cells), full)],
         )
@@ -283,58 +316,79 @@
         [through] = call(backward_through, meta, (turned, adjoint_in, *swap), [rows_half], "backward_through")
         return through
 
-    def rest(pieces, adjoint_in, *others, flops=0):
+    def rest(pieces, adjoint_in, *others):
         *second, kept = call(
             backward_rest, meta, (held, after(adjoint_in, *others)), [*cut(pieces), rows_full],
-            "backward_rest", flops=flops,
+            "backward_rest",
         )
         return second, kept
 
-    def finished(c, gradient, second, *terms):
-        terms += tuple(second)
-        chunk_spec = pl.BlockSpec((members, part, cells), lambda i: (0, c, 0))
+    def one(place, out, name, adjoint_in, *others, flops=0):
+        [value] = call(
+            functools.partial(backward_one, place), meta, (held, after(adjoint_in, *others)), [out], name,
+            flops=flops,
+        )
+        return value
+
+    def settled(c, *terms):
         return pl.pallas_call(
-            functools.partial(finish, len(second)),
+            settle,
             grid=(1,),
-            in_specs=[chunk_spec] + [pl.BlockSpec(v.shape, lambda i: (0, 0)) for v in terms]
+            in_specs=[pl.BlockSpec((members, part, cells), lambda i: (0, c, 0))]
+            + [pl.BlockSpec(v.shape, lambda i: (0, 0)) for v in terms],
+            out_specs=pl.BlockSpec((rows, cells), lambda i: (0, 0)),
+            out_shape=rows_full,
+            compiler_params=pltpu.CompilerParams(vmem_limit_bytes=VMEM_LIMIT),
+            cost_estimate=pl.CostEstimate(flops=0, bytes_accessed=0, transcendentals=0),
+            name="settle",
+        )(coeffs, *terms)
+
+    def finished(c, gradient, *terms):
+        return pl.pallas_call(
+            functools.partial(finish, c, len(terms)),
+            in_specs=[pl.BlockSpec(memory_space=pltpu.VMEM)] * len(terms)
             + [pl.BlockSpec(memory_space=pl.ANY)] * len(gradient),
-            out_specs=chunk_spec,
+            out_specs=pl.BlockSpec(memory_space=pl.ANY),
             out_shape=shape(coeffs.shape, full),
-            input_output_aliases={1 + len(terms): 0} if gradient else {},
+            scratch_shapes=[pltpu.VMEM((members, part, cells), full), pltpu.SemaphoreType.DMA((2,))],
+            input_output_aliases={len(terms): 0} if gradient else {},
             compiler_params=pltpu.CompilerParams(vmem_limit_bytes=VMEM_LIMIT),
             cost_estimate=pl.CostEstimate(flops=0, bytes_accessed=0, transcendentals=0),
             name="finish",
-        )(coeffs, *terms, *gradient)
+        )(*terms, *gradient)
 
     early0 = lax.ppermute(own[0], "tile", inward)
     late0 = lax.ppermute(own[0], "tile", outward)
     partner = lax.ppermute(jnp.concatenate(after(own, near[0])), "tile", across)
-    swapped0 = lax.ppermute(after(early0, late0, near[0]), "tile", across)
+    swapped0 = forwarded(2, early0, late0, near[0])
     early1 = lax.ppermute(after(own[1], early0, late0), "tile", inward)
     late1 = lax.ppermute(after(own[1], early0, late0), "tile", outward)
     total0 = add(0, near[0], "forward_mid", partner=partner, early=early0, late=late0)
     increment0, sent0 = observe(0, total0, swapped0)
     terms0 = member_terms(increment0, sent0, groups)
     near1 = add(1, near[1], "forward_near", partner=partner)
-    adjoint0, swap0, direct0, part0 = respond(0, 1, terms0, near1)
+    adjoint0, swap0, direct0, part0 = respond(0, 2, terms0, near1)
     swap0 = [lax.ppermute(v, "tile", across) for v in swap0]
     direct0 = lax.ppermute(direct0, "tile", inward)
-    swapped1 = lax.ppermute(after(early1, late1, adjoint0), "tile", across)
+    swapped1 = forwarded(2, early1, late1, adjoint0)
     total1 = add(1, near1, "forward_mid", early=early1, late=late1)
     increment1, sent1 = observe(1, total1, swapped1)
     through0 = add_through(adjoint0, swap0)
-    second0, kept0 = rest(1, adjoint0, through0, direct0, flops=HEAVY)
+    second0 = one(PARTNER, rows_half, "backward_second", adjoint0, direct0, flops=HEAVY)
     through0 = lax.ppermute(through0, "tile", outward)
-    second0 = [lax.ppermute(v, "tile", across) for v in second0]
     terms1 = member_terms(increment1, sent1, groups)
-    adjoint1, swap1, direct1, part1 = respond(1, 2, terms1, kept0)
+    adjoint1, swap1, direct1, part1 = respond(1, 2, terms1, second0)
     swap1 = [lax.ppermute(v, "tile", across) for v in swap1]
+    second0 = lax.ppermute(second0, "tile", across)
     direct1 = lax.ppermute(direct1, "tile", inward)
-    through1 = lax.ppermute(add_through(after(adjoint1, through0, direct0), swap1), "tile", outward)
-    second1, kept1 = rest(2, adjoint1, *swap1)
+    through1 = lax.ppermute(add_through(adjoint1, swap1), "tile", outward)
+    second1, kept1 = rest(2, adjoint1, *swap1, through0)
     second1 = [lax.ppermute(v, "tile", across) for v in second1]
-    gradient = finished(0, (), second0, kept0, direct0, through0)
-    gradient = finished(1, (gradient,), second1, kept1, direct1, through1)
+    kept0 = one(OWN, rows_full, "backward_kept", adjoint0, *second1)
+    found0 = settled(0, direct0)
+    found1 = settled(1, kept1, *second1)
+    gradient = finished(0, (), found0, kept0, second0, through0)
+    gradient = finished(1, (gradient,), found1, direct1, through1)
     return (jnp.concatenate((part0, part1), axis=1), gradient)
 
 

time: 72.4 us -> 74.1 us (1.023)
  Pallas kernels: 18.7 us -> 23.4 us
  waiting for transfers between devices: 21.3 us -> 20 us
  starting transfers between devices: 26.1 us -> 25 us
    pallas_call x12 -> x13, Pallas kernels: 16.6 us -> 21.4 us  [call(): pl.pallas_call(body, in_specs=[pl.BlockSpec(memory_space=pltpu.SMEM)] + [...]
    ppermute x1, waiting for transfers between devices: 0.28 us -> 4.79 us  [shards(): late0 = lax.ppermute(own[0], 'tile', outward)]
    ppermute x1, starting transfers between devices: 3.08 us -> 0.01 us  [shards(): late0 = lax.ppermute(own[0], 'tile', outward)]
    ppermute x1, starting transfers between devices: 2.09 us -> 5.1 us  [shards(): early0 = lax.ppermute(own[0], 'tile', inward)]
    ppermute x1, waiting for transfers between devices: 3.59 us -> 1.01 us  [shards(): early0 = lax.ppermute(own[0], 'tile', inward)]
    ppermute x4 -> x6, waiting for transfers between devices: 2.5 us -> 0.65 us  [the longest x1 0.63 us: shards(): through1 = lax.ppermute(add_through(adjoint1, swap1), 'tile', outward)]
    ppermute x4 -> x6, starting transfers between devices: 2.67 us -> 1.27 us  [the longest x4 1.14 us: forwarded(): lax.ppermute(early[k * size:(k + 1) * size], 'tile', across)]
    ppermute x1, starting transfers between devices: 2.32 us -> 3.68 us  [shards(): direct1 = lax.ppermute(direct1, 'tile', inward)]
  transfers between devices with their start and end apart: 23 -> 26, of which waited for: 13 -> 11; matrix products, arithmetic and copies ran while one was open for 3% -> 3% of each run, Pallas kernels for 25% -> 30%
where the time goes in v3:
time: 74.1 us; the launch traced here: 73.9 us
  starting transfers between devices  25 us (34%)
  Pallas kernels  23.4 us (32%)
  waiting for transfers between devices  20 us (27%)
  local copies, waits for them, and re-layouts  2.33 us (3%)
  between operations  2.25 us (3%)
  other arithmetic  0.96 us (1%)
    pallas_call x13, Pallas kernels, call(): pl.pallas_call(body, in_specs=[pl.BlockSpec(memory_space=pltpu.SMEM)] + [...  21.4 us
    ppermute x1, waiting for transfers between devices, shards(): direct1 = lax.ppermute(direct1, 'tile', inward)  7.66 us
    ppermute x6, starting transfers between devices, member_terms(): terms.append(lax.ppermute(sent, 'member', pairs))  7.11 us
    ppermute x1, starting transfers between devices, shards(): early0 = lax.ppermute(own[0], 'tile', inward)  5.1 us
    ppermute x6, waiting for transfers between devices, member_terms(): terms.append(lax.ppermute(sent, 'member', pairs))  5.09 us
    ppermute x1, waiting for transfers between devices, shards(): late0 = lax.ppermute(own[0], 'tile', outward)  4.79 us
    ppermute x1, starting transfers between devices, shards(): direct0 = lax.ppermute(direct0, 'tile', inward)  4.07 us
    ppermute x1, starting transfers between devices, shards(): direct1 = lax.ppermute(direct1, 'tile', inward)  3.68 us
  transfers between devices with their start and end apart: 26, of which 11 were waited for; matrix products, arithmetic and copies ran while one was open for 3% of the time, Pallas kernels for 30%

profile of v3, /device:TPU:0, one launch (start us, length us, event | category | flops | bytes accessed | tf_op | source)
XLA Modules:
  0.0 73.9 jit_solution(1859562723860252429)
XLA Ops:
  0.7 1.1 %slice.31 = bf16[10,16,1024]{2,1,0:T(8,128)(2,1)S(1)} slice(f32[10,32,1024]{2,1,0:T(8,128)} %coeffs.3), slice={[0:10], [0:16], [0:1024]} | slice | bytes 655360 | tf_op jit(solution)/shard_map/slice | solution.py:268
  1.8 5.1 %collective-permute-start.1 = (bf16[160,1024]{1,0:T(8,128)(2,1)S(1)}, bf16[160,1024]{1,0:T(8,128)(2,1)S(1)}, u32[]{:S(2)}, u32[]{:S(2)}) collective-permute-start(bf16[160,1024]{1,0:T(8,128)(2,1)S(1)} %bitcast.11), channel_id=1, source_target_pairs={{0,24},{4,12},{8,0},{12,20},{16,8},{20,28},{24,16},{28,4},{1,25},{... | collective-permute-start | bytes 983048 | tf_op jit(solution)/shard_map/ppermute | solution.py:360
  8.2 1.1 %slice.30 = bf16[10,16,1024]{2,1,0:T(8,128)(2,1)S(1)} slice(f32[10,32,1024]{2,1,0:T(8,128)} %coeffs.3), slice={[0:10], [16:32], [0:1024]} | slice | bytes 655360 | tf_op jit(solution)/shard_map/slice | solution.py:268
  9.7 6.0 %load.1 = (f32[160,1024]{1,0:T(8,128)S(1)}, f32[160,1024]{1,0:T(8,128)S(1)}, bf16[5,1024,1024]{2,1,0:T(8,128)(2,1)S(1)}, bf16[2,10,32,1024]{3,2,1,0:T(8,128)(2,1...) custom-call(s32[12]{0:T(128)S(1)} %pad_add_fusion.meta, ...), custom_call_target="tpu_custom_call" | custom-call | tf_op jit(solution)/shard_map/load/pallas_call | solution.py:47
  16.8 4.8 %collective-permute-done.2.refs_2_ = bf16[160,1024]{1,0:T(8,128)(2,1)S(1)} collective-permute-done((bf16[160,1024]{1,0:T(8,128)(2,1)S(1)}, bf16[160,1024]{1,0:T(8,128)(2,1)S(1)}, u32[]{:S(2)}, u32[]{:S(2)}) %collective-permute-start.2) | collective-permute-done | bytes 327712 | tf_op jit(solution)/shard_map/ppermute | solution.py:361
  21.6 1.7 %collective-permute-start.8 = (bf16[160,1024]{1,0:T(8,128)(2,1)S(1)}, bf16[160,1024]{1,0:T(8,128)(2,1)S(1)}, u32[]{:S(2)}, u32[]{:S(2)}) collective-permute-start(bf16[160,1024]{1,0:T(8,128)(2,1)S(1)} %bitcast.9), channel_id=1, source_target_pairs={{0,24},{4,12},{8,0},{12,20},{16,8},{20,28},{24,16},{28,4},{1,25},{... | collective-permute-start | bytes 983048 | tf_op jit(solution)/shard_map/ppermute | solution.py:364
  24.3 1.6 %forward_mid.2.before = f32[160,1024]{1,0:T(8,128)S(1)} custom-call(s32[12]{0:T(128)S(1)} %pad_add_fusion.meta, bf16[5,1024,1024]{2,1,0:T(8,128)(2,1)S(1)} %get-tuple-element.42.held, f32[160,1024]{1,0:T(8,128)S(1)} %get-tuple-element.43.before, bf16[320,1024]{1,0:T(8,128)(2,1)S(1)} %collective-permute-done.refs_0_, ...), custom_call_target="tpu_custom_call" | custom-call | tf_op jit(solution)/shard_map/forward_mid/pallas_call | solution.py:47
  25.9 1.3 %forward_far.2 = (f32[2,16,1024]{2,1,0:T(8,128)S(1)}, bf16[2,16,1024]{2,1,0:T(8,128)(2,1)S(1)}) custom-call(s32[12]{0:T(128)S(1)} %pad_add_fusion.meta, bf16[5,1024,1024]{2,1,0:T(8,128)(2,1)S(1)} %get-tuple-element.42.held, bf16[2,10,32,1024]{3,2,1,0:T(8,128)(2,1)S(1)} %get-tuple-element.39.perturb, f32[160,1024]{1,0:T(8,128)S(1)} %forward_mid.2.before, ...), custom_call_target="tpu_custom_call" | custom-call | tf_op jit(solution)/shard_map/forward_far/pallas_call | solution.py:47
  27.2 1.6 %collective-permute-start.5 = (bf16[2,16,1024]{2,1,0:T(8,128)(2,1)S(1)}, bf16[2,16,1024]{2,1,0:T(8,128)(2,1)S(1)}, u32[]{:S(2)}, u32[]{:S(2)}) collective-permute-start(bf16[2,16,1024]{2,1,0:T(8,128)(2,1)S(1)} %get-tuple-element.50), channel_id=1, source_target_pairs={{0,1},{1,0},{2,3},{3,2},{4,5},{5,4},{6,7},{7,6},{8,9},{9,8},{10,11... | collective-permute-start | bytes 196616 | tf_op jit(solution)/shard_map/ppermute | solution.py:32
  28.8 1.5 %collective-permute-start.6 = (bf16[2,16,1024]{2,1,0:T(8,128)(2,1)S(1)}, bf16[2,16,1024]{2,1,0:T(8,128)(2,1)S(1)}, u32[]{:S(2)}, u32[]{:S(2)}) collective-permute-start(bf16[2,16,1024]{2,1,0:T(8,128)(2,1)S(1)} %get-tuple-element.50), channel_id=1, source_target_pairs={{0,2},{1,3},{2,0},{3,1},{4,6},{5,7},{6,4},{7,5},{8,10},{9,11},{10,... | collective-permute-start | bytes 196616 | tf_op jit(solution)/shard_map/ppermute | solution.py:32
  31.5 1.5 %collective-permute-done.6.refs_2_ = bf16[2,16,1024]{2,1,0:T(8,128)(2,1)S(1)} collective-permute-done((bf16[2,16,1024]{2,1,0:T(8,128)(2,1)S(1)}, bf16[2,16,1024]{2,1,0:T(8,128)(2,1)S(1)}, u32[]{:S(2)}, u32[]{:S(2)}) %collective-permute-start.6) | collective-permute-done | bytes 65568 | tf_op jit(solution)/shard_map/ppermute | solution.py:32
  33.1 2.4 %collective-permute-done.7.refs_3_ = bf16[2,16,1024]{2,1,0:T(8,128)(2,1)S(1)} collective-permute-done((bf16[2,16,1024]{2,1,0:T(8,128)(2,1)S(1)}, bf16[2,16,1024]{2,1,0:T(8,128)(2,1)S(1)}, u32[]{:S(2)}, u32[]{:S(2)}) %collective-permute-start.7) | collective-permute-done | bytes 65568 | tf_op jit(solution)/shard_map/ppermute | solution.py:32
  35.5 1.8 %backward_first.2 = (bf16[160,1024]{1,0:T(8,128)(2,1)S(1)}, bf16[80,1024]{1,0:T(8,128)(2,1)S(1)}, bf16[80,1024]{1,0:T(8,128)(2,1)S(1)}, bf16[160,1024]{1,0:T(8,128)(2,1)S(1)}, f32[2,16,256]{2,1,0:T(8,128)S(1)}) custom-call(s32[12]{0:T(128)S(1)} %pad_add_fusion.meta, bf16[3,1024,1024]{2,1,0:T(8,128)(2,1)S(1)} %get-tuple-element.38.turned, ...), custom_call_target="tpu_custom_call" | custom-call | tf_op jit(solution)/shard_map/backward_first/pallas_call | solution.py:47
  37.2 4.1 %collective-permute-start.12 = (bf16[160,1024]{1,0:T(8,128)(2,1)S(1)}, bf16[160,1024]{1,0:T(8,128)(2,1)S(1)}, u32[]{:S(2)}, u32[]{:S(2)}) collective-permute-start(bf16[160,1024]{1,0:T(8,128)(2,1)S(1)} %get-tuple-element.56), channel_id=1, source_target_pairs={{0,24},{4,12},{8,0},{12,20},{16,8},{20,28},{24,16},{28,4},{1,25},{... | collective-permute-start | bytes 983048 | tf_op jit(solution)/shard_map/ppermute | solution.py:372
  42.4 1.6 %forward_mid.3.before = f32[160,1024]{1,0:T(8,128)S(1)} custom-call(s32[12]{0:T(128)S(1)} %pad_add_fusion.meta, bf16[5,1024,1024]{2,1,0:T(8,128)(2,1)S(1)} %get-tuple-element.42.held, f32[160,1024]{1,0:T(8,128)S(1)} %forward_near.1.before, bf16[160,1024]{1,0:T(8,128)(2,1)S(1)} %collective-permute-done.8.refs_0_, ...), custom_call_target="tpu_custom_call" | custom-call | tf_op jit(solution)/shard_map/forward_mid/pallas_call | solution.py:47
  44.1 1.3 %forward_far.3 = (f32[2,16,1024]{2,1,0:T(8,128)S(1)}, bf16[2,16,1024]{2,1,0:T(8,128)(2,1)S(1)}) custom-call(s32[12]{0:T(128)S(1)} %pad_add_fusion.meta, bf16[5,1024,1024]{2,1,0:T(8,128)(2,1)S(1)} %get-tuple-element.42.held, bf16[2,10,32,1024]{3,2,1,0:T(8,128)(2,1)S(1)} %get-tuple-element.39.perturb, f32[160,1024]{1,0:T(8,128)S(1)} %forward_mid.3.before, ...), custom_call_target="tpu_custom_call" | custom-call | tf_op jit(solution)/shard_map/forward_far/pallas_call | solution.py:47
  46.4 2.5 %collective-permute-start.15 = (bf16[2,16,1024]{2,1,0:T(8,128)(2,1)S(1)}, bf16[2,16,1024]{2,1,0:T(8,128)(2,1)S(1)}, u32[]{:S(2)}, u32[]{:S(2)}) collective-permute-start(bf16[2,16,1024]{2,1,0:T(8,128)(2,1)S(1)} %get-tuple-element.59), channel_id=1, source_target_pairs={{0,3},{1,2},{2,1},{3,0},{4,7},{5,6},{6,5},{7,4},{8,11},{9,10},{10,... | collective-permute-start | bytes 196616 | tf_op jit(solution)/shard_map/ppermute | solution.py:32
  48.9 1.1 %backward_through.2 = bf16[160,1024]{1,0:T(8,128)(2,1)S(1)} custom-call(s32[12]{0:T(128)S(1)} %pad_add_fusion.meta, bf16[3,1024,1024]{2,1,0:T(8,128)(2,1)S(1)} %get-tuple-element.38.turned, bf16[160,1024]{1,0:T(8,128)(2,1)S(1)} %get-tuple-element.71.adjoint_in, bf16[80,1024]{1,0:T(8,128)(2,1)S(1)} %collective-permute-done.18.refs_0_, ...), custom_call_target="tpu_custom_call" | custom-call | tf_op jit(solution)/shard_map/backward_through/pallas_call | solution.py:47
  51.6 1.8 %backward_first.3 = (bf16[160,1024]{1,0:T(8,128)(2,1)S(1)}, bf16[80,1024]{1,0:T(8,128)(2,1)S(1)}, bf16[80,1024]{1,0:T(8,128)(2,1)S(1)}, bf16[160,1024]{1,0:T(8,128)(2,1)S(1)}, f32[2,16,256]{2,1,0:T(8,128)S(1)}) custom-call(s32[12]{0:T(128)S(1)} %pad_add_fusion.meta, bf16[3,1024,1024]{2,1,0:T(8,128)(2,1)S(1)} %get-tuple-element.38.turned, ...), custom_call_target="tpu_custom_call" | custom-call | tf_op jit(solution)/shard_map/backward_first/pallas_call | solution.py:47
  54.0 3.7 %collective-permute-start.23 = (bf16[160,1024]{1,0:T(8,128)(2,1)S(1)}, bf16[160,1024]{1,0:T(8,128)(2,1)S(1)}, u32[]{:S(2)}, u32[]{:S(2)}) collective-permute-start(bf16[160,1024]{1,0:T(8,128)(2,1)S(1)} %get-tuple-element.70), channel_id=1, source_target_pairs={{0,24},{4,12},{8,0},{12,20},{16,8},{20,28},{24,16},{28,4},{1,25},{... | collective-permute-start | bytes 983048 | tf_op jit(solution)/shard_map/ppermute | solution.py:383
  57.7 1.1 %backward_through.3 = bf16[160,1024]{1,0:T(8,128)(2,1)S(1)} custom-call(s32[12]{0:T(128)S(1)} %pad_add_fusion.meta, bf16[3,1024,1024]{2,1,0:T(8,128)(2,1)S(1)} %get-tuple-element.38.turned, bf16[160,1024]{1,0:T(8,128)(2,1)S(1)} %get-tuple-element.66.adjoint_in, bf16[80,1024]{1,0:T(8,128)(2,1)S(1)} %collective-permute-done.16.refs_0_, ...), custom_call_target="tpu_custom_call" | custom-call | tf_op jit(solution)/shard_map/backward_through/pallas_call | solution.py:47
  59.1 1.4 %backward_rest.1 = (bf16[80,1024]{1,0:T(8,128)(2,1)S(1)}, bf16[80,1024]{1,0:T(8,128)(2,1)S(1)}, f32[160,1024]{1,0:T(8,128)S(1)}) custom-call(s32[12]{0:T(128)S(1)} %pad_add_fusion.meta, bf16[5,1024,1024]{2,1,0:T(8,128)(2,1)S(1)} %get-tuple-element.42.held, bf16[160,1024]{1,0:T(8,128)(2,1)S(1)} %get-tuple-element.66.adjoint_in), custom_call_target="tpu_custom_call" | custom-call | tf_op jit(solution)/shard_map/backward_rest/pallas_call | solution.py:47
  62.3 1.4 %backward_kept.1.refs_1_ = f32[160,1024]{1,0:T(8,128)S(1)} custom-call(s32[12]{0:T(128)S(1)} %pad_add_fusion.meta, bf16[5,1024,1024]{2,1,0:T(8,128)(2,1)S(1)} %get-tuple-element.42.held, bf16[160,1024]{1,0:T(8,128)(2,1)S(1)} %get-tuple-element.71.adjoint_in), custom_call_target="tpu_custom_call" | custom-call | tf_op jit(solution)/shard_map/backward_kept/pallas_call | solution.py:47
  64.7 7.7 %collective-permute-done.23.refs_1_ = bf16[160,1024]{1,0:T(8,128)(2,1)S(1)} collective-permute-done((bf16[160,1024]{1,0:T(8,128)(2,1)S(1)}, bf16[160,1024]{1,0:T(8,128)(2,1)S(1)}, u32[]{:S(2)}, u32[]{:S(2)}) %collective-permute-start.23) | collective-permute-done | bytes 327712 | tf_op jit(solution)/shard_map/ppermute | solution.py:383
  (61 shorter events, 12.6 us)
Async XLA Ops:
  1.8 15.0 %collective-permute-start.1 = (bf16[160,1024]{1,0:T(8,128)(2,1)S(1)}, bf16[160,1024]{1,0:T(8,128)(2,1)S(1)}, u32[]{:S(2)}, u32[]{:S(2)}) collective-permute-start(bf16[160,1024]{1,0:T(8,128)(2,1)S(1)} %bitcast.11), channel_id=1, source_target_pairs={{0,24},{4,12},{8,0},{12,20},{16,8},{20,28},{24,16},{28,4},{1,25},{... | collective-permute-start | bytes 983048 | tf_op jit(solution)/shard_map/ppermute | solution.py:360
  6.9 14.7 %collective-permute-start.2 = (bf16[160,1024]{1,0:T(8,128)(2,1)S(1)}, bf16[160,1024]{1,0:T(8,128)(2,1)S(1)}, u32[]{:S(2)}, u32[]{:S(2)}) collective-permute-start(bf16[160,1024]{1,0:T(8,128)(2,1)S(1)} %bitcast.12), channel_id=1, source_target_pairs={{0,8},{4,28},{8,16},{12,4},{16,24},{20,12},{24,0},{28,20},{1,9},{5... | collective-permute-start | bytes 983048 | tf_op jit(solution)/shard_map/ppermute | solution.py:361
  15.7 8.5 %collective-permute-start = (bf16[320,1024]{1,0:T(8,128)(2,1)S(1)}, bf16[320,1024]{1,0:T(8,128)(2,1)S(1)}, u32[]{:S(2)}, u32[]{:S(2)}) collective-permute-start(bf16[320,1024]{1,0:T(8,128)(2,1)S(1)} %pad_maximum_fusion), channel_id=1, source_target_pairs={{0,4},{4,0},{8,12},{12,8},{16,20},{20,16},{24,28},{28,24},{1,5},{5... | collective-permute-start | bytes 1966088 | tf_op jit(solution)/shard_map/ppermute | solution.py:362
  21.6 19.7 %collective-permute-start.8 = (bf16[160,1024]{1,0:T(8,128)(2,1)S(1)}, bf16[160,1024]{1,0:T(8,128)(2,1)S(1)}, u32[]{:S(2)}, u32[]{:S(2)}) collective-permute-start(bf16[160,1024]{1,0:T(8,128)(2,1)S(1)} %bitcast.9), channel_id=1, source_target_pairs={{0,24},{4,12},{8,0},{12,20},{16,8},{20,28},{24,16},{28,4},{1,25},{... | collective-permute-start | bytes 983048 | tf_op jit(solution)/shard_map/ppermute | solution.py:364
  23.4 17.9 %collective-permute-start.9 = (bf16[160,1024]{1,0:T(8,128)(2,1)S(1)}, bf16[160,1024]{1,0:T(8,128)(2,1)S(1)}, u32[]{:S(2)}, u32[]{:S(2)}) collective-permute-start(bf16[160,1024]{1,0:T(8,128)(2,1)S(1)} %bitcast.10), channel_id=1, source_target_pairs={{0,8},{4,28},{8,16},{12,4},{16,24},{20,12},{24,0},{28,20},{1,9},{5... | collective-permute-start | bytes 983048 | tf_op jit(solution)/shard_map/ppermute | solution.py:365
  23.7 2.2 %collective-permute-start.3 = (bf16[80,1024]{1,0:T(8,128)(2,1)S(1)}, bf16[80,1024]{1,0:T(8,128)(2,1)S(1)}, u32[]{:S(2)}, u32[]{:S(2)}) collective-permute-start(bf16[80,1024]{1,0:T(8,128)(2,1)S(1)} %get-tuple-element.75), channel_id=1, source_target_pairs={{0,4},{4,0},{8,12},{12,8},{16,20},{20,16},{24,28},{28,24},{1,5},{5... | collective-permute-start | bytes 491528 | tf_op jit(solution)/shard_map/ppermute | solution.py:294
  23.8 2.2 %collective-permute-start.4 = (bf16[80,1024]{1,0:T(8,128)(2,1)S(1)}, bf16[80,1024]{1,0:T(8,128)(2,1)S(1)}, u32[]{:S(2)}, u32[]{:S(2)}) collective-permute-start(bf16[80,1024]{1,0:T(8,128)(2,1)S(1)} %get-tuple-element.74), channel_id=1, source_target_pairs={{0,4},{4,0},{8,12},{12,8},{16,20},{20,16},{24,28},{28,24},{1,5},{5... | collective-permute-start | bytes 491528 | tf_op jit(solution)/shard_map/ppermute | solution.py:294
  27.2 4.3 %collective-permute-start.5 = (bf16[2,16,1024]{2,1,0:T(8,128)(2,1)S(1)}, bf16[2,16,1024]{2,1,0:T(8,128)(2,1)S(1)}, u32[]{:S(2)}, u32[]{:S(2)}) collective-permute-start(bf16[2,16,1024]{2,1,0:T(8,128)(2,1)S(1)} %get-tuple-element.50), channel_id=1, source_target_pairs={{0,1},{1,0},{2,3},{3,2},{4,5},{5,4},{6,7},{7,6},{8,9},{9,8},{10,11... | collective-permute-start | bytes 196616 | tf_op jit(solution)/shard_map/ppermute | solution.py:32
  28.8 4.3 %collective-permute-start.6 = (bf16[2,16,1024]{2,1,0:T(8,128)(2,1)S(1)}, bf16[2,16,1024]{2,1,0:T(8,128)(2,1)S(1)}, u32[]{:S(2)}, u32[]{:S(2)}) collective-permute-start(bf16[2,16,1024]{2,1,0:T(8,128)(2,1)S(1)} %get-tuple-element.50), channel_id=1, source_target_pairs={{0,2},{1,3},{2,0},{3,1},{4,6},{5,7},{6,4},{7,5},{8,10},{9,11},{10,... | collective-permute-start | bytes 196616 | tf_op jit(solution)/shard_map/ppermute | solution.py:32
  30.3 5.2 %collective-permute-start.7 = (bf16[2,16,1024]{2,1,0:T(8,128)(2,1)S(1)}, bf16[2,16,1024]{2,1,0:T(8,128)(2,1)S(1)}, u32[]{:S(2)}, u32[]{:S(2)}) collective-permute-start(bf16[2,16,1024]{2,1,0:T(8,128)(2,1)S(1)} %get-tuple-element.50), channel_id=1, source_target_pairs={{0,3},{1,2},{2,1},{3,0},{4,7},{5,6},{6,5},{7,4},{8,11},{9,10},{10,... | collective-permute-start | bytes 196616 | tf_op jit(solution)/shard_map/ppermute | solution.py:32
  37.2 12.8 %collective-permute-start.12 = (bf16[160,1024]{1,0:T(8,128)(2,1)S(1)}, bf16[160,1024]{1,0:T(8,128)(2,1)S(1)}, u32[]{:S(2)}, u32[]{:S(2)}) collective-permute-start(bf16[160,1024]{1,0:T(8,128)(2,1)S(1)} %get-tuple-element.56), channel_id=1, source_target_pairs={{0,24},{4,12},{8,0},{12,20},{16,8},{20,28},{24,16},{28,4},{1,25},{... | collective-permute-start | bytes 983048 | tf_op jit(solution)/shard_map/ppermute | solution.py:372
  41.3 2.7 %collective-permute-start.10 = (bf16[80,1024]{1,0:T(8,128)(2,1)S(1)}, bf16[80,1024]{1,0:T(8,128)(2,1)S(1)}, u32[]{:S(2)}, u32[]{:S(2)}) collective-permute-start(bf16[80,1024]{1,0:T(8,128)(2,1)S(1)} %get-tuple-element.73), channel_id=1, source_target_pairs={{0,4},{4,0},{8,12},{12,8},{16,20},{20,16},{24,28},{28,24},{1,5},{5... | collective-permute-start | bytes 491528 | tf_op jit(solution)/shard_map/ppermute | solution.py:294
  41.4 2.6 %collective-permute-start.11 = (bf16[80,1024]{1,0:T(8,128)(2,1)S(1)}, bf16[80,1024]{1,0:T(8,128)(2,1)S(1)}, u32[]{:S(2)}, u32[]{:S(2)}) collective-permute-start(bf16[80,1024]{1,0:T(8,128)(2,1)S(1)} %get-tuple-element.72), channel_id=1, source_target_pairs={{0,4},{4,0},{8,12},{12,8},{16,20},{20,16},{24,28},{28,24},{1,5},{5... | collective-permute-start | bytes 491528 | tf_op jit(solution)/shard_map/ppermute | solution.py:294
  41.9 4.5 %collective-permute-start.18 = (bf16[80,1024]{1,0:T(8,128)(2,1)S(1)}, bf16[80,1024]{1,0:T(8,128)(2,1)S(1)}, u32[]{:S(2)}, u32[]{:S(2)}) collective-permute-start(bf16[80,1024]{1,0:T(8,128)(2,1)S(1)} %get-tuple-element.64), channel_id=1, source_target_pairs={{0,4},{4,0},{8,12},{12,8},{16,20},{20,16},{24,28},{28,24},{1,5},{5... | collective-permute-start | bytes 491528 | tf_op jit(solution)/shard_map/ppermute | solution.py:371
  42.0 6.9 %collective-permute-start.19 = (bf16[80,1024]{1,0:T(8,128)(2,1)S(1)}, bf16[80,1024]{1,0:T(8,128)(2,1)S(1)}, u32[]{:S(2)}, u32[]{:S(2)}) collective-permute-start(bf16[80,1024]{1,0:T(8,128)(2,1)S(1)} %get-tuple-element.65), channel_id=1, source_target_pairs={{0,4},{4,0},{8,12},{12,8},{16,20},{20,16},{24,28},{28,24},{1,5},{5... | collective-permute-start | bytes 491528 | tf_op jit(solution)/shard_map/ppermute | solution.py:371
  45.3 5.3 %collective-permute-start.13 = (bf16[2,16,1024]{2,1,0:T(8,128)(2,1)S(1)}, bf16[2,16,1024]{2,1,0:T(8,128)(2,1)S(1)}, u32[]{:S(2)}, u32[]{:S(2)}) collective-permute-start(bf16[2,16,1024]{2,1,0:T(8,128)(2,1)S(1)} %get-tuple-element.59), channel_id=1, source_target_pairs={{0,1},{1,0},{2,3},{3,2},{4,5},{5,4},{6,7},{7,6},{8,9},{9,8},{10,11... | collective-permute-start | bytes 196616 | tf_op jit(solution)/shard_map/ppermute | solution.py:32
  45.9 4.7 %collective-permute-start.14 = (bf16[2,16,1024]{2,1,0:T(8,128)(2,1)S(1)}, bf16[2,16,1024]{2,1,0:T(8,128)(2,1)S(1)}, u32[]{:S(2)}, u32[]{:S(2)}) collective-permute-start(bf16[2,16,1024]{2,1,0:T(8,128)(2,1)S(1)} %get-tuple-element.59), channel_id=1, source_target_pairs={{0,2},{1,3},{2,0},{3,1},{4,6},{5,7},{6,4},{7,5},{8,10},{9,11},{10,... | collective-permute-start | bytes 196616 | tf_op jit(solution)/shard_map/ppermute | solution.py:32
  46.4 5.2 %collective-permute-start.15 = (bf16[2,16,1024]{2,1,0:T(8,128)(2,1)S(1)}, bf16[2,16,1024]{2,1,0:T(8,128)(2,1)S(1)}, u32[]{:S(2)}, u32[]{:S(2)}) collective-permute-start(bf16[2,16,1024]{2,1,0:T(8,128)(2,1)S(1)} %get-tuple-element.59), channel_id=1, source_target_pairs={{0,3},{1,2},{2,1},{3,0},{4,7},{5,6},{6,5},{7,4},{8,11},{9,10},{10,... | collective-permute-start | bytes 196616 | tf_op jit(solution)/shard_map/ppermute | solution.py:32
  50.0 9.1 %collective-permute-start.20 = (bf16[160,1024]{1,0:T(8,128)(2,1)S(1)}, bf16[160,1024]{1,0:T(8,128)(2,1)S(1)}, u32[]{:S(2)}, u32[]{:S(2)}) collective-permute-start(bf16[160,1024]{1,0:T(8,128)(2,1)S(1)} %backward_through.2), channel_id=1, source_target_pairs={{0,8},{4,28},{8,16},{12,4},{16,24},{20,12},{24,0},{28,20},{1,9},{5... | collective-permute-start | bytes 983048 | tf_op jit(solution)/shard_map/ppermute | solution.py:378
  53.4 4.3 %collective-permute-start.16 = (bf16[80,1024]{1,0:T(8,128)(2,1)S(1)}, bf16[80,1024]{1,0:T(8,128)(2,1)S(1)}, u32[]{:S(2)}, u32[]{:S(2)}) collective-permute-start(bf16[80,1024]{1,0:T(8,128)(2,1)S(1)} %get-tuple-element.62), channel_id=1, source_target_pairs={{0,4},{4,0},{8,12},{12,8},{16,20},{20,16},{24,28},{28,24},{1,5},{5... | collective-permute-start | bytes 491528 | tf_op jit(solution)/shard_map/ppermute | solution.py:381
  53.4 4.3 %collective-permute-start.17 = (bf16[80,1024]{1,0:T(8,128)(2,1)S(1)}, bf16[80,1024]{1,0:T(8,128)(2,1)S(1)}, u32[]{:S(2)}, u32[]{:S(2)}) collective-permute-start(bf16[80,1024]{1,0:T(8,128)(2,1)S(1)} %get-tuple-element.63), channel_id=1, source_target_pairs={{0,4},{4,0},{8,12},{12,8},{16,20},{20,16},{24,28},{28,24},{1,5},{5... | collective-permute-start | bytes 491528 | tf_op jit(solution)/shard_map/ppermute | solution.py:381
  53.9 9.9 %collective-permute-start.25 = (bf16[160,1024]{1,0:T(8,128)(2,1)S(1)}, bf16[160,1024]{1,0:T(8,128)(2,1)S(1)}, u32[]{:S(2)}, u32[]{:S(2)}) collective-permute-start(bf16[160,1024]{1,0:T(8,128)(2,1)S(1)} %backward_second.1), channel_id=1, source_target_pairs={{0,4},{4,0},{8,12},{12,8},{16,20},{20,16},{24,28},{28,24},{1,5},{5... | collective-permute-start | bytes 983048 | tf_op jit(solution)/shard_map/ppermute | solution.py:382
  54.0 18.4 %collective-permute-start.23 = (bf16[160,1024]{1,0:T(8,128)(2,1)S(1)}, bf16[160,1024]{1,0:T(8,128)(2,1)S(1)}, u32[]{:S(2)}, u32[]{:S(2)}) collective-permute-start(bf16[160,1024]{1,0:T(8,128)(2,1)S(1)} %get-tuple-element.70), channel_id=1, source_target_pairs={{0,24},{4,12},{8,0},{12,20},{16,8},{20,28},{24,16},{28,4},{1,25},{... | collective-permute-start | bytes 983048 | tf_op jit(solution)/shard_map/ppermute | solution.py:383
  58.8 14.2 %collective-permute-start.24 = (bf16[160,1024]{1,0:T(8,128)(2,1)S(1)}, bf16[160,1024]{1,0:T(8,128)(2,1)S(1)}, u32[]{:S(2)}, u32[]{:S(2)}) collective-permute-start(bf16[160,1024]{1,0:T(8,128)(2,1)S(1)} %backward_through.3), channel_id=1, source_target_pairs={{0,8},{4,28},{8,16},{12,4},{16,24},{20,12},{24,0},{28,20},{1,9},{5... | collective-permute-start | bytes 983048 | tf_op jit(solution)/shard_map/ppermute | solution.py:384
  (5 other events, 22.6 us)

commit v4 on v3

--- a/solution.py
+++ b/solution.py
@@ -10,13 +10,13 @@
 HEAVY = 100 * 10**9
 VMEM_LIMIT = 20 * 1024 * 1024
 OWN, PARTNER, EARLY, SWAPPED, LATE = range(5)
-PLACES = {"partner": PARTNER, "early": EARLY, "late": LATE}
+PLACES = {"partner": PARTNER, "below": (12,), "above": (13,)}
 ORDER = (0, 1, 2, -1, -2)
 TURNED = (SWAPPED, LATE, EARLY)
 
 
 def shift_pairs(count, step):
-    return [(source, (source + step(source % 2)) % count) for source in range(count)]
+    return [(tile, (tile + step(tile % 2, tile // 2)) % count) for tile in range(count)]
 
 
 def member_terms(value, sent, groups):
@@ -111,6 +111,7 @@
     out[...] = before[...]
     count = out.shape[0]
     for place, rows in zip(places, refs):
+        place = meta[place[0]] if isinstance(place, tuple) else place
         if rows.shape[0] > count:
             rows = rows.at[chunk * count:(chunk + 1) * count]
         add_times(meta, held, place, rows, out)
@@ -254,13 +255,17 @@
     offset = jnp.where(offset > radius, offset - tile_count, offset) * side
     match = offset[None, :] == jnp.array(ORDER, jnp.int32)[:, None]
     slot = jnp.sum(jnp.where(match, jnp.arange(slots)[None, :], 0), axis=1)
+    places = jnp.where((tile_index // 2) % 2 == 0, jnp.array([LATE, EARLY]), jnp.array([EARLY, LATE]))
     meta = jnp.concatenate(
-        [(slot < live[0]).astype(slot.dtype), slot, obs_count, group_index[None]]
+        [(slot < live[0]).astype(slot.dtype), slot, obs_count, group_index[None], places]
     ).astype(jnp.int32)
 
-    inward = shift_pairs(tile_count, lambda core: -2 if core == 0 else 2)
-    outward = shift_pairs(tile_count, lambda core: 2 if core == 0 else -2)
-    across = shift_pairs(tile_count, lambda core: 1 if core == 0 else -1)
+    inward = shift_pairs(tile_count, lambda core, chip: -2 if core == 0 else 2)
+    outward = shift_pairs(tile_count, lambda core, chip: 2 if core == 0 else -2)
+    below = shift_pairs(tile_count, lambda core, chip: -2 if (core + chip) % 2 == 0 else 2)
+    above = shift_pairs(tile_count, lambda core, chip: 2 if (core + chip) % 2 == 0 else -2)
+    even = (tile_index // 2) % 2 == 0
+    across = shift_pairs(tile_count, lambda core, chip: 1 if core == 0 else -1)
 
     own = []
     for c in range(CHUNKS):
@@ -289,9 +294,11 @@
         )
         return total
 
-    def forwarded(pieces, early, *others):
-        early, size = after(early, *others), rows // pieces
-        return [lax.ppermute(early[k * size:(k + 1) * size], "tile", across) for k in range(pieces)]
+    def forwarded(pieces, below, above, other):
+        below, above, _ = lax.optimization_barrier((below, above, other))
+        size = rows // pieces
+        cuts = [slice(k * size, (k + 1) * size) for k in range(pieces)]
+        return [lax.ppermute(jnp.where(even, above[at], below[at]), "tile", across) for at in cuts]
 
     def observe(c, total, swapped):
         return call(
@@ -312,8 +319,10 @@
         )
         return adjoint_in, swap, direct, increment
 
-    def add_through(adjoint_in, swap):
-        [through] = call(backward_through, meta, (turned, adjoint_in, *swap), [rows_half], "backward_through")
+    def add_through(adjoint_in, swap, flops=0):
+        [through] = call(
+            backward_through, meta, (turned, adjoint_in, *swap), [rows_half], "backward_through", flops=flops
+        )
         return through
 
     def rest(pieces, adjoint_in, *others):
@@ -323,10 +332,9 @@
         )
         return second, kept
 
-    def one(place, out, name, adjoint_in, *others, flops=0):
+    def one(place, out, name, adjoint_in, *others):
         [value] = call(
-            functools.partial(backward_one, place), meta, (held, after(adjoint_in, *others)), [out], name,
-            flops=flops,
+            functools.partial(backward_one, place), meta, (held, after(adjoint_in, *others)), [out], name
         )
         return value
 
@@ -357,28 +365,28 @@
             name="finish",
         )(*terms, *gradient)
 
-    early0 = lax.ppermute(own[0], "tile", inward)
-    late0 = lax.ppermute(own[0], "tile", outward)
+    below0 = lax.ppermute(own[0], "tile", below)
+    above0 = lax.ppermute(own[0], "tile", above)
     partner = lax.ppermute(jnp.concatenate(after(own, near[0])), "tile", across)
-    swapped0 = forwarded(2, early0, late0, near[0])
-    early1 = lax.ppermute(after(own[1], early0, late0), "tile", inward)
-    late1 = lax.ppermute(after(own[1], early0, late0), "tile", outward)
-    total0 = add(0, near[0], "forward_mid", partner=partner, early=early0, late=late0)
+    swapped0 = forwarded(2, below0, above0, near[0])
+    below1 = lax.ppermute(after(own[1], below0, above0), "tile", below)
+    above1 = lax.ppermute(after(own[1], below0, above0), "tile", above)
+    total0 = add(0, near[0], "forward_mid", partner=partner, below=below0, above=above0)
     increment0, sent0 = observe(0, total0, swapped0)
     terms0 = member_terms(increment0, sent0, groups)
     near1 = add(1, near[1], "forward_near", partner=partner)
-    adjoint0, swap0, direct0, part0 = respond(0, 2, terms0, near1)
+    adjoint0, swap0, direct0, part0 = respond(0, 1, terms0, near1)
     swap0 = [lax.ppermute(v, "tile", across) for v in swap0]
     direct0 = lax.ppermute(direct0, "tile", inward)
-    swapped1 = forwarded(2, early1, late1, adjoint0)
-    total1 = add(1, near1, "forward_mid", early=early1, late=late1)
+    swapped1 = forwarded(2, below1, above1, adjoint0)
+    total1 = add(1, near1, "forward_mid", below=below1, above=above1)
     increment1, sent1 = observe(1, total1, swapped1)
-    through0 = add_through(adjoint0, swap0)
-    second0 = one(PARTNER, rows_half, "backward_second", adjoint0, direct0, flops=HEAVY)
+    through0 = add_through(after(adjoint0, direct0), swap0, flops=HEAVY)
+    terms1 = member_terms(increment1, sent1, groups)
+    adjoint1, swap1, direct1, part1 = respond(1, 2, terms1, through0)
     through0 = lax.ppermute(through0, "tile", outward)
-    terms1 = member_terms(increment1, sent1, groups)
-    adjoint1, swap1, direct1, part1 = respond(1, 2, terms1, second0)
     swap1 = [lax.ppermute(v, "tile", across) for v in swap1]
+    second0 = one(PARTNER, rows_half, "backward_second", adjoint0, *swap1)
     second0 = lax.ppermute(second0, "tile", across)
     direct1 = lax.ppermute(direct1, "tile", inward)
     through1 = lax.ppermute(add_through(adjoint1, swap1), "tile", outward)

time: 74.1 us -> 73.1 us (0.987)
  waiting for transfers between devices: 20 us -> 18.4 us
    ppermute x8, starting transfers between devices: 8.27 us -> 11.3 us  [the longest x1 5.11 us: shards(): below0 = lax.ppermute(own[0], 'tile', below)]
    ppermute x1, waiting for transfers between devices: 7.66 us -> 4.76 us  [shards(): direct1 = lax.ppermute(direct1, 'tile', inward)]
    ppermute x1, starting transfers between devices: 4.07 us -> 1.69 us  [shards(): direct0 = lax.ppermute(direct0, 'tile', inward)]
    ppermute x8, waiting for transfers between devices: 5.82 us -> 3.99 us  [the longest x1 3.38 us: shards(): above0 = lax.ppermute(own[0], 'tile', above)]
    ppermute x1, waiting for transfers between devices: 0.01 us -> 1.71 us  [shards(): direct0 = lax.ppermute(direct0, 'tile', inward)]
    ppermute x1, starting transfers between devices: 3.68 us -> 1.98 us  [shards(): direct1 = lax.ppermute(direct1, 'tile', inward)]
    ppermute x1, starting transfers between devices: 0.06 us -> 1.25 us  [shards(): through1 = lax.ppermute(add_through(adjoint1, swap1), 'tile', outward)]
    ppermute x1, waiting for transfers between devices: 0.63 us -> 1.65 us  [shards(): through1 = lax.ppermute(add_through(adjoint1, swap1), 'tile', outward)]
  transfers between devices with their start and end apart: 26 -> 25, of which waited for: 11 -> 12; matrix products, arithmetic and copies ran while one was open for 3% -> 3% of each run, Pallas kernels for 30% -> 31%
where the time goes in v4:
time: 73.1 us; the launch traced here: 72.8 us
  starting transfers between devices  25.5 us (35%)
  Pallas kernels  23.4 us (32%)
  waiting for transfers between devices  18.4 us (25%)
  local copies, waits for them, and re-layouts  2.4 us (3%)
  between operations  2.24 us (3%)
  other arithmetic  0.96 us (1%)
    pallas_call x13, Pallas kernels, call(): pl.pallas_call(body, in_specs=[pl.BlockSpec(memory_space=pltpu.SMEM)] + [...  21.4 us
    ppermute x6, starting transfers between devices, member_terms(): terms.append(lax.ppermute(sent, 'member', pairs))  7.11 us
    ppermute x1, starting transfers between devices, shards(): below0 = lax.ppermute(own[0], 'tile', below)  5.11 us
    ppermute x1, waiting for transfers between devices, shards(): direct1 = lax.ppermute(direct1, 'tile', inward)  4.76 us
    ppermute x6, waiting for transfers between devices, member_terms(): terms.append(lax.ppermute(sent, 'member', pairs))  4.65 us
    ppermute x1, starting transfers between devices, shards(): below1 = lax.ppermute(after(own[1], below0, above0), 'tile', below)  4.46 us
    ppermute x1, waiting for transfers between devices, shards(): above0 = lax.ppermute(own[0], 'tile', above)  3.38 us
    slice x2, local copies, waits for them, and re-layouts, shards(): source[:, c * part:(c + 1) * part].astype(half).reshape(rows, cells)  2.28 us
  transfers between devices with their start and end apart: 25, of which 12 were waited for; matrix products, arithmetic and copies ran while one was open for 3% of the time, Pallas kernels for 31%

profile of v4, /device:TPU:0, one launch (start us, length us, event | category | flops | bytes accessed | tf_op | source)
XLA Modules:
  0.0 72.8 jit_solution(14433345156887608756)
XLA Ops:
  1.8 5.1 %collective-permute-start.1 = (bf16[160,1024]{1,0:T(8,128)(2,1)S(1)}, bf16[160,1024]{1,0:T(8,128)(2,1)S(1)}, u32[]{:S(2)}, u32[]{:S(2)}) collective-permute-start(bf16[160,1024]{1,0:T(8,128)(2,1)S(1)} %bitcast.11), channel_id=1, source_target_pairs={{0,24},{4,12},{8,16},{12,4},{16,8},{20,28},{24,0},{28,20},{1,25},{... | collective-permute-start | bytes 983048 | tf_op jit(solution)/shard_map/ppermute | solution.py:368
  9.7 5.4 %load.1 = (f32[160,1024]{1,0:T(8,128)S(1)}, f32[160,1024]{1,0:T(8,128)S(1)}, bf16[5,1024,1024]{2,1,0:T(8,128)(2,1)S(1)}, bf16[2,10,32,1024]{3,2,1,0:T(8,128)(2,1...) custom-call(s32[14]{0:T(128)S(1)} %concatenate.9.meta, ...), custom_call_target="tpu_custom_call" | custom-call | tf_op jit(solution)/shard_map/load/pallas_call | solution.py:47
  15.6 3.4 %collective-permute-done.2.refs_2_ = bf16[160,1024]{1,0:T(8,128)(2,1)S(1)} collective-permute-done((bf16[160,1024]{1,0:T(8,128)(2,1)S(1)}, bf16[160,1024]{1,0:T(8,128)(2,1)S(1)}, u32[]{:S(2)}, u32[]{:S(2)}) %collective-permute-start.2) | collective-permute-done | bytes 327712 | tf_op jit(solution)/shard_map/ppermute | solution.py:369
  19.0 4.5 %collective-permute-start.8 = (bf16[160,1024]{1,0:T(8,128)(2,1)S(1)}, bf16[160,1024]{1,0:T(8,128)(2,1)S(1)}, u32[]{:S(2)}, u32[]{:S(2)}) collective-permute-start(bf16[160,1024]{1,0:T(8,128)(2,1)S(1)} %bitcast.9), channel_id=1, source_target_pairs={{0,24},{4,12},{8,16},{12,4},{16,8},{20,28},{24,0},{28,20},{1,25},{... | collective-permute-start | bytes 983048 | tf_op jit(solution)/shard_map/ppermute | solution.py:372
  24.6 1.6 %forward_mid.2.before = f32[160,1024]{1,0:T(8,128)S(1)} custom-call(s32[14]{0:T(128)S(1)} %concatenate.9.meta, bf16[5,1024,1024]{2,1,0:T(8,128)(2,1)S(1)} %get-tuple-element.44.held, f32[160,1024]{1,0:T(8,128)S(1)} %get-tuple-element.45.before, bf16[320,1024]{1,0:T(8,128)(2,1)S(1)} %collective-permute-done.refs_0_, ...), custom_call_target="tpu_custom_call" | custom-call | tf_op jit(solution)/shard_map/forward_mid/pallas_call | solution.py:47
  26.2 1.3 %forward_far.2 = (f32[2,16,1024]{2,1,0:T(8,128)S(1)}, bf16[2,16,1024]{2,1,0:T(8,128)(2,1)S(1)}) custom-call(s32[14]{0:T(128)S(1)} %concatenate.9.meta, bf16[5,1024,1024]{2,1,0:T(8,128)(2,1)S(1)} %get-tuple-element.44.held, bf16[2,10,32,1024]{3,2,1,0:T(8,128)(2,1)S(1)} %get-tuple-element.41.perturb, f32[160,1024]{1,0:T(8,128)S(1)} %forward_mid.2.before, ...), custom_call_target="tpu_custom_call" | custom-call | tf_op jit(solution)/shard_map/forward_far/pallas_call | solution.py:47
  27.5 1.6 %collective-permute-start.5 = (bf16[2,16,1024]{2,1,0:T(8,128)(2,1)S(1)}, bf16[2,16,1024]{2,1,0:T(8,128)(2,1)S(1)}, u32[]{:S(2)}, u32[]{:S(2)}) collective-permute-start(bf16[2,16,1024]{2,1,0:T(8,128)(2,1)S(1)} %get-tuple-element.53), channel_id=1, source_target_pairs={{0,1},{1,0},{2,3},{3,2},{4,5},{5,4},{6,7},{7,6},{8,9},{9,8},{10,11... | collective-permute-start | bytes 196616 | tf_op jit(solution)/shard_map/ppermute | solution.py:32
  29.1 1.5 %collective-permute-start.6 = (bf16[2,16,1024]{2,1,0:T(8,128)(2,1)S(1)}, bf16[2,16,1024]{2,1,0:T(8,128)(2,1)S(1)}, u32[]{:S(2)}, u32[]{:S(2)}) collective-permute-start(bf16[2,16,1024]{2,1,0:T(8,128)(2,1)S(1)} %get-tuple-element.53), channel_id=1, source_target_pairs={{0,2},{1,3},{2,0},{3,1},{4,6},{5,7},{6,4},{7,5},{8,10},{9,11},{10,... | collective-permute-start | bytes 196616 | tf_op jit(solution)/shard_map/ppermute | solution.py:32
  32.2 1.8 %collective-permute-done.6.refs_2_ = bf16[2,16,1024]{2,1,0:T(8,128)(2,1)S(1)} collective-permute-done((bf16[2,16,1024]{2,1,0:T(8,128)(2,1)S(1)}, bf16[2,16,1024]{2,1,0:T(8,128)(2,1)S(1)}, u32[]{:S(2)}, u32[]{:S(2)}) %collective-permute-start.6) | collective-permute-done | bytes 65568 | tf_op jit(solution)/shard_map/ppermute | solution.py:32
  34.0 1.7 %collective-permute-done.7.refs_3_ = bf16[2,16,1024]{2,1,0:T(8,128)(2,1)S(1)} collective-permute-done((bf16[2,16,1024]{2,1,0:T(8,128)(2,1)S(1)}, bf16[2,16,1024]{2,1,0:T(8,128)(2,1)S(1)}, u32[]{:S(2)}, u32[]{:S(2)}) %collective-permute-start.7) | collective-permute-done | bytes 65568 | tf_op jit(solution)/shard_map/ppermute | solution.py:32
  35.8 1.3 %backward_first.2 = (bf16[160,1024]{1,0:T(8,128)(2,1)S(1)}, bf16[160,1024]{1,0:T(8,128)(2,1)S(1)}, bf16[160,1024]{1,0:T(8,128)(2,1)S(1)}, f32[2,16,256]{2,1,0:T(8,128)S(1)}) custom-call(s32[14]{0:T(128)S(1)} %concatenate.9.meta, bf16[3,1024,1024]{2,1,0:T(8,128)(2,1)S(1)} %get-tuple-element.40.turned, ...), custom_call_target="tpu_custom_call" | custom-call | tf_op jit(solution)/shard_map/backward_first/pallas_call | solution.py:47
  37.0 1.7 %collective-permute-start.12 = (bf16[160,1024]{1,0:T(8,128)(2,1)S(1)}, bf16[160,1024]{1,0:T(8,128)(2,1)S(1)}, u32[]{:S(2)}, u32[]{:S(2)}) collective-permute-start(bf16[160,1024]{1,0:T(8,128)(2,1)S(1)} %get-tuple-element.60), channel_id=1, source_target_pairs={{0,24},{4,12},{8,0},{12,20},{16,8},{20,28},{24,16},{28,4},{1,25},{... | collective-permute-start | bytes 983048 | tf_op jit(solution)/shard_map/ppermute | solution.py:380
  40.8 1.3 %forward_far.3 = (f32[2,16,1024]{2,1,0:T(8,128)S(1)}, bf16[2,16,1024]{2,1,0:T(8,128)(2,1)S(1)}) custom-call(s32[14]{0:T(128)S(1)} %concatenate.9.meta, bf16[5,1024,1024]{2,1,0:T(8,128)(2,1)S(1)} %get-tuple-element.44.held, bf16[2,10,32,1024]{3,2,1,0:T(8,128)(2,1)S(1)} %get-tuple-element.41.perturb, f32[160,1024]{1,0:T(8,128)S(1)} %forward_mid.3.before, ...), custom_call_target="tpu_custom_call" | custom-call | tf_op jit(solution)/shard_map/forward_far/pallas_call | solution.py:47
  43.1 2.0 %collective-permute-start.15 = (bf16[2,16,1024]{2,1,0:T(8,128)(2,1)S(1)}, bf16[2,16,1024]{2,1,0:T(8,128)(2,1)S(1)}, u32[]{:S(2)}, u32[]{:S(2)}) collective-permute-start(bf16[2,16,1024]{2,1,0:T(8,128)(2,1)S(1)} %get-tuple-element.64), channel_id=1, source_target_pairs={{0,2},{1,3},{2,0},{3,1},{4,6},{5,7},{6,4},{7,5},{8,10},{9,11},{10,... | collective-permute-start | bytes 196616 | tf_op jit(solution)/shard_map/ppermute | solution.py:32
  45.6 1.7 %collective-permute-done.12.refs_0_ = bf16[160,1024]{1,0:T(8,128)(2,1)S(1)} collective-permute-done((bf16[160,1024]{1,0:T(8,128)(2,1)S(1)}, bf16[160,1024]{1,0:T(8,128)(2,1)S(1)}, u32[]{:S(2)}, u32[]{:S(2)}) %collective-permute-start.12) | collective-permute-done | bytes 327712 | tf_op jit(solution)/shard_map/ppermute | solution.py:380
  50.3 1.3 %backward_first.3 = (bf16[160,1024]{1,0:T(8,128)(2,1)S(1)}, bf16[80,1024]{1,0:T(8,128)(2,1)S(1)}, bf16[80,1024]{1,0:T(8,128)(2,1)S(1)}, bf16[160,1024]{1,0:T(8,128)(2,1)S(1)}, f32[2,16,256]{2,1,0:T(8,128)S(1)}) custom-call(s32[14]{0:T(128)S(1)} %concatenate.9.meta, bf16[3,1024,1024]{2,1,0:T(8,128)(2,1)S(1)} %get-tuple-element.40.turned, ...), custom_call_target="tpu_custom_call" | custom-call | tf_op jit(solution)/shard_map/backward_first/pallas_call | solution.py:47
  52.2 2.0 %collective-permute-start.22 = (bf16[160,1024]{1,0:T(8,128)(2,1)S(1)}, bf16[160,1024]{1,0:T(8,128)(2,1)S(1)}, u32[]{:S(2)}, u32[]{:S(2)}) collective-permute-start(bf16[160,1024]{1,0:T(8,128)(2,1)S(1)} %get-tuple-element.73), channel_id=1, source_target_pairs={{0,24},{4,12},{8,0},{12,20},{16,8},{20,28},{24,16},{28,4},{1,25},{... | collective-permute-start | bytes 983048 | tf_op jit(solution)/shard_map/ppermute | solution.py:391
  54.2 1.4 %backward_second.1 = bf16[160,1024]{1,0:T(8,128)(2,1)S(1)} custom-call(s32[14]{0:T(128)S(1)} %concatenate.9.meta, bf16[5,1024,1024]{2,1,0:T(8,128)(2,1)S(1)} %get-tuple-element.44.held, bf16[160,1024]{1,0:T(8,128)(2,1)S(1)} %get-tuple-element.75.adjoint_in), custom_call_target="tpu_custom_call" | custom-call | tf_op jit(solution)/shard_map/backward_second/pallas_call | solution.py:47
  56.7 1.2 %collective-permute-start.23 = (bf16[160,1024]{1,0:T(8,128)(2,1)S(1)}, bf16[160,1024]{1,0:T(8,128)(2,1)S(1)}, u32[]{:S(2)}, u32[]{:S(2)}) collective-permute-start(bf16[160,1024]{1,0:T(8,128)(2,1)S(1)} %backward_through.3), channel_id=1, source_target_pairs={{0,8},{4,28},{8,16},{12,4},{16,24},{20,12},{24,0},{28,20},{1,9},{5... | collective-permute-start | bytes 983048 | tf_op jit(solution)/shard_map/ppermute | solution.py:392
  58.0 1.2 %collective-permute-done.19.refs_3_ = bf16[160,1024]{1,0:T(8,128)(2,1)S(1)} collective-permute-done((bf16[160,1024]{1,0:T(8,128)(2,1)S(1)}, bf16[160,1024]{1,0:T(8,128)(2,1)S(1)}, u32[]{:S(2)}, u32[]{:S(2)}) %collective-permute-start.19) | collective-permute-done | bytes 327712 | tf_op jit(solution)/shard_map/ppermute | solution.py:387
  59.2 2.2 %backward_rest.1 = (bf16[80,1024]{1,0:T(8,128)(2,1)S(1)}, bf16[80,1024]{1,0:T(8,128)(2,1)S(1)}, f32[160,1024]{1,0:T(8,128)S(1)}) custom-call(s32[14]{0:T(128)S(1)} %concatenate.9.meta, bf16[5,1024,1024]{2,1,0:T(8,128)(2,1)S(1)} %get-tuple-element.44.held, bf16[160,1024]{1,0:T(8,128)(2,1)S(1)} %get-tuple-element.69.adjoint_in), custom_call_target="tpu_custom_call" | custom-call | tf_op jit(solution)/shard_map/backward_rest/pallas_call | solution.py:47
  63.1 1.4 %backward_kept.1.refs_1_ = f32[160,1024]{1,0:T(8,128)S(1)} custom-call(s32[14]{0:T(128)S(1)} %concatenate.9.meta, bf16[5,1024,1024]{2,1,0:T(8,128)(2,1)S(1)} %get-tuple-element.44.held, bf16[160,1024]{1,0:T(8,128)(2,1)S(1)} %get-tuple-element.75.adjoint_in), custom_call_target="tpu_custom_call" | custom-call | tf_op jit(solution)/shard_map/backward_kept/pallas_call | solution.py:47
  65.5 4.8 %collective-permute-done.22.refs_1_ = bf16[160,1024]{1,0:T(8,128)(2,1)S(1)} collective-permute-done((bf16[160,1024]{1,0:T(8,128)(2,1)S(1)}, bf16[160,1024]{1,0:T(8,128)(2,1)S(1)}, u32[]{:S(2)}, u32[]{:S(2)}) %collective-permute-start.22) | collective-permute-done | bytes 327712 | tf_op jit(solution)/shard_map/ppermute | solution.py:391
  70.3 1.7 %collective-permute-done.23.refs_2_ = bf16[160,1024]{1,0:T(8,128)(2,1)S(1)} collective-permute-done((bf16[160,1024]{1,0:T(8,128)(2,1)S(1)}, bf16[160,1024]{1,0:T(8,128)(2,1)S(1)}, u32[]{:S(2)}, u32[]{:S(2)}) %collective-permute-start.23) | collective-permute-done | bytes 327712 | tf_op jit(solution)/shard_map/ppermute | solution.py:392
  (64 shorter events, 17.7 us)
Async XLA Ops:
  1.8 13.7 %collective-permute-start.1 = (bf16[160,1024]{1,0:T(8,128)(2,1)S(1)}, bf16[160,1024]{1,0:T(8,128)(2,1)S(1)}, u32[]{:S(2)}, u32[]{:S(2)}) collective-permute-start(bf16[160,1024]{1,0:T(8,128)(2,1)S(1)} %bitcast.11), channel_id=1, source_target_pairs={{0,24},{4,12},{8,16},{12,4},{16,8},{20,28},{24,0},{28,20},{1,25},{... | collective-permute-start | bytes 983048 | tf_op jit(solution)/shard_map/ppermute | solution.py:368
  6.9 12.0 %collective-permute-start.2 = (bf16[160,1024]{1,0:T(8,128)(2,1)S(1)}, bf16[160,1024]{1,0:T(8,128)(2,1)S(1)}, u32[]{:S(2)}, u32[]{:S(2)}) collective-permute-start(bf16[160,1024]{1,0:T(8,128)(2,1)S(1)} %bitcast.12), channel_id=1, source_target_pairs={{0,8},{4,28},{8,0},{12,20},{16,24},{20,12},{24,16},{28,4},{1,9},{5... | collective-permute-start | bytes 983048 | tf_op jit(solution)/shard_map/ppermute | solution.py:369
  15.2 9.4 %collective-permute-start = (bf16[320,1024]{1,0:T(8,128)(2,1)S(1)}, bf16[320,1024]{1,0:T(8,128)(2,1)S(1)}, u32[]{:S(2)}, u32[]{:S(2)}) collective-permute-start(bf16[320,1024]{1,0:T(8,128)(2,1)S(1)} %pad_maximum_fusion), channel_id=1, source_target_pairs={{0,4},{4,0},{8,12},{12,8},{16,20},{20,16},{24,28},{28,24},{1,5},{5... | collective-permute-start | bytes 1966088 | tf_op jit(solution)/shard_map/ppermute | solution.py:370
  19.0 19.8 %collective-permute-start.8 = (bf16[160,1024]{1,0:T(8,128)(2,1)S(1)}, bf16[160,1024]{1,0:T(8,128)(2,1)S(1)}, u32[]{:S(2)}, u32[]{:S(2)}) collective-permute-start(bf16[160,1024]{1,0:T(8,128)(2,1)S(1)} %bitcast.9), channel_id=1, source_target_pairs={{0,24},{4,12},{8,16},{12,4},{16,8},{20,28},{24,0},{28,20},{1,25},{... | collective-permute-start | bytes 983048 | tf_op jit(solution)/shard_map/ppermute | solution.py:372
  23.4 15.3 %collective-permute-start.9 = (bf16[160,1024]{1,0:T(8,128)(2,1)S(1)}, bf16[160,1024]{1,0:T(8,128)(2,1)S(1)}, u32[]{:S(2)}, u32[]{:S(2)}) collective-permute-start(bf16[160,1024]{1,0:T(8,128)(2,1)S(1)} %bitcast.10), channel_id=1, source_target_pairs={{0,8},{4,28},{8,0},{12,20},{16,24},{20,12},{24,16},{28,4},{1,9},{5... | collective-permute-start | bytes 983048 | tf_op jit(solution)/shard_map/ppermute | solution.py:373
  24.0 2.2 %collective-permute-start.3 = (bf16[80,1024]{1,0:T(8,128)(2,1)S(1)}, bf16[80,1024]{1,0:T(8,128)(2,1)S(1)}, u32[]{:S(2)}, u32[]{:S(2)}) collective-permute-start(bf16[80,1024]{1,0:T(8,128)(2,1)S(1)} %get-tuple-element.79), channel_id=1, source_target_pairs={{0,4},{4,0},{8,12},{12,8},{16,20},{20,16},{24,28},{28,24},{1,5},{5... | collective-permute-start | bytes 491528 | tf_op jit(solution)/shard_map/ppermute | solution.py:301
  24.5 1.7 %collective-permute-start.4 = (bf16[80,1024]{1,0:T(8,128)(2,1)S(1)}, bf16[80,1024]{1,0:T(8,128)(2,1)S(1)}, u32[]{:S(2)}, u32[]{:S(2)}) collective-permute-start(bf16[80,1024]{1,0:T(8,128)(2,1)S(1)} %get-tuple-element.78), channel_id=1, source_target_pairs={{0,4},{4,0},{8,12},{12,8},{16,20},{20,16},{24,28},{28,24},{1,5},{5... | collective-permute-start | bytes 491528 | tf_op jit(solution)/shard_map/ppermute | solution.py:301
  27.5 4.7 %collective-permute-start.5 = (bf16[2,16,1024]{2,1,0:T(8,128)(2,1)S(1)}, bf16[2,16,1024]{2,1,0:T(8,128)(2,1)S(1)}, u32[]{:S(2)}, u32[]{:S(2)}) collective-permute-start(bf16[2,16,1024]{2,1,0:T(8,128)(2,1)S(1)} %get-tuple-element.53), channel_id=1, source_target_pairs={{0,1},{1,0},{2,3},{3,2},{4,5},{5,4},{6,7},{7,6},{8,9},{9,8},{10,11... | collective-permute-start | bytes 196616 | tf_op jit(solution)/shard_map/ppermute | solution.py:32
  29.1 5.0 %collective-permute-start.6 = (bf16[2,16,1024]{2,1,0:T(8,128)(2,1)S(1)}, bf16[2,16,1024]{2,1,0:T(8,128)(2,1)S(1)}, u32[]{:S(2)}, u32[]{:S(2)}) collective-permute-start(bf16[2,16,1024]{2,1,0:T(8,128)(2,1)S(1)} %get-tuple-element.53), channel_id=1, source_target_pairs={{0,2},{1,3},{2,0},{3,1},{4,6},{5,7},{6,4},{7,5},{8,10},{9,11},{10,... | collective-permute-start | bytes 196616 | tf_op jit(solution)/shard_map/ppermute | solution.py:32
  30.6 5.2 %collective-permute-start.7 = (bf16[2,16,1024]{2,1,0:T(8,128)(2,1)S(1)}, bf16[2,16,1024]{2,1,0:T(8,128)(2,1)S(1)}, u32[]{:S(2)}, u32[]{:S(2)}) collective-permute-start(bf16[2,16,1024]{2,1,0:T(8,128)(2,1)S(1)} %get-tuple-element.53), channel_id=1, source_target_pairs={{0,3},{1,2},{2,1},{3,0},{4,7},{5,6},{6,5},{7,4},{8,11},{9,10},{10,... | collective-permute-start | bytes 196616 | tf_op jit(solution)/shard_map/ppermute | solution.py:32
  37.0 10.3 %collective-permute-start.12 = (bf16[160,1024]{1,0:T(8,128)(2,1)S(1)}, bf16[160,1024]{1,0:T(8,128)(2,1)S(1)}, u32[]{:S(2)}, u32[]{:S(2)}) collective-permute-start(bf16[160,1024]{1,0:T(8,128)(2,1)S(1)} %get-tuple-element.60), channel_id=1, source_target_pairs={{0,24},{4,12},{8,0},{12,20},{16,8},{20,28},{24,16},{28,4},{1,25},{... | collective-permute-start | bytes 983048 | tf_op jit(solution)/shard_map/ppermute | solution.py:380
  38.7 8.6 %collective-permute-start.13 = (bf16[160,1024]{1,0:T(8,128)(2,1)S(1)}, bf16[160,1024]{1,0:T(8,128)(2,1)S(1)}, u32[]{:S(2)}, u32[]{:S(2)}) collective-permute-start(bf16[160,1024]{1,0:T(8,128)(2,1)S(1)} %get-tuple-element.62), channel_id=1, source_target_pairs={{0,4},{4,0},{8,12},{12,8},{16,20},{20,16},{24,28},{28,24},{1,5},{5... | collective-permute-start | bytes 983048 | tf_op jit(solution)/shard_map/ppermute | solution.py:379
  38.8 1.8 %collective-permute-start.10 = (bf16[80,1024]{1,0:T(8,128)(2,1)S(1)}, bf16[80,1024]{1,0:T(8,128)(2,1)S(1)}, u32[]{:S(2)}, u32[]{:S(2)}) collective-permute-start(bf16[80,1024]{1,0:T(8,128)(2,1)S(1)} %get-tuple-element.77), channel_id=1, source_target_pairs={{0,4},{4,0},{8,12},{12,8},{16,20},{20,16},{24,28},{28,24},{1,5},{5... | collective-permute-start | bytes 491528 | tf_op jit(solution)/shard_map/ppermute | solution.py:301
  39.3 1.5 %collective-permute-start.11 = (bf16[80,1024]{1,0:T(8,128)(2,1)S(1)}, bf16[80,1024]{1,0:T(8,128)(2,1)S(1)}, u32[]{:S(2)}, u32[]{:S(2)}) collective-permute-start(bf16[80,1024]{1,0:T(8,128)(2,1)S(1)} %get-tuple-element.76), channel_id=1, source_target_pairs={{0,4},{4,0},{8,12},{12,8},{16,20},{20,16},{24,28},{28,24},{1,5},{5... | collective-permute-start | bytes 491528 | tf_op jit(solution)/shard_map/ppermute | solution.py:301
  42.1 7.2 %collective-permute-start.14 = (bf16[2,16,1024]{2,1,0:T(8,128)(2,1)S(1)}, bf16[2,16,1024]{2,1,0:T(8,128)(2,1)S(1)}, u32[]{:S(2)}, u32[]{:S(2)}) collective-permute-start(bf16[2,16,1024]{2,1,0:T(8,128)(2,1)S(1)} %get-tuple-element.64), channel_id=1, source_target_pairs={{0,1},{1,0},{2,3},{3,2},{4,5},{5,4},{6,7},{7,6},{8,9},{9,8},{10,11... | collective-permute-start | bytes 196616 | tf_op jit(solution)/shard_map/ppermute | solution.py:32
  43.1 6.1 %collective-permute-start.15 = (bf16[2,16,1024]{2,1,0:T(8,128)(2,1)S(1)}, bf16[2,16,1024]{2,1,0:T(8,128)(2,1)S(1)}, u32[]{:S(2)}, u32[]{:S(2)}) collective-permute-start(bf16[2,16,1024]{2,1,0:T(8,128)(2,1)S(1)} %get-tuple-element.64), channel_id=1, source_target_pairs={{0,2},{1,3},{2,0},{3,1},{4,6},{5,7},{6,4},{7,5},{8,10},{9,11},{10,... | collective-permute-start | bytes 196616 | tf_op jit(solution)/shard_map/ppermute | solution.py:32
  45.2 5.2 %collective-permute-start.16 = (bf16[2,16,1024]{2,1,0:T(8,128)(2,1)S(1)}, bf16[2,16,1024]{2,1,0:T(8,128)(2,1)S(1)}, u32[]{:S(2)}, u32[]{:S(2)}) collective-permute-start(bf16[2,16,1024]{2,1,0:T(8,128)(2,1)S(1)} %get-tuple-element.64), channel_id=1, source_target_pairs={{0,3},{1,2},{2,1},{3,0},{4,7},{5,6},{6,5},{7,4},{8,11},{9,10},{10,... | collective-permute-start | bytes 196616 | tf_op jit(solution)/shard_map/ppermute | solution.py:32
  48.4 10.7 %collective-permute-start.19 = (bf16[160,1024]{1,0:T(8,128)(2,1)S(1)}, bf16[160,1024]{1,0:T(8,128)(2,1)S(1)}, u32[]{:S(2)}, u32[]{:S(2)}) collective-permute-start(bf16[160,1024]{1,0:T(8,128)(2,1)S(1)} %backward_through.2), channel_id=1, source_target_pairs={{0,8},{4,28},{8,16},{12,4},{16,24},{20,12},{24,0},{28,20},{1,9},{5... | collective-permute-start | bytes 983048 | tf_op jit(solution)/shard_map/ppermute | solution.py:387
  51.6 2.6 %collective-permute-start.17 = (bf16[80,1024]{1,0:T(8,128)(2,1)S(1)}, bf16[80,1024]{1,0:T(8,128)(2,1)S(1)}, u32[]{:S(2)}, u32[]{:S(2)}) collective-permute-start(bf16[80,1024]{1,0:T(8,128)(2,1)S(1)} %get-tuple-element.67), channel_id=1, source_target_pairs={{0,4},{4,0},{8,12},{12,8},{16,20},{20,16},{24,28},{28,24},{1,5},{5... | collective-permute-start | bytes 491528 | tf_op jit(solution)/shard_map/ppermute | solution.py:388
  51.7 2.5 %collective-permute-start.18 = (bf16[80,1024]{1,0:T(8,128)(2,1)S(1)}, bf16[80,1024]{1,0:T(8,128)(2,1)S(1)}, u32[]{:S(2)}, u32[]{:S(2)}) collective-permute-start(bf16[80,1024]{1,0:T(8,128)(2,1)S(1)} %get-tuple-element.68), channel_id=1, source_target_pairs={{0,4},{4,0},{8,12},{12,8},{16,20},{20,16},{24,28},{28,24},{1,5},{5... | collective-permute-start | bytes 491528 | tf_op jit(solution)/shard_map/ppermute | solution.py:388
  52.2 18.1 %collective-permute-start.22 = (bf16[160,1024]{1,0:T(8,128)(2,1)S(1)}, bf16[160,1024]{1,0:T(8,128)(2,1)S(1)}, u32[]{:S(2)}, u32[]{:S(2)}) collective-permute-start(bf16[160,1024]{1,0:T(8,128)(2,1)S(1)} %get-tuple-element.73), channel_id=1, source_target_pairs={{0,24},{4,12},{8,0},{12,20},{16,8},{20,28},{24,16},{28,4},{1,25},{... | collective-permute-start | bytes 983048 | tf_op jit(solution)/shard_map/ppermute | solution.py:391
  55.6 9.0 %collective-permute-start.24 = (bf16[160,1024]{1,0:T(8,128)(2,1)S(1)}, bf16[160,1024]{1,0:T(8,128)(2,1)S(1)}, u32[]{:S(2)}, u32[]{:S(2)}) collective-permute-start(bf16[160,1024]{1,0:T(8,128)(2,1)S(1)} %backward_second.1), channel_id=1, source_target_pairs={{0,4},{4,0},{8,12},{12,8},{16,20},{20,16},{24,28},{28,24},{1,5},{5... | collective-permute-start | bytes 983048 | tf_op jit(solution)/shard_map/ppermute | solution.py:390
  56.7 15.2 %collective-permute-start.23 = (bf16[160,1024]{1,0:T(8,128)(2,1)S(1)}, bf16[160,1024]{1,0:T(8,128)(2,1)S(1)}, u32[]{:S(2)}, u32[]{:S(2)}) collective-permute-start(bf16[160,1024]{1,0:T(8,128)(2,1)S(1)} %backward_through.3), channel_id=1, source_target_pairs={{0,8},{4,28},{8,16},{12,4},{16,24},{20,12},{24,0},{28,20},{1,9},{5... | collective-permute-start | bytes 983048 | tf_op jit(solution)/shard_map/ppermute | solution.py:392
  61.5 1.6 %collective-permute-start.21 = (bf16[80,1024]{1,0:T(8,128)(2,1)S(1)}, bf16[80,1024]{1,0:T(8,128)(2,1)S(1)}, u32[]{:S(2)}, u32[]{:S(2)}) collective-permute-start(bf16[80,1024]{1,0:T(8,128)(2,1)S(1)} %get-tuple-element.72), channel_id=1, source_target_pairs={{0,4},{4,0},{8,12},{12,8},{16,20},{20,16},{24,28},{28,24},{1,5},{5... | collective-permute-start | bytes 491528 | tf_op jit(solution)/shard_map/ppermute | solution.py:394
  (6 other events, 42.2 us)

commit v5 on v4

--- a/solution.py
+++ b/solution.py
@@ -206,6 +206,10 @@
     transposed_or_zero(meta, held, None, place, adjoint_in, out)
 
 
+def mark(meta, value, kept, out):
+    out[...] = kept[...]
+
+
 def settle(coeffs, *refs):
     *terms, out = refs
     value = coeffs[...].reshape(out.shape)
@@ -310,20 +314,27 @@
     def cut(pieces):
         return [shape((rows // pieces, cells), half)] * pieces
 
-    def respond(c, pieces, terms, *others):
+    def respond(c, pieces, terms, weight, *others):
         adjoint_in, *swap, direct, increment = call(
             functools.partial(backward_first, c, pieces), meta,
-            (turned, held_perturb, held_innovation, held_weight, after(terms[0], *others), *terms[1:]),
+            (turned, held_perturb, held_innovation, weight, after(terms[0], *others), *terms[1:]),
             [rows_half, *cut(pieces), rows_half, shape((window, part, width), full)],
             "backward_first", [pltpu.VMEM((window, part, cells), full)],
         )
         return adjoint_in, swap, direct, increment
 
-    def add_through(adjoint_in, swap, flops=0):
+    def add_through(adjoint_in, swap):
         [through] = call(
-            backward_through, meta, (turned, adjoint_in, *swap), [rows_half], "backward_through", flops=flops
+            backward_through, meta, (turned, adjoint_in, *swap), [rows_half], "backward_through"
         )
         return through
+
+    def arrived(value, kept):
+        [kept] = call(
+            mark, meta, (value, kept), [pltpu.VMEM(kept.shape, kept.dtype)], "mark",
+            spaces=[pl.ANY, pltpu.VMEM], flops=HEAVY,
+        )
+        return resident(kept)
 
     def rest(pieces, adjoint_in, *others):
         *second, kept = call(
@@ -375,16 +386,16 @@
     increment0, sent0 = observe(0, total0, swapped0)
     terms0 = member_terms(increment0, sent0, groups)
     near1 = add(1, near[1], "forward_near", partner=partner)
-    adjoint0, swap0, direct0, part0 = respond(0, 1, terms0, near1)
+    adjoint0, swap0, direct0, part0 = respond(0, 1, terms0, held_weight, near1)
     swap0 = [lax.ppermute(v, "tile", across) for v in swap0]
     direct0 = lax.ppermute(direct0, "tile", inward)
     swapped1 = forwarded(2, below1, above1, adjoint0)
     total1 = add(1, near1, "forward_mid", below=below1, above=above1)
     increment1, sent1 = observe(1, total1, swapped1)
-    through0 = add_through(after(adjoint0, direct0), swap0, flops=HEAVY)
+    through0 = add_through(adjoint0, swap0)
     terms1 = member_terms(increment1, sent1, groups)
-    adjoint1, swap1, direct1, part1 = respond(1, 2, terms1, through0)
     through0 = lax.ppermute(through0, "tile", outward)
+    adjoint1, swap1, direct1, part1 = respond(1, 2, terms1, arrived(direct0, held_weight))
     swap1 = [lax.ppermute(v, "tile", across) for v in swap1]
     second0 = one(PARTNER, rows_half, "backward_second", adjoint0, *swap1)
     second0 = lax.ppermute(second0, "tile", across)

time: 73.1 us -> 72.4 us (level)
  starting transfers between devices: 25.5 us -> 27.9 us
  waiting for transfers between devices: 18.4 us -> 17 us
  Pallas kernels: 23.4 us -> 22.4 us
    ppermute x2, starting transfers between devices: 0.57 us -> 2.68 us  [shards(): second1 = [lax.ppermute(v, 'tile', across) for v in second1]]
    ppermute x1, waiting for transfers between devices: 1.71 us -> 0.01 us  [shards(): direct0 = lax.ppermute(direct0, 'tile', inward)]
    ppermute x1, waiting for transfers between devices: 4.76 us -> 6.04 us  [shards(): direct1 = lax.ppermute(direct1, 'tile', inward)]
    ppermute x6, waiting for transfers between devices: 4.65 us -> 5.82 us  [member_terms(): terms.append(lax.ppermute(sent, 'member', pairs))]
    pallas_call x13 -> x14, Pallas kernels: 21.4 us -> 20.4 us  [call(): pl.pallas_call(body, in_specs=[pl.BlockSpec(memory_space=pltpu.SMEM)] + [...]
    ppermute x1, waiting for transfers between devices: 1.16 us -> 0.33 us  [shards(): through0 = lax.ppermute(through0, 'tile', outward)]
  transfers between devices with their start and end apart: 25 -> 25, of which waited for: 12 -> 10; matrix products, arithmetic and copies ran while one was open for 3% -> 3% of each run, Pallas kernels for 31% -> 29%
where the time goes in v5:
time: 72.4 us; the launch traced here: 72.9 us
  starting transfers between devices  27.9 us (39%)
  Pallas kernels  22.4 us (31%)
  waiting for transfers between devices  17 us (23%)
  local copies, waits for them, and re-layouts  2.4 us (3%)
  between operations  2.28 us (3%)
  other arithmetic  0.96 us (1%)
    pallas_call x14, Pallas kernels, call(): pl.pallas_call(body, in_specs=[pl.BlockSpec(memory_space=pltpu.SMEM)] + [...  20.4 us
    ppermute x6, starting transfers between devices, member_terms(): terms.append(lax.ppermute(sent, 'member', pairs))  7.11 us
    ppermute x1, waiting for transfers between devices, shards(): direct1 = lax.ppermute(direct1, 'tile', inward)  6.04 us
    ppermute x6, waiting for transfers between devices, member_terms(): terms.append(lax.ppermute(sent, 'member', pairs))  5.82 us
    ppermute x1, starting transfers between devices, shards(): below0 = lax.ppermute(own[0], 'tile', below)  5.11 us
    ppermute x1, starting transfers between devices, shards(): below1 = lax.ppermute(after(own[1], below0, above0), 'tile', below)  4.46 us
    ppermute x1, waiting for transfers between devices, shards(): above0 = lax.ppermute(own[0], 'tile', above)  3.03 us
    ppermute x2, starting transfers between devices, shards(): second1 = [lax.ppermute(v, 'tile', across) for v in second1]  2.68 us
  transfers between devices with their start and end apart: 25, of which 10 were waited for; matrix products, arithmetic and copies ran while one was open for 3% of the time, Pallas kernels for 29%

profile of v5, /device:TPU:0, one launch (start us, length us, event | category | flops | bytes accessed | tf_op | source)
XLA Modules:
  0.0 72.9 jit_solution(12698017066258262454)
XLA Ops:
  0.7 1.1 %slice.55 = bf16[10,16,1024]{2,1,0:T(8,128)(2,1)S(1)} slice(f32[10,32,1024]{2,1,0:T(8,128)} %coeffs.3), slice={[0:10], [0:16], [0:1024]} | slice | bytes 655360 | tf_op jit(solution)/shard_map/slice | solution.py:277
  1.8 5.1 %collective-permute-start.1 = (bf16[160,1024]{1,0:T(8,128)(2,1)S(1)}, bf16[160,1024]{1,0:T(8,128)(2,1)S(1)}, u32[]{:S(2)}, u32[]{:S(2)}) collective-permute-start(bf16[160,1024]{1,0:T(8,128)(2,1)S(1)} %bitcast.7), channel_id=1, source_target_pairs={{0,24},{4,12},{8,16},{12,4},{16,8},{20,28},{24,0},{28,20},{1,25},{... | collective-permute-start | bytes 983048 | tf_op jit(solution)/shard_map/ppermute | solution.py:379
  9.7 6.0 %load.1 = (f32[160,1024]{1,0:T(8,128)S(1)}, f32[160,1024]{1,0:T(8,128)S(1)}, bf16[5,1024,1024]{2,1,0:T(8,128)(2,1)S(1)}, bf16[2,10,32,1024]{3,2,1,0:T(8,128)(2,1...) custom-call(s32[14]{0:T(128)S(1)} %concatenate.9.meta, ...), custom_call_target="tpu_custom_call" | custom-call | tf_op jit(solution)/shard_map/load/pallas_call | solution.py:47
  15.9 3.0 %collective-permute-done.2.refs_2_ = bf16[160,1024]{1,0:T(8,128)(2,1)S(1)} collective-permute-done((bf16[160,1024]{1,0:T(8,128)(2,1)S(1)}, bf16[160,1024]{1,0:T(8,128)(2,1)S(1)}, u32[]{:S(2)}, u32[]{:S(2)}) %collective-permute-start.2) | collective-permute-done | bytes 327712 | tf_op jit(solution)/shard_map/ppermute | solution.py:380
  19.0 4.5 %collective-permute-start.9 = (bf16[160,1024]{1,0:T(8,128)(2,1)S(1)}, bf16[160,1024]{1,0:T(8,128)(2,1)S(1)}, u32[]{:S(2)}, u32[]{:S(2)}) collective-permute-start(bf16[160,1024]{1,0:T(8,128)(2,1)S(1)} %bitcast.13), channel_id=1, source_target_pairs={{0,24},{4,12},{8,16},{12,4},{16,8},{20,28},{24,0},{28,20},{1,25},{... | collective-permute-start | bytes 983048 | tf_op jit(solution)/shard_map/ppermute | solution.py:383
  24.6 1.6 %forward_mid.2.before = f32[160,1024]{1,0:T(8,128)S(1)} custom-call(s32[14]{0:T(128)S(1)} %concatenate.9.meta, bf16[5,1024,1024]{2,1,0:T(8,128)(2,1)S(1)} %get-tuple-element.42.held, f32[160,1024]{1,0:T(8,128)S(1)} %get-tuple-element.43.before, bf16[320,1024]{1,0:T(8,128)(2,1)S(1)} %collective-permute-done.refs_0_, ...), custom_call_target="tpu_custom_call" | custom-call | tf_op jit(solution)/shard_map/forward_mid/pallas_call | solution.py:47
  26.3 1.3 %forward_far.2 = (f32[2,16,1024]{2,1,0:T(8,128)S(1)}, bf16[2,16,1024]{2,1,0:T(8,128)(2,1)S(1)}) custom-call(s32[14]{0:T(128)S(1)} %concatenate.9.meta, bf16[5,1024,1024]{2,1,0:T(8,128)(2,1)S(1)} %get-tuple-element.42.held, bf16[2,10,32,1024]{3,2,1,0:T(8,128)(2,1)S(1)} %get-tuple-element.39.perturb, f32[160,1024]{1,0:T(8,128)S(1)} %forward_mid.2.before, ...), custom_call_target="tpu_custom_call" | custom-call | tf_op jit(solution)/shard_map/forward_far/pallas_call | solution.py:47
  27.5 1.6 %collective-permute-start.5 = (bf16[2,16,1024]{2,1,0:T(8,128)(2,1)S(1)}, bf16[2,16,1024]{2,1,0:T(8,128)(2,1)S(1)}, u32[]{:S(2)}, u32[]{:S(2)}) collective-permute-start(bf16[2,16,1024]{2,1,0:T(8,128)(2,1)S(1)} %get-tuple-element.51), channel_id=1, source_target_pairs={{0,1},{1,0},{2,3},{3,2},{4,5},{5,4},{6,7},{7,6},{8,9},{9,8},{10,11... | collective-permute-start | bytes 196616 | tf_op jit(solution)/shard_map/ppermute | solution.py:32
  29.1 1.5 %collective-permute-start.6 = (bf16[2,16,1024]{2,1,0:T(8,128)(2,1)S(1)}, bf16[2,16,1024]{2,1,0:T(8,128)(2,1)S(1)}, u32[]{:S(2)}, u32[]{:S(2)}) collective-permute-start(bf16[2,16,1024]{2,1,0:T(8,128)(2,1)S(1)} %get-tuple-element.51), channel_id=1, source_target_pairs={{0,2},{1,3},{2,0},{3,1},{4,6},{5,7},{6,4},{7,5},{8,10},{9,11},{10,... | collective-permute-start | bytes 196616 | tf_op jit(solution)/shard_map/ppermute | solution.py:32
  31.9 2.2 %collective-permute-done.6.refs_2_ = bf16[2,16,1024]{2,1,0:T(8,128)(2,1)S(1)} collective-permute-done((bf16[2,16,1024]{2,1,0:T(8,128)(2,1)S(1)}, bf16[2,16,1024]{2,1,0:T(8,128)(2,1)S(1)}, u32[]{:S(2)}, u32[]{:S(2)}) %collective-permute-start.6) | collective-permute-done | bytes 65568 | tf_op jit(solution)/shard_map/ppermute | solution.py:32
  34.0 1.7 %collective-permute-done.7.refs_3_ = bf16[2,16,1024]{2,1,0:T(8,128)(2,1)S(1)} collective-permute-done((bf16[2,16,1024]{2,1,0:T(8,128)(2,1)S(1)}, bf16[2,16,1024]{2,1,0:T(8,128)(2,1)S(1)}, u32[]{:S(2)}, u32[]{:S(2)}) %collective-permute-start.7) | collective-permute-done | bytes 65568 | tf_op jit(solution)/shard_map/ppermute | solution.py:32
  35.8 1.8 %backward_first.2 = (bf16[160,1024]{1,0:T(8,128)(2,1)S(1)}, bf16[160,1024]{1,0:T(8,128)(2,1)S(1)}, bf16[160,1024]{1,0:T(8,128)(2,1)S(1)}, f32[2,16,256]{2,1,0:T(8,128)S(1)}) custom-call(s32[14]{0:T(128)S(1)} %concatenate.9.meta, bf16[3,1024,1024]{2,1,0:T(8,128)(2,1)S(1)} %get-tuple-element.38.turned, ...), custom_call_target="tpu_custom_call" | custom-call | tf_op jit(solution)/shard_map/backward_first/pallas_call | solution.py:47
  37.5 2.0 %collective-permute-start.8 = (bf16[160,1024]{1,0:T(8,128)(2,1)S(1)}, bf16[160,1024]{1,0:T(8,128)(2,1)S(1)}, u32[]{:S(2)}, u32[]{:S(2)}) collective-permute-start(bf16[160,1024]{1,0:T(8,128)(2,1)S(1)} %get-tuple-element.53), channel_id=1, source_target_pairs={{0,24},{4,12},{8,0},{12,20},{16,8},{20,28},{24,16},{28,4},{1,25},{... | collective-permute-start | bytes 983048 | tf_op jit(solution)/shard_map/ppermute | solution.py:391
  40.3 1.6 %forward_mid.3.before = f32[160,1024]{1,0:T(8,128)S(1)} custom-call(s32[14]{0:T(128)S(1)} %concatenate.9.meta, bf16[5,1024,1024]{2,1,0:T(8,128)(2,1)S(1)} %get-tuple-element.42.held, f32[160,1024]{1,0:T(8,128)S(1)} %forward_near.1.before, bf16[160,1024]{1,0:T(8,128)(2,1)S(1)} %collective-permute-done.9.refs_0_, ...), custom_call_target="tpu_custom_call" | custom-call | tf_op jit(solution)/shard_map/forward_mid/pallas_call | solution.py:47
  41.9 1.3 %forward_far.3 = (f32[2,16,1024]{2,1,0:T(8,128)S(1)}, bf16[2,16,1024]{2,1,0:T(8,128)(2,1)S(1)}) custom-call(s32[14]{0:T(128)S(1)} %concatenate.9.meta, bf16[5,1024,1024]{2,1,0:T(8,128)(2,1)S(1)} %get-tuple-element.42.held, bf16[2,10,32,1024]{3,2,1,0:T(8,128)(2,1)S(1)} %get-tuple-element.39.perturb, f32[160,1024]{1,0:T(8,128)S(1)} %forward_mid.3.before, ...), custom_call_target="tpu_custom_call" | custom-call | tf_op jit(solution)/shard_map/forward_far/pallas_call | solution.py:47
  43.9 1.5 %collective-permute-start.14 = (bf16[2,16,1024]{2,1,0:T(8,128)(2,1)S(1)}, bf16[2,16,1024]{2,1,0:T(8,128)(2,1)S(1)}, u32[]{:S(2)}, u32[]{:S(2)}) collective-permute-start(bf16[2,16,1024]{2,1,0:T(8,128)(2,1)S(1)} %get-tuple-element.59), channel_id=1, source_target_pairs={{0,2},{1,3},{2,0},{3,1},{4,6},{5,7},{6,4},{7,5},{8,10},{9,11},{10,... | collective-permute-start | bytes 196616 | tf_op jit(solution)/shard_map/ppermute | solution.py:32
  45.4 1.3 %collective-permute-start.15 = (bf16[2,16,1024]{2,1,0:T(8,128)(2,1)S(1)}, bf16[2,16,1024]{2,1,0:T(8,128)(2,1)S(1)}, u32[]{:S(2)}, u32[]{:S(2)}) collective-permute-start(bf16[2,16,1024]{2,1,0:T(8,128)(2,1)S(1)} %get-tuple-element.59), channel_id=1, source_target_pairs={{0,3},{1,2},{2,1},{3,0},{4,7},{5,6},{6,5},{7,4},{8,11},{9,10},{10,... | collective-permute-start | bytes 196616 | tf_op jit(solution)/shard_map/ppermute | solution.py:32
  48.9 1.7 %collective-permute-done.15.refs_3_ = bf16[2,16,1024]{2,1,0:T(8,128)(2,1)S(1)} collective-permute-done((bf16[2,16,1024]{2,1,0:T(8,128)(2,1)S(1)}, bf16[2,16,1024]{2,1,0:T(8,128)(2,1)S(1)}, u32[]{:S(2)}, u32[]{:S(2)}) %collective-permute-start.15) | collective-permute-done | bytes 65568 | tf_op jit(solution)/shard_map/ppermute | solution.py:32
  50.6 1.8 %backward_first.3 = (bf16[160,1024]{1,0:T(8,128)(2,1)S(1)}, bf16[80,1024]{1,0:T(8,128)(2,1)S(1)}, bf16[80,1024]{1,0:T(8,128)(2,1)S(1)}, bf16[160,1024]{1,0:T(8,128)(2,1)S(1)}, f32[2,16,256]{2,1,0:T(8,128)S(1)}) custom-call(s32[14]{0:T(128)S(1)} %concatenate.9.meta, bf16[3,1024,1024]{2,1,0:T(8,128)(2,1)S(1)} %get-tuple-element.38.turned, ...), custom_call_target="tpu_custom_call" | custom-call | tf_op jit(solution)/shard_map/backward_first/pallas_call | solution.py:47
  52.9 1.7 %collective-permute-start.22 = (bf16[160,1024]{1,0:T(8,128)(2,1)S(1)}, bf16[160,1024]{1,0:T(8,128)(2,1)S(1)}, u32[]{:S(2)}, u32[]{:S(2)}) collective-permute-start(bf16[160,1024]{1,0:T(8,128)(2,1)S(1)} %get-tuple-element.69), channel_id=1, source_target_pairs={{0,24},{4,12},{8,0},{12,20},{16,8},{20,28},{24,16},{28,4},{1,25},{... | collective-permute-start | bytes 983048 | tf_op jit(solution)/shard_map/ppermute | solution.py:402
  56.9 1.3 %collective-permute-start.23 = (bf16[160,1024]{1,0:T(8,128)(2,1)S(1)}, bf16[160,1024]{1,0:T(8,128)(2,1)S(1)}, u32[]{:S(2)}, u32[]{:S(2)}) collective-permute-start(bf16[160,1024]{1,0:T(8,128)(2,1)S(1)} %backward_through.3), channel_id=1, source_target_pairs={{0,8},{4,28},{8,16},{12,4},{16,24},{20,12},{24,0},{28,20},{1,9},{5... | collective-permute-start | bytes 983048 | tf_op jit(solution)/shard_map/ppermute | solution.py:403
  59.1 2.6 %collective-permute-start.20 = (bf16[80,1024]{1,0:T(8,128)(2,1)S(1)}, bf16[80,1024]{1,0:T(8,128)(2,1)S(1)}, u32[]{:S(2)}, u32[]{:S(2)}) collective-permute-start(bf16[80,1024]{1,0:T(8,128)(2,1)S(1)} %get-tuple-element.67), channel_id=1, source_target_pairs={{0,4},{4,0},{8,12},{12,8},{16,20},{20,16},{24,28},{28,24},{1,5},{5... | collective-permute-start | bytes 491528 | tf_op jit(solution)/shard_map/ppermute | solution.py:405
  64.8 6.0 %collective-permute-done.22.refs_1_ = bf16[160,1024]{1,0:T(8,128)(2,1)S(1)} collective-permute-done((bf16[160,1024]{1,0:T(8,128)(2,1)S(1)}, bf16[160,1024]{1,0:T(8,128)(2,1)S(1)}, u32[]{:S(2)}, u32[]{:S(2)}) %collective-permute-start.22) | collective-permute-done | bytes 327712 | tf_op jit(solution)/shard_map/ppermute | solution.py:402
  70.8 1.1 %collective-permute-done.23.refs_2_ = bf16[160,1024]{1,0:T(8,128)(2,1)S(1)} collective-permute-done((bf16[160,1024]{1,0:T(8,128)(2,1)S(1)}, bf16[160,1024]{1,0:T(8,128)(2,1)S(1)}, u32[]{:S(2)}, u32[]{:S(2)}) %collective-permute-start.23) | collective-permute-done | bytes 327712 | tf_op jit(solution)/shard_map/ppermute | solution.py:403
  (65 shorter events, 15.1 us)
Async XLA Ops:
  1.8 14.1 %collective-permute-start.1 = (bf16[160,1024]{1,0:T(8,128)(2,1)S(1)}, bf16[160,1024]{1,0:T(8,128)(2,1)S(1)}, u32[]{:S(2)}, u32[]{:S(2)}) collective-permute-start(bf16[160,1024]{1,0:T(8,128)(2,1)S(1)} %bitcast.7), channel_id=1, source_target_pairs={{0,24},{4,12},{8,16},{12,4},{16,8},{20,28},{24,0},{28,20},{1,25},{... | collective-permute-start | bytes 983048 | tf_op jit(solution)/shard_map/ppermute | solution.py:379
  6.9 12.0 %collective-permute-start.2 = (bf16[160,1024]{1,0:T(8,128)(2,1)S(1)}, bf16[160,1024]{1,0:T(8,128)(2,1)S(1)}, u32[]{:S(2)}, u32[]{:S(2)}) collective-permute-start(bf16[160,1024]{1,0:T(8,128)(2,1)S(1)} %bitcast.8), channel_id=1, source_target_pairs={{0,8},{4,28},{8,0},{12,20},{16,24},{20,12},{24,16},{28,4},{1,9},{5... | collective-permute-start | bytes 983048 | tf_op jit(solution)/shard_map/ppermute | solution.py:380
  15.8 8.7 %collective-permute-start = (bf16[320,1024]{1,0:T(8,128)(2,1)S(1)}, bf16[320,1024]{1,0:T(8,128)(2,1)S(1)}, u32[]{:S(2)}, u32[]{:S(2)}) collective-permute-start(bf16[320,1024]{1,0:T(8,128)(2,1)S(1)} %pad_maximum_fusion), channel_id=1, source_target_pairs={{0,4},{4,0},{8,12},{12,8},{16,20},{20,16},{24,28},{28,24},{1,5},{5... | collective-permute-start | bytes 1966088 | tf_op jit(solution)/shard_map/ppermute | solution.py:381
  19.0 20.6 %collective-permute-start.9 = (bf16[160,1024]{1,0:T(8,128)(2,1)S(1)}, bf16[160,1024]{1,0:T(8,128)(2,1)S(1)}, u32[]{:S(2)}, u32[]{:S(2)}) collective-permute-start(bf16[160,1024]{1,0:T(8,128)(2,1)S(1)} %bitcast.13), channel_id=1, source_target_pairs={{0,24},{4,12},{8,16},{12,4},{16,8},{20,28},{24,0},{28,20},{1,25},{... | collective-permute-start | bytes 983048 | tf_op jit(solution)/shard_map/ppermute | solution.py:383
  23.4 16.2 %collective-permute-start.10 = (bf16[160,1024]{1,0:T(8,128)(2,1)S(1)}, bf16[160,1024]{1,0:T(8,128)(2,1)S(1)}, u32[]{:S(2)}, u32[]{:S(2)}) collective-permute-start(bf16[160,1024]{1,0:T(8,128)(2,1)S(1)} %bitcast.14), channel_id=1, source_target_pairs={{0,8},{4,28},{8,0},{12,20},{16,24},{20,12},{24,16},{28,4},{1,9},{5... | collective-permute-start | bytes 983048 | tf_op jit(solution)/shard_map/ppermute | solution.py:384
  24.0 2.3 %collective-permute-start.3 = (bf16[80,1024]{1,0:T(8,128)(2,1)S(1)}, bf16[80,1024]{1,0:T(8,128)(2,1)S(1)}, u32[]{:S(2)}, u32[]{:S(2)}) collective-permute-start(bf16[80,1024]{1,0:T(8,128)(2,1)S(1)} %get-tuple-element.75), channel_id=1, source_target_pairs={{0,4},{4,0},{8,12},{12,8},{16,20},{20,16},{24,28},{28,24},{1,5},{5... | collective-permute-start | bytes 491528 | tf_op jit(solution)/shard_map/ppermute | solution.py:305
  24.5 1.7 %collective-permute-start.4 = (bf16[80,1024]{1,0:T(8,128)(2,1)S(1)}, bf16[80,1024]{1,0:T(8,128)(2,1)S(1)}, u32[]{:S(2)}, u32[]{:S(2)}) collective-permute-start(bf16[80,1024]{1,0:T(8,128)(2,1)S(1)} %get-tuple-element.74), channel_id=1, source_target_pairs={{0,4},{4,0},{8,12},{12,8},{16,20},{20,16},{24,28},{28,24},{1,5},{5... | collective-permute-start | bytes 491528 | tf_op jit(solution)/shard_map/ppermute | solution.py:305
  27.5 4.3 %collective-permute-start.5 = (bf16[2,16,1024]{2,1,0:T(8,128)(2,1)S(1)}, bf16[2,16,1024]{2,1,0:T(8,128)(2,1)S(1)}, u32[]{:S(2)}, u32[]{:S(2)}) collective-permute-start(bf16[2,16,1024]{2,1,0:T(8,128)(2,1)S(1)} %get-tuple-element.51), channel_id=1, source_target_pairs={{0,1},{1,0},{2,3},{3,2},{4,5},{5,4},{6,7},{7,6},{8,9},{9,8},{10,11... | collective-permute-start | bytes 196616 | tf_op jit(solution)/shard_map/ppermute | solution.py:32
  29.1 5.0 %collective-permute-start.6 = (bf16[2,16,1024]{2,1,0:T(8,128)(2,1)S(1)}, bf16[2,16,1024]{2,1,0:T(8,128)(2,1)S(1)}, u32[]{:S(2)}, u32[]{:S(2)}) collective-permute-start(bf16[2,16,1024]{2,1,0:T(8,128)(2,1)S(1)} %get-tuple-element.51), channel_id=1, source_target_pairs={{0,2},{1,3},{2,0},{3,1},{4,6},{5,7},{6,4},{7,5},{8,10},{9,11},{10,... | collective-permute-start | bytes 196616 | tf_op jit(solution)/shard_map/ppermute | solution.py:32
  30.6 5.2 %collective-permute-start.7 = (bf16[2,16,1024]{2,1,0:T(8,128)(2,1)S(1)}, bf16[2,16,1024]{2,1,0:T(8,128)(2,1)S(1)}, u32[]{:S(2)}, u32[]{:S(2)}) collective-permute-start(bf16[2,16,1024]{2,1,0:T(8,128)(2,1)S(1)} %get-tuple-element.51), channel_id=1, source_target_pairs={{0,3},{1,2},{2,1},{3,0},{4,7},{5,6},{6,5},{7,4},{8,11},{9,10},{10,... | collective-permute-start | bytes 196616 | tf_op jit(solution)/shard_map/ppermute | solution.py:32
  37.5 10.8 %collective-permute-start.8 = (bf16[160,1024]{1,0:T(8,128)(2,1)S(1)}, bf16[160,1024]{1,0:T(8,128)(2,1)S(1)}, u32[]{:S(2)}, u32[]{:S(2)}) collective-permute-start(bf16[160,1024]{1,0:T(8,128)(2,1)S(1)} %get-tuple-element.53), channel_id=1, source_target_pairs={{0,24},{4,12},{8,0},{12,20},{16,8},{20,28},{24,16},{28,4},{1,25},{... | collective-permute-start | bytes 983048 | tf_op jit(solution)/shard_map/ppermute | solution.py:391
  39.6 7.2 %collective-permute-start.18 = (bf16[160,1024]{1,0:T(8,128)(2,1)S(1)}, bf16[160,1024]{1,0:T(8,128)(2,1)S(1)}, u32[]{:S(2)}, u32[]{:S(2)}) collective-permute-start(bf16[160,1024]{1,0:T(8,128)(2,1)S(1)} %get-tuple-element.64), channel_id=1, source_target_pairs={{0,4},{4,0},{8,12},{12,8},{16,20},{20,16},{24,28},{28,24},{1,5},{5... | collective-permute-start | bytes 983048 | tf_op jit(solution)/shard_map/ppermute | solution.py:390
  39.7 2.3 %collective-permute-start.11 = (bf16[80,1024]{1,0:T(8,128)(2,1)S(1)}, bf16[80,1024]{1,0:T(8,128)(2,1)S(1)}, u32[]{:S(2)}, u32[]{:S(2)}) collective-permute-start(bf16[80,1024]{1,0:T(8,128)(2,1)S(1)} %get-tuple-element.73), channel_id=1, source_target_pairs={{0,4},{4,0},{8,12},{12,8},{16,20},{20,16},{24,28},{28,24},{1,5},{5... | collective-permute-start | bytes 491528 | tf_op jit(solution)/shard_map/ppermute | solution.py:305
  40.2 1.7 %collective-permute-start.12 = (bf16[80,1024]{1,0:T(8,128)(2,1)S(1)}, bf16[80,1024]{1,0:T(8,128)(2,1)S(1)}, u32[]{:S(2)}, u32[]{:S(2)}) collective-permute-start(bf16[80,1024]{1,0:T(8,128)(2,1)S(1)} %get-tuple-element.72), channel_id=1, source_target_pairs={{0,4},{4,0},{8,12},{12,8},{16,20},{20,16},{24,28},{28,24},{1,5},{5... | collective-permute-start | bytes 491528 | tf_op jit(solution)/shard_map/ppermute | solution.py:305
  43.2 5.7 %collective-permute-start.13 = (bf16[2,16,1024]{2,1,0:T(8,128)(2,1)S(1)}, bf16[2,16,1024]{2,1,0:T(8,128)(2,1)S(1)}, u32[]{:S(2)}, u32[]{:S(2)}) collective-permute-start(bf16[2,16,1024]{2,1,0:T(8,128)(2,1)S(1)} %get-tuple-element.59), channel_id=1, source_target_pairs={{0,1},{1,0},{2,3},{3,2},{4,5},{5,4},{6,7},{7,6},{8,9},{9,8},{10,11... | collective-permute-start | bytes 196616 | tf_op jit(solution)/shard_map/ppermute | solution.py:32
  43.9 5.0 %collective-permute-start.14 = (bf16[2,16,1024]{2,1,0:T(8,128)(2,1)S(1)}, bf16[2,16,1024]{2,1,0:T(8,128)(2,1)S(1)}, u32[]{:S(2)}, u32[]{:S(2)}) collective-permute-start(bf16[2,16,1024]{2,1,0:T(8,128)(2,1)S(1)} %get-tuple-element.59), channel_id=1, source_target_pairs={{0,2},{1,3},{2,0},{3,1},{4,6},{5,7},{6,4},{7,5},{8,10},{9,11},{10,... | collective-permute-start | bytes 196616 | tf_op jit(solution)/shard_map/ppermute | solution.py:32
  45.4 5.2 %collective-permute-start.15 = (bf16[2,16,1024]{2,1,0:T(8,128)(2,1)S(1)}, bf16[2,16,1024]{2,1,0:T(8,128)(2,1)S(1)}, u32[]{:S(2)}, u32[]{:S(2)}) collective-permute-start(bf16[2,16,1024]{2,1,0:T(8,128)(2,1)S(1)} %get-tuple-element.59), channel_id=1, source_target_pairs={{0,3},{1,2},{2,1},{3,0},{4,7},{5,6},{6,5},{7,4},{8,11},{9,10},{10,... | collective-permute-start | bytes 196616 | tf_op jit(solution)/shard_map/ppermute | solution.py:32
  47.8 10.7 %collective-permute-start.19 = (bf16[160,1024]{1,0:T(8,128)(2,1)S(1)}, bf16[160,1024]{1,0:T(8,128)(2,1)S(1)}, u32[]{:S(2)}, u32[]{:S(2)}) collective-permute-start(bf16[160,1024]{1,0:T(8,128)(2,1)S(1)} %backward_through.2), channel_id=1, source_target_pairs={{0,8},{4,28},{8,16},{12,4},{16,24},{20,12},{24,0},{28,20},{1,9},{5... | collective-permute-start | bytes 983048 | tf_op jit(solution)/shard_map/ppermute | solution.py:397
  52.4 2.3 %collective-permute-start.16 = (bf16[80,1024]{1,0:T(8,128)(2,1)S(1)}, bf16[80,1024]{1,0:T(8,128)(2,1)S(1)}, u32[]{:S(2)}, u32[]{:S(2)}) collective-permute-start(bf16[80,1024]{1,0:T(8,128)(2,1)S(1)} %get-tuple-element.62), channel_id=1, source_target_pairs={{0,4},{4,0},{8,12},{12,8},{16,20},{20,16},{24,28},{28,24},{1,5},{5... | collective-permute-start | bytes 491528 | tf_op jit(solution)/shard_map/ppermute | solution.py:399
  52.4 2.2 %collective-permute-start.17 = (bf16[80,1024]{1,0:T(8,128)(2,1)S(1)}, bf16[80,1024]{1,0:T(8,128)(2,1)S(1)}, u32[]{:S(2)}, u32[]{:S(2)}) collective-permute-start(bf16[80,1024]{1,0:T(8,128)(2,1)S(1)} %get-tuple-element.63), channel_id=1, source_target_pairs={{0,4},{4,0},{8,12},{12,8},{16,20},{20,16},{24,28},{28,24},{1,5},{5... | collective-permute-start | bytes 491528 | tf_op jit(solution)/shard_map/ppermute | solution.py:399
  52.9 17.9 %collective-permute-start.22 = (bf16[160,1024]{1,0:T(8,128)(2,1)S(1)}, bf16[160,1024]{1,0:T(8,128)(2,1)S(1)}, u32[]{:S(2)}, u32[]{:S(2)}) collective-permute-start(bf16[160,1024]{1,0:T(8,128)(2,1)S(1)} %get-tuple-element.69), channel_id=1, source_target_pairs={{0,24},{4,12},{8,0},{12,20},{16,8},{20,28},{24,16},{28,4},{1,25},{... | collective-permute-start | bytes 983048 | tf_op jit(solution)/shard_map/ppermute | solution.py:402
  55.2 8.6 %collective-permute-start.24 = (bf16[160,1024]{1,0:T(8,128)(2,1)S(1)}, bf16[160,1024]{1,0:T(8,128)(2,1)S(1)}, u32[]{:S(2)}, u32[]{:S(2)}) collective-permute-start(bf16[160,1024]{1,0:T(8,128)(2,1)S(1)} %backward_second.1), channel_id=1, source_target_pairs={{0,4},{4,0},{8,12},{12,8},{16,20},{20,16},{24,28},{28,24},{1,5},{5... | collective-permute-start | bytes 983048 | tf_op jit(solution)/shard_map/ppermute | solution.py:401
  56.9 15.1 %collective-permute-start.23 = (bf16[160,1024]{1,0:T(8,128)(2,1)S(1)}, bf16[160,1024]{1,0:T(8,128)(2,1)S(1)}, u32[]{:S(2)}, u32[]{:S(2)}) collective-permute-start(bf16[160,1024]{1,0:T(8,128)(2,1)S(1)} %backward_through.3), channel_id=1, source_target_pairs={{0,8},{4,28},{8,16},{12,4},{16,24},{20,12},{24,0},{28,20},{1,9},{5... | collective-permute-start | bytes 983048 | tf_op jit(solution)/shard_map/ppermute | solution.py:403
  59.1 3.6 %collective-permute-start.20 = (bf16[80,1024]{1,0:T(8,128)(2,1)S(1)}, bf16[80,1024]{1,0:T(8,128)(2,1)S(1)}, u32[]{:S(2)}, u32[]{:S(2)}) collective-permute-start(bf16[80,1024]{1,0:T(8,128)(2,1)S(1)} %get-tuple-element.67), channel_id=1, source_target_pairs={{0,4},{4,0},{8,12},{12,8},{16,20},{20,16},{24,28},{28,24},{1,5},{5... | collective-permute-start | bytes 491528 | tf_op jit(solution)/shard_map/ppermute | solution.py:405
  (6 other events, 41.9 us)

commit v6 on v5

--- a/solution.py
+++ b/solution.py
@@ -206,10 +206,6 @@
     transposed_or_zero(meta, held, None, place, adjoint_in, out)
 
 
-def mark(meta, value, kept, out):
-    out[...] = kept[...]
-
-
 def settle(coeffs, *refs):
     *terms, out = refs
     value = coeffs[...].reshape(out.shape)
@@ -329,13 +325,6 @@
         )
         return through
 
-    def arrived(value, kept):
-        [kept] = call(
-            mark, meta, (value, kept), [pltpu.VMEM(kept.shape, kept.dtype)], "mark",
-            spaces=[pl.ANY, pltpu.VMEM], flops=HEAVY,
-        )
-        return resident(kept)
-
     def rest(pieces, adjoint_in, *others):
         *second, kept = call(
             backward_rest, meta, (held, after(adjoint_in, *others)), [*cut(pieces), rows_full],
@@ -343,9 +332,10 @@
         )
         return second, kept
 
-    def one(place, out, name, adjoint_in, *others):
+    def one(place, out, name, adjoint_in, *others, flops=0):
         [value] = call(
-            functools.partial(backward_one, place), meta, (held, after(adjoint_in, *others)), [out], name
+            functools.partial(backward_one, place), meta, (held, after(adjoint_in, *others)), [out], name,
+            flops=flops,
         )
         return value
 
@@ -395,9 +385,9 @@
     through0 = add_through(adjoint0, swap0)
     terms1 = member_terms(increment1, sent1, groups)
     through0 = lax.ppermute(through0, "tile", outward)
-    adjoint1, swap1, direct1, part1 = respond(1, 2, terms1, arrived(direct0, held_weight))
+    second0 = one(PARTNER, rows_half, "backward_second", adjoint0, direct0, flops=HEAVY)
+    adjoint1, swap1, direct1, part1 = respond(1, 2, terms1, held_weight, second0)
     swap1 = [lax.ppermute(v, "tile", across) for v in swap1]
-    second0 = one(PARTNER, rows_half, "backward_second", adjoint0, *swap1)
     second0 = lax.ppermute(second0, "tile", across)
     direct1 = lax.ppermute(direct1, "tile", inward)
     through1 = lax.ppermute(add_through(adjoint1, swap1), "tile", outward)

time: 72.4 us -> 72.7 us (level)
  Pallas kernels: 22.4 us -> 26.1 us
  starting transfers between devices: 27.9 us -> 24.9 us
  waiting for transfers between devices: 17 us -> 16 us
    pallas_call x14 -> x13, Pallas kernels: 20.4 us -> 24.1 us  [call(): pl.pallas_call(body, in_specs=[pl.BlockSpec(memory_space=pltpu.SMEM)] + [...]
    ppermute x6, waiting for transfers between devices: 5.82 us -> 3.56 us  [member_terms(): terms.append(lax.ppermute(sent, 'member', pairs))]
    ppermute x2, starting transfers between devices: 2.68 us -> 0.57 us  [shards(): second1 = [lax.ppermute(v, 'tile', across) for v in second1]]
    ppermute x1, starting transfers between devices: 1.32 us -> 0.06 us  [shards(): through1 = lax.ppermute(add_through(adjoint1, swap1), 'tile', outward)]
    ppermute x1, starting transfers between devices: 1.71 us -> 2.97 us  [shards(): direct1 = lax.ppermute(direct1, 'tile', inward)]
    ppermute x1, waiting for transfers between devices: 6.04 us -> 6.94 us  [shards(): direct1 = lax.ppermute(direct1, 'tile', inward)]
    ppermute x1, waiting for transfers between devices: 0.33 us -> 1.21 us  [shards(): through0 = lax.ppermute(through0, 'tile', outward)]
  transfers between devices with their start and end apart: 25 -> 25, of which waited for: 10 -> 9; matrix products, arithmetic and copies ran while one was open for 3% -> 3% of each run, Pallas kernels for 29% -> 35%
where the time goes in v6:
time: 72.7 us; the launch traced here: 72.6 us
  Pallas kernels  26.1 us (36%)
  starting transfers between devices  24.9 us (34%)
  waiting for transfers between devices  16 us (22%)
  local copies, waits for them, and re-layouts  2.4 us (3%)
  between operations  2.28 us (3%)
  other arithmetic  0.96 us (1%)
    pallas_call x13, Pallas kernels, call(): pl.pallas_call(body, in_specs=[pl.BlockSpec(memory_space=pltpu.SMEM)] + [...  24.1 us
    ppermute x6, starting transfers between devices, member_terms(): terms.append(lax.ppermute(sent, 'member', pairs))  7.11 us
    ppermute x1, waiting for transfers between devices, shards(): direct1 = lax.ppermute(direct1, 'tile', inward)  6.94 us
    ppermute x1, starting transfers between devices, shards(): below0 = lax.ppermute(own[0], 'tile', below)  5.11 us
    ppermute x1, starting transfers between devices, shards(): below1 = lax.ppermute(after(own[1], below0, above0), 'tile', below)  4.46 us
    ppermute x6, waiting for transfers between devices, member_terms(): terms.append(lax.ppermute(sent, 'member', pairs))  3.56 us
    ppermute x1, waiting for transfers between devices, shards(): above0 = lax.ppermute(own[0], 'tile', above)  3.04 us
    ppermute x1, starting transfers between devices, shards(): direct1 = lax.ppermute(direct1, 'tile', inward)  2.97 us
  transfers between devices with their start and end apart: 25, of which 9 were waited for; matrix products, arithmetic and copies ran while one was open for 3% of the time, Pallas kernels for 35%

profile of v6, /device:TPU:0, one launch (start us, length us, event | category | flops | bytes accessed | tf_op | source)
XLA Modules:
  0.0 72.6 jit_solution(11528130291293126172)
XLA Ops:
  0.7 1.1 %slice.55 = bf16[10,16,1024]{2,1,0:T(8,128)(2,1)S(1)} slice(f32[10,32,1024]{2,1,0:T(8,128)} %coeffs.3), slice={[0:10], [0:16], [0:1024]} | slice | bytes 655360 | tf_op jit(solution)/shard_map/slice | solution.py:273
  1.8 5.1 %collective-permute-start.1 = (bf16[160,1024]{1,0:T(8,128)(2,1)S(1)}, bf16[160,1024]{1,0:T(8,128)(2,1)S(1)}, u32[]{:S(2)}, u32[]{:S(2)}) collective-permute-start(bf16[160,1024]{1,0:T(8,128)(2,1)S(1)} %bitcast.11), channel_id=1, source_target_pairs={{0,24},{4,12},{8,16},{12,4},{16,8},{20,28},{24,0},{28,20},{1,25},{... | collective-permute-start | bytes 983048 | tf_op jit(solution)/shard_map/ppermute | solution.py:369
  9.7 6.0 %load.1 = (f32[160,1024]{1,0:T(8,128)S(1)}, f32[160,1024]{1,0:T(8,128)S(1)}, bf16[5,1024,1024]{2,1,0:T(8,128)(2,1)S(1)}, bf16[2,10,32,1024]{3,2,1,0:T(8,128)(2,1...) custom-call(s32[14]{0:T(128)S(1)} %concatenate.9.meta, ...), custom_call_target="tpu_custom_call" | custom-call | tf_op jit(solution)/shard_map/load/pallas_call | solution.py:47
  15.9 3.0 %collective-permute-done.2.refs_2_ = bf16[160,1024]{1,0:T(8,128)(2,1)S(1)} collective-permute-done((bf16[160,1024]{1,0:T(8,128)(2,1)S(1)}, bf16[160,1024]{1,0:T(8,128)(2,1)S(1)}, u32[]{:S(2)}, u32[]{:S(2)}) %collective-permute-start.2) | collective-permute-done | bytes 327712 | tf_op jit(solution)/shard_map/ppermute | solution.py:370
  19.0 4.5 %collective-permute-start.8 = (bf16[160,1024]{1,0:T(8,128)(2,1)S(1)}, bf16[160,1024]{1,0:T(8,128)(2,1)S(1)}, u32[]{:S(2)}, u32[]{:S(2)}) collective-permute-start(bf16[160,1024]{1,0:T(8,128)(2,1)S(1)} %bitcast.9), channel_id=1, source_target_pairs={{0,24},{4,12},{8,16},{12,4},{16,8},{20,28},{24,0},{28,20},{1,25},{... | collective-permute-start | bytes 983048 | tf_op jit(solution)/shard_map/ppermute | solution.py:373
  24.6 2.2 %forward_mid.2.before = f32[160,1024]{1,0:T(8,128)S(1)} custom-call(s32[14]{0:T(128)S(1)} %concatenate.9.meta, bf16[5,1024,1024]{2,1,0:T(8,128)(2,1)S(1)} %get-tuple-element.43.held, f32[160,1024]{1,0:T(8,128)S(1)} %get-tuple-element.44.before, bf16[320,1024]{1,0:T(8,128)(2,1)S(1)} %collective-permute-done.refs_0_, ...), custom_call_target="tpu_custom_call" | custom-call | tf_op jit(solution)/shard_map/forward_mid/pallas_call | solution.py:47
  26.8 1.3 %forward_far.2 = (f32[2,16,1024]{2,1,0:T(8,128)S(1)}, bf16[2,16,1024]{2,1,0:T(8,128)(2,1)S(1)}) custom-call(s32[14]{0:T(128)S(1)} %concatenate.9.meta, bf16[5,1024,1024]{2,1,0:T(8,128)(2,1)S(1)} %get-tuple-element.43.held, bf16[2,10,32,1024]{3,2,1,0:T(8,128)(2,1)S(1)} %get-tuple-element.40.perturb, f32[160,1024]{1,0:T(8,128)S(1)} %forward_mid.2.before, ...), custom_call_target="tpu_custom_call" | custom-call | tf_op jit(solution)/shard_map/forward_far/pallas_call | solution.py:47
  28.0 1.6 %collective-permute-start.5 = (bf16[2,16,1024]{2,1,0:T(8,128)(2,1)S(1)}, bf16[2,16,1024]{2,1,0:T(8,128)(2,1)S(1)}, u32[]{:S(2)}, u32[]{:S(2)}) collective-permute-start(bf16[2,16,1024]{2,1,0:T(8,128)(2,1)S(1)} %get-tuple-element.52), channel_id=1, source_target_pairs={{0,1},{1,0},{2,3},{3,2},{4,5},{5,4},{6,7},{7,6},{8,9},{9,8},{10,11... | collective-permute-start | bytes 196616 | tf_op jit(solution)/shard_map/ppermute | solution.py:32
  29.6 1.5 %collective-permute-start.6 = (bf16[2,16,1024]{2,1,0:T(8,128)(2,1)S(1)}, bf16[2,16,1024]{2,1,0:T(8,128)(2,1)S(1)}, u32[]{:S(2)}, u32[]{:S(2)}) collective-permute-start(bf16[2,16,1024]{2,1,0:T(8,128)(2,1)S(1)} %get-tuple-element.52), channel_id=1, source_target_pairs={{0,2},{1,3},{2,0},{3,1},{4,6},{5,7},{6,4},{7,5},{8,10},{9,11},{10,... | collective-permute-start | bytes 196616 | tf_op jit(solution)/shard_map/ppermute | solution.py:32
  32.7 1.1 %collective-permute-done.6.refs_2_ = bf16[2,16,1024]{2,1,0:T(8,128)(2,1)S(1)} collective-permute-done((bf16[2,16,1024]{2,1,0:T(8,128)(2,1)S(1)}, bf16[2,16,1024]{2,1,0:T(8,128)(2,1)S(1)}, u32[]{:S(2)}, u32[]{:S(2)}) %collective-permute-start.6) | collective-permute-done | bytes 65568 | tf_op jit(solution)/shard_map/ppermute | solution.py:32
  33.9 2.4 %collective-permute-done.7.refs_3_ = bf16[2,16,1024]{2,1,0:T(8,128)(2,1)S(1)} collective-permute-done((bf16[2,16,1024]{2,1,0:T(8,128)(2,1)S(1)}, bf16[2,16,1024]{2,1,0:T(8,128)(2,1)S(1)}, u32[]{:S(2)}, u32[]{:S(2)}) %collective-permute-start.7) | collective-permute-done | bytes 65568 | tf_op jit(solution)/shard_map/ppermute | solution.py:32
  36.3 1.8 %backward_first.2 = (bf16[160,1024]{1,0:T(8,128)(2,1)S(1)}, bf16[160,1024]{1,0:T(8,128)(2,1)S(1)}, bf16[160,1024]{1,0:T(8,128)(2,1)S(1)}, f32[2,16,256]{2,1,0:T(8,128)S(1)}) custom-call(s32[14]{0:T(128)S(1)} %concatenate.9.meta, bf16[3,1024,1024]{2,1,0:T(8,128)(2,1)S(1)} %get-tuple-element.39.turned, ...), custom_call_target="tpu_custom_call" | custom-call | tf_op jit(solution)/shard_map/backward_first/pallas_call | solution.py:47
  38.1 1.6 %collective-permute-start.12 = (bf16[160,1024]{1,0:T(8,128)(2,1)S(1)}, bf16[160,1024]{1,0:T(8,128)(2,1)S(1)}, u32[]{:S(2)}, u32[]{:S(2)}) collective-permute-start(bf16[160,1024]{1,0:T(8,128)(2,1)S(1)} %get-tuple-element.59), channel_id=1, source_target_pairs={{0,24},{4,12},{8,0},{12,20},{16,8},{20,28},{24,16},{28,4},{1,25},{... | collective-permute-start | bytes 983048 | tf_op jit(solution)/shard_map/ppermute | solution.py:381
  40.3 1.6 %forward_mid.3.before = f32[160,1024]{1,0:T(8,128)S(1)} custom-call(s32[14]{0:T(128)S(1)} %concatenate.9.meta, bf16[5,1024,1024]{2,1,0:T(8,128)(2,1)S(1)} %get-tuple-element.43.held, f32[160,1024]{1,0:T(8,128)S(1)} %forward_near.1.before, bf16[160,1024]{1,0:T(8,128)(2,1)S(1)} %collective-permute-done.8.refs_0_, ...), custom_call_target="tpu_custom_call" | custom-call | tf_op jit(solution)/shard_map/forward_mid/pallas_call | solution.py:47
  41.9 1.3 %forward_far.3 = (f32[2,16,1024]{2,1,0:T(8,128)S(1)}, bf16[2,16,1024]{2,1,0:T(8,128)(2,1)S(1)}) custom-call(s32[14]{0:T(128)S(1)} %concatenate.9.meta, bf16[5,1024,1024]{2,1,0:T(8,128)(2,1)S(1)} %get-tuple-element.43.held, bf16[2,10,32,1024]{3,2,1,0:T(8,128)(2,1)S(1)} %get-tuple-element.40.perturb, f32[160,1024]{1,0:T(8,128)S(1)} %forward_mid.3.before, ...), custom_call_target="tpu_custom_call" | custom-call | tf_op jit(solution)/shard_map/forward_far/pallas_call | solution.py:47
  43.8 1.2 %collective-permute-start.14 = (bf16[2,16,1024]{2,1,0:T(8,128)(2,1)S(1)}, bf16[2,16,1024]{2,1,0:T(8,128)(2,1)S(1)}, u32[]{:S(2)}, u32[]{:S(2)}) collective-permute-start(bf16[2,16,1024]{2,1,0:T(8,128)(2,1)S(1)} %get-tuple-element.62), channel_id=1, source_target_pairs={{0,2},{1,3},{2,0},{3,1},{4,6},{5,7},{6,4},{7,5},{8,10},{9,11},{10,... | collective-permute-start | bytes 196616 | tf_op jit(solution)/shard_map/ppermute | solution.py:32
  45.0 1.8 %collective-permute-start.15 = (bf16[2,16,1024]{2,1,0:T(8,128)(2,1)S(1)}, bf16[2,16,1024]{2,1,0:T(8,128)(2,1)S(1)}, u32[]{:S(2)}, u32[]{:S(2)}) collective-permute-start(bf16[2,16,1024]{2,1,0:T(8,128)(2,1)S(1)} %get-tuple-element.62), channel_id=1, source_target_pairs={{0,3},{1,2},{2,1},{3,0},{4,7},{5,6},{6,5},{7,4},{8,11},{9,10},{10,... | collective-permute-start | bytes 196616 | tf_op jit(solution)/shard_map/ppermute | solution.py:32
  48.8 1.4 %backward_second.1 = bf16[160,1024]{1,0:T(8,128)(2,1)S(1)} custom-call(s32[14]{0:T(128)S(1)} %concatenate.9.meta, bf16[5,1024,1024]{2,1,0:T(8,128)(2,1)S(1)} %get-tuple-element.43.held, bf16[160,1024]{1,0:T(8,128)(2,1)S(1)} %get-tuple-element.73.adjoint_in), custom_call_target="tpu_custom_call" | custom-call | flops 99999997952 | tf_op jit(solution)/shard_map/backward_second/pallas_call | solution.py:47
  50.2 1.8 %backward_first.3 = (bf16[160,1024]{1,0:T(8,128)(2,1)S(1)}, bf16[80,1024]{1,0:T(8,128)(2,1)S(1)}, bf16[80,1024]{1,0:T(8,128)(2,1)S(1)}, bf16[160,1024]{1,0:T(8,128)(2,1)S(1)}, f32[2,16,256]{2,1,0:T(8,128)S(1)}) custom-call(s32[14]{0:T(128)S(1)} %concatenate.9.meta, bf16[3,1024,1024]{2,1,0:T(8,128)(2,1)S(1)} %get-tuple-element.39.turned, ...), custom_call_target="tpu_custom_call" | custom-call | tf_op jit(solution)/shard_map/backward_first/pallas_call | solution.py:47
  52.6 3.0 %collective-permute-start.22 = (bf16[160,1024]{1,0:T(8,128)(2,1)S(1)}, bf16[160,1024]{1,0:T(8,128)(2,1)S(1)}, u32[]{:S(2)}, u32[]{:S(2)}) collective-permute-start(bf16[160,1024]{1,0:T(8,128)(2,1)S(1)} %get-tuple-element.72), channel_id=1, source_target_pairs={{0,24},{4,12},{8,0},{12,20},{16,8},{20,28},{24,16},{28,4},{1,25},{... | collective-permute-start | bytes 983048 | tf_op jit(solution)/shard_map/ppermute | solution.py:392
  56.7 1.2 %collective-permute-done.19.refs_3_ = bf16[160,1024]{1,0:T(8,128)(2,1)S(1)} collective-permute-done((bf16[160,1024]{1,0:T(8,128)(2,1)S(1)}, bf16[160,1024]{1,0:T(8,128)(2,1)S(1)}, u32[]{:S(2)}, u32[]{:S(2)}) %collective-permute-start.19) | collective-permute-done | bytes 327712 | tf_op jit(solution)/shard_map/ppermute | solution.py:387
  57.9 2.2 %backward_rest.1 = (bf16[80,1024]{1,0:T(8,128)(2,1)S(1)}, bf16[80,1024]{1,0:T(8,128)(2,1)S(1)}, f32[160,1024]{1,0:T(8,128)S(1)}) custom-call(s32[14]{0:T(128)S(1)} %concatenate.9.meta, bf16[5,1024,1024]{2,1,0:T(8,128)(2,1)S(1)} %get-tuple-element.43.held, bf16[160,1024]{1,0:T(8,128)(2,1)S(1)} %get-tuple-element.68.adjoint_in), custom_call_target="tpu_custom_call" | custom-call | tf_op jit(solution)/shard_map/backward_rest/pallas_call | solution.py:47
  61.9 1.4 %backward_kept.1.refs_1_ = f32[160,1024]{1,0:T(8,128)S(1)} custom-call(s32[14]{0:T(128)S(1)} %concatenate.9.meta, bf16[5,1024,1024]{2,1,0:T(8,128)(2,1)S(1)} %get-tuple-element.43.held, bf16[160,1024]{1,0:T(8,128)(2,1)S(1)} %get-tuple-element.73.adjoint_in), custom_call_target="tpu_custom_call" | custom-call | tf_op jit(solution)/shard_map/backward_kept/pallas_call | solution.py:47
  64.3 6.9 %collective-permute-done.22.refs_1_ = bf16[160,1024]{1,0:T(8,128)(2,1)S(1)} collective-permute-done((bf16[160,1024]{1,0:T(8,128)(2,1)S(1)}, bf16[160,1024]{1,0:T(8,128)(2,1)S(1)}, u32[]{:S(2)}, u32[]{:S(2)}) %collective-permute-start.22) | collective-permute-done | bytes 327712 | tf_op jit(solution)/shard_map/ppermute | solution.py:392
  (64 shorter events, 13.5 us)
Async XLA Ops:
  1.8 14.1 %collective-permute-start.1 = (bf16[160,1024]{1,0:T(8,128)(2,1)S(1)}, bf16[160,1024]{1,0:T(8,128)(2,1)S(1)}, u32[]{:S(2)}, u32[]{:S(2)}) collective-permute-start(bf16[160,1024]{1,0:T(8,128)(2,1)S(1)} %bitcast.11), channel_id=1, source_target_pairs={{0,24},{4,12},{8,16},{12,4},{16,8},{20,28},{24,0},{28,20},{1,25},{... | collective-permute-start | bytes 983048 | tf_op jit(solution)/shard_map/ppermute | solution.py:369
  6.9 12.0 %collective-permute-start.2 = (bf16[160,1024]{1,0:T(8,128)(2,1)S(1)}, bf16[160,1024]{1,0:T(8,128)(2,1)S(1)}, u32[]{:S(2)}, u32[]{:S(2)}) collective-permute-start(bf16[160,1024]{1,0:T(8,128)(2,1)S(1)} %bitcast.12), channel_id=1, source_target_pairs={{0,8},{4,28},{8,0},{12,20},{16,24},{20,12},{24,16},{28,4},{1,9},{5... | collective-permute-start | bytes 983048 | tf_op jit(solution)/shard_map/ppermute | solution.py:370
  15.8 8.8 %collective-permute-start = (bf16[320,1024]{1,0:T(8,128)(2,1)S(1)}, bf16[320,1024]{1,0:T(8,128)(2,1)S(1)}, u32[]{:S(2)}, u32[]{:S(2)}) collective-permute-start(bf16[320,1024]{1,0:T(8,128)(2,1)S(1)} %pad_maximum_fusion), channel_id=1, source_target_pairs={{0,4},{4,0},{8,12},{12,8},{16,20},{20,16},{24,28},{28,24},{1,5},{5... | collective-permute-start | bytes 1966088 | tf_op jit(solution)/shard_map/ppermute | solution.py:371
  19.0 20.7 %collective-permute-start.8 = (bf16[160,1024]{1,0:T(8,128)(2,1)S(1)}, bf16[160,1024]{1,0:T(8,128)(2,1)S(1)}, u32[]{:S(2)}, u32[]{:S(2)}) collective-permute-start(bf16[160,1024]{1,0:T(8,128)(2,1)S(1)} %bitcast.9), channel_id=1, source_target_pairs={{0,24},{4,12},{8,16},{12,4},{16,8},{20,28},{24,0},{28,20},{1,25},{... | collective-permute-start | bytes 983048 | tf_op jit(solution)/shard_map/ppermute | solution.py:373
  23.4 16.3 %collective-permute-start.9 = (bf16[160,1024]{1,0:T(8,128)(2,1)S(1)}, bf16[160,1024]{1,0:T(8,128)(2,1)S(1)}, u32[]{:S(2)}, u32[]{:S(2)}) collective-permute-start(bf16[160,1024]{1,0:T(8,128)(2,1)S(1)} %bitcast.10), channel_id=1, source_target_pairs={{0,8},{4,28},{8,0},{12,20},{16,24},{20,12},{24,16},{28,4},{1,9},{5... | collective-permute-start | bytes 983048 | tf_op jit(solution)/shard_map/ppermute | solution.py:374
  24.0 2.8 %collective-permute-start.3 = (bf16[80,1024]{1,0:T(8,128)(2,1)S(1)}, bf16[80,1024]{1,0:T(8,128)(2,1)S(1)}, u32[]{:S(2)}, u32[]{:S(2)}) collective-permute-start(bf16[80,1024]{1,0:T(8,128)(2,1)S(1)} %get-tuple-element.77), channel_id=1, source_target_pairs={{0,4},{4,0},{8,12},{12,8},{16,20},{20,16},{24,28},{28,24},{1,5},{5... | collective-permute-start | bytes 491528 | tf_op jit(solution)/shard_map/ppermute | solution.py:301
  24.5 2.3 %collective-permute-start.4 = (bf16[80,1024]{1,0:T(8,128)(2,1)S(1)}, bf16[80,1024]{1,0:T(8,128)(2,1)S(1)}, u32[]{:S(2)}, u32[]{:S(2)}) collective-permute-start(bf16[80,1024]{1,0:T(8,128)(2,1)S(1)} %get-tuple-element.76), channel_id=1, source_target_pairs={{0,4},{4,0},{8,12},{12,8},{16,20},{20,16},{24,28},{28,24},{1,5},{5... | collective-permute-start | bytes 491528 | tf_op jit(solution)/shard_map/ppermute | solution.py:301
  28.0 4.7 %collective-permute-start.5 = (bf16[2,16,1024]{2,1,0:T(8,128)(2,1)S(1)}, bf16[2,16,1024]{2,1,0:T(8,128)(2,1)S(1)}, u32[]{:S(2)}, u32[]{:S(2)}) collective-permute-start(bf16[2,16,1024]{2,1,0:T(8,128)(2,1)S(1)} %get-tuple-element.52), channel_id=1, source_target_pairs={{0,1},{1,0},{2,3},{3,2},{4,5},{5,4},{6,7},{7,6},{8,9},{9,8},{10,11... | collective-permute-start | bytes 196616 | tf_op jit(solution)/shard_map/ppermute | solution.py:32
  29.6 4.3 %collective-permute-start.6 = (bf16[2,16,1024]{2,1,0:T(8,128)(2,1)S(1)}, bf16[2,16,1024]{2,1,0:T(8,128)(2,1)S(1)}, u32[]{:S(2)}, u32[]{:S(2)}) collective-permute-start(bf16[2,16,1024]{2,1,0:T(8,128)(2,1)S(1)} %get-tuple-element.52), channel_id=1, source_target_pairs={{0,2},{1,3},{2,0},{3,1},{4,6},{5,7},{6,4},{7,5},{8,10},{9,11},{10,... | collective-permute-start | bytes 196616 | tf_op jit(solution)/shard_map/ppermute | solution.py:32
  31.1 5.2 %collective-permute-start.7 = (bf16[2,16,1024]{2,1,0:T(8,128)(2,1)S(1)}, bf16[2,16,1024]{2,1,0:T(8,128)(2,1)S(1)}, u32[]{:S(2)}, u32[]{:S(2)}) collective-permute-start(bf16[2,16,1024]{2,1,0:T(8,128)(2,1)S(1)} %get-tuple-element.52), channel_id=1, source_target_pairs={{0,3},{1,2},{2,1},{3,0},{4,7},{5,6},{6,5},{7,4},{8,11},{9,10},{10,... | collective-permute-start | bytes 196616 | tf_op jit(solution)/shard_map/ppermute | solution.py:32
  38.0 8.7 %collective-permute-start.18 = (bf16[160,1024]{1,0:T(8,128)(2,1)S(1)}, bf16[160,1024]{1,0:T(8,128)(2,1)S(1)}, u32[]{:S(2)}, u32[]{:S(2)}) collective-permute-start(bf16[160,1024]{1,0:T(8,128)(2,1)S(1)} %get-tuple-element.67), channel_id=1, source_target_pairs={{0,4},{4,0},{8,12},{12,8},{16,20},{20,16},{24,28},{28,24},{1,5},{5... | collective-permute-start | bytes 983048 | tf_op jit(solution)/shard_map/ppermute | solution.py:380
  38.1 10.6 %collective-permute-start.12 = (bf16[160,1024]{1,0:T(8,128)(2,1)S(1)}, bf16[160,1024]{1,0:T(8,128)(2,1)S(1)}, u32[]{:S(2)}, u32[]{:S(2)}) collective-permute-start(bf16[160,1024]{1,0:T(8,128)(2,1)S(1)} %get-tuple-element.59), channel_id=1, source_target_pairs={{0,24},{4,12},{8,0},{12,20},{16,8},{20,28},{24,16},{28,4},{1,25},{... | collective-permute-start | bytes 983048 | tf_op jit(solution)/shard_map/ppermute | solution.py:381
  39.7 2.2 %collective-permute-start.10 = (bf16[80,1024]{1,0:T(8,128)(2,1)S(1)}, bf16[80,1024]{1,0:T(8,128)(2,1)S(1)}, u32[]{:S(2)}, u32[]{:S(2)}) collective-permute-start(bf16[80,1024]{1,0:T(8,128)(2,1)S(1)} %get-tuple-element.75), channel_id=1, source_target_pairs={{0,4},{4,0},{8,12},{12,8},{16,20},{20,16},{24,28},{28,24},{1,5},{5... | collective-permute-start | bytes 491528 | tf_op jit(solution)/shard_map/ppermute | solution.py:301
  39.9 2.0 %collective-permute-start.11 = (bf16[80,1024]{1,0:T(8,128)(2,1)S(1)}, bf16[80,1024]{1,0:T(8,128)(2,1)S(1)}, u32[]{:S(2)}, u32[]{:S(2)}) collective-permute-start(bf16[80,1024]{1,0:T(8,128)(2,1)S(1)} %get-tuple-element.74), channel_id=1, source_target_pairs={{0,4},{4,0},{8,12},{12,8},{16,20},{20,16},{24,28},{28,24},{1,5},{5... | collective-permute-start | bytes 491528 | tf_op jit(solution)/shard_map/ppermute | solution.py:301
  43.2 6.9 %collective-permute-start.13 = (bf16[2,16,1024]{2,1,0:T(8,128)(2,1)S(1)}, bf16[2,16,1024]{2,1,0:T(8,128)(2,1)S(1)}, u32[]{:S(2)}, u32[]{:S(2)}) collective-permute-start(bf16[2,16,1024]{2,1,0:T(8,128)(2,1)S(1)} %get-tuple-element.62), channel_id=1, source_target_pairs={{0,1},{1,0},{2,3},{3,2},{4,5},{5,4},{6,7},{7,6},{8,9},{9,8},{10,11... | collective-permute-start | bytes 196616 | tf_op jit(solution)/shard_map/ppermute | solution.py:32
  43.8 6.4 %collective-permute-start.14 = (bf16[2,16,1024]{2,1,0:T(8,128)(2,1)S(1)}, bf16[2,16,1024]{2,1,0:T(8,128)(2,1)S(1)}, u32[]{:S(2)}, u32[]{:S(2)}) collective-permute-start(bf16[2,16,1024]{2,1,0:T(8,128)(2,1)S(1)} %get-tuple-element.62), channel_id=1, source_target_pairs={{0,2},{1,3},{2,0},{3,1},{4,6},{5,7},{6,4},{7,5},{8,10},{9,11},{10,... | collective-permute-start | bytes 196616 | tf_op jit(solution)/shard_map/ppermute | solution.py:32
  45.0 5.2 %collective-permute-start.15 = (bf16[2,16,1024]{2,1,0:T(8,128)(2,1)S(1)}, bf16[2,16,1024]{2,1,0:T(8,128)(2,1)S(1)}, u32[]{:S(2)}, u32[]{:S(2)}) collective-permute-start(bf16[2,16,1024]{2,1,0:T(8,128)(2,1)S(1)} %get-tuple-element.62), channel_id=1, source_target_pairs={{0,3},{1,2},{2,1},{3,0},{4,7},{5,6},{6,5},{7,4},{8,11},{9,10},{10,... | collective-permute-start | bytes 196616 | tf_op jit(solution)/shard_map/ppermute | solution.py:32
  47.8 10.1 %collective-permute-start.19 = (bf16[160,1024]{1,0:T(8,128)(2,1)S(1)}, bf16[160,1024]{1,0:T(8,128)(2,1)S(1)}, u32[]{:S(2)}, u32[]{:S(2)}) collective-permute-start(bf16[160,1024]{1,0:T(8,128)(2,1)S(1)} %backward_through.2), channel_id=1, source_target_pairs={{0,8},{4,28},{8,16},{12,4},{16,24},{20,12},{24,0},{28,20},{1,9},{5... | collective-permute-start | bytes 983048 | tf_op jit(solution)/shard_map/ppermute | solution.py:387
  51.9 3.6 %collective-permute-start.16 = (bf16[80,1024]{1,0:T(8,128)(2,1)S(1)}, bf16[80,1024]{1,0:T(8,128)(2,1)S(1)}, u32[]{:S(2)}, u32[]{:S(2)}) collective-permute-start(bf16[80,1024]{1,0:T(8,128)(2,1)S(1)} %get-tuple-element.65), channel_id=1, source_target_pairs={{0,4},{4,0},{8,12},{12,8},{16,20},{20,16},{24,28},{28,24},{1,5},{5... | collective-permute-start | bytes 491528 | tf_op jit(solution)/shard_map/ppermute | solution.py:390
  52.0 3.5 %collective-permute-start.17 = (bf16[80,1024]{1,0:T(8,128)(2,1)S(1)}, bf16[80,1024]{1,0:T(8,128)(2,1)S(1)}, u32[]{:S(2)}, u32[]{:S(2)}) collective-permute-start(bf16[80,1024]{1,0:T(8,128)(2,1)S(1)} %get-tuple-element.66), channel_id=1, source_target_pairs={{0,4},{4,0},{8,12},{12,8},{16,20},{20,16},{24,28},{28,24},{1,5},{5... | collective-permute-start | bytes 491528 | tf_op jit(solution)/shard_map/ppermute | solution.py:390
  52.5 10.9 %collective-permute-start.24 = (bf16[160,1024]{1,0:T(8,128)(2,1)S(1)}, bf16[160,1024]{1,0:T(8,128)(2,1)S(1)}, u32[]{:S(2)}, u32[]{:S(2)}) collective-permute-start(bf16[160,1024]{1,0:T(8,128)(2,1)S(1)} %backward_second.1), channel_id=1, source_target_pairs={{0,4},{4,0},{8,12},{12,8},{16,20},{20,16},{24,28},{28,24},{1,5},{5... | collective-permute-start | bytes 983048 | tf_op jit(solution)/shard_map/ppermute | solution.py:391
  52.6 18.7 %collective-permute-start.22 = (bf16[160,1024]{1,0:T(8,128)(2,1)S(1)}, bf16[160,1024]{1,0:T(8,128)(2,1)S(1)}, u32[]{:S(2)}, u32[]{:S(2)}) collective-permute-start(bf16[160,1024]{1,0:T(8,128)(2,1)S(1)} %get-tuple-element.72), channel_id=1, source_target_pairs={{0,24},{4,12},{8,0},{12,20},{16,8},{20,28},{24,16},{28,4},{1,25},{... | collective-permute-start | bytes 983048 | tf_op jit(solution)/shard_map/ppermute | solution.py:392
  56.7 15.0 %collective-permute-start.23 = (bf16[160,1024]{1,0:T(8,128)(2,1)S(1)}, bf16[160,1024]{1,0:T(8,128)(2,1)S(1)}, u32[]{:S(2)}, u32[]{:S(2)}) collective-permute-start(bf16[160,1024]{1,0:T(8,128)(2,1)S(1)} %backward_through.3), channel_id=1, source_target_pairs={{0,8},{4,28},{8,16},{12,4},{16,24},{20,12},{24,0},{28,20},{1,9},{5... | collective-permute-start | bytes 983048 | tf_op jit(solution)/shard_map/ppermute | solution.py:393
  60.2 1.6 %collective-permute-start.21 = (bf16[80,1024]{1,0:T(8,128)(2,1)S(1)}, bf16[80,1024]{1,0:T(8,128)(2,1)S(1)}, u32[]{:S(2)}, u32[]{:S(2)}) collective-permute-start(bf16[80,1024]{1,0:T(8,128)(2,1)S(1)} %get-tuple-element.71), channel_id=1, source_target_pairs={{0,4},{4,0},{8,12},{12,8},{16,20},{20,16},{24,28},{28,24},{1,5},{5... | collective-permute-start | bytes 491528 | tf_op jit(solution)/shard_map/ppermute | solution.py:395
  (6 other events, 41.0 us)
